TPU v7x, 256 devices: a whole 4x4x8 slice. The times are simulated.
256 devices in a mesh: dp: 32 (over x, y, core), tensor: 8 (over z).
Axes of the slice: x: 4, y: 4, z: 8, core: 2. Of those that a mesh axis runs over, the one named last changes fastest.
Arguments:
- grad: bfloat16 [32, 8192, 1024], P('dp', None, 'tensor'), may hold values from -9 to 9
- error: float32 [32, 8192, 1024], P('dp', None, 'tensor'), may hold values from -4 to 4
- warm_q: float32 [1024, 64], P('tensor'), may hold values from -6 to 6
Outputs:
- update: bfloat16 [8192, 1024], P(None, 'tensor')
- new_error: float32 [32, 8192, 1024], P('dp', None, 'tensor')
- new_q: float32 [1024, 64], P('tensor')
All inputs are finite; a program needn't handle non-finite values.
Results may differ from a plain program's by a relative error of at most 0.001.
Values sent between devices are 32-bit elements; how exact they have to be, the bound alone decides.
No kernel may reach another device: no remote copies, remote signals or barrier semaphores. Data moves between devices by JAX's collectives and lax.ppermute only.
A program may use at most 64 MiB of HBM per device.

v0:
```python
import jax
import jax.numpy as jnp
from jax import lax
from jax.sharding import PartitionSpec as P


def orthonormal(factor):
    highest = lax.Precision.HIGHEST
    gram = lax.dot_general(factor, factor, (((0,), (0,)), ((), ())), precision=highest)
    lower = jnp.linalg.cholesky(gram)
    return lax.linalg.triangular_solve(lower, factor, left_side=False, lower=True, transpose_a=True)


def shards(grad, error, warm_q):
    highest = lax.Precision.HIGHEST
    combined = grad[0].astype(jnp.float32) + error[0]
    scale = 1.0 / lax.axis_size("dp")
    local_term = jnp.dot(combined, warm_q, precision=highest)
    factor = lax.psum(local_term, ("dp", "tensor")) * scale
    basis = orthonormal(factor)
    right_term = lax.dot_general(combined, basis, (((0,), (0,)), ((), ())), precision=highest)
    new_q = lax.psum(right_term, "dp") * scale
    lowrank = lax.dot_general(basis, new_q, (((1,), (1,)), ((), ())), precision=highest)
    update = lowrank.astype(jnp.bfloat16)
    new_error = (combined - lowrank)[None, :, :]
    return (update, new_error, new_q)


def solution(mesh):
    return jax.shard_map(
        shards,
        mesh=mesh,
        in_specs=(P("dp", None, "tensor"), P("dp", None, "tensor"), P("tensor", None)),
        out_specs=(P(None, "tensor"), P("dp", None, "tensor"), P("tensor", None)),
        check_vma=False,
    )
```

profile of v0, /device:TPU:96, one launch (start us, length us, event | category | flops | bytes accessed | tf_op | source)
XLA Modules:
  0.0 449.6 jit_solution(5288554628498689968)
XLA Ops:
  7.2 0.0 copy-start
  7.2 0.0 all-reduce.2.cloned.1.call-start
  7.2 0.7 copy-done
  7.9 9.0 %fusion.2 = f32[8192,64]{0,1:T(8,128)} fusion(f32[128,64]{0,1:T(8,128)S(1)} %copy-done, f32[1,8192,128]{2,1,0:T(8,128)} %param.4, bf16[1,8192,128]{2,1,0:T(8,128)(2,1)} %param.3), kind=kOutput, calls=%fused_computation.3 | convolution fusion | flops 807403520 | bytes 8421376 | tf_op jit(solution)/shard_map/dot_general | solution.py:18
  17.0 0.0 all-reduce.2.cloned.1.call-update
  17.0 260.9 %all-reduce.2.cloned.1.call-done = f32[8192,64]{0,1:T(8,128)} async-done(((f32[8192,64]{0,1:T(8,128)}), f32[8192,64]{0,1:T(8,128)}) %all-reduce.2.cloned.1.call-update) | async-done | bytes 2097168 | tf_op jit(solution)/shard_map/psum | solution.py:19
  277.9 4.1 fusion.7
  282.0 0.1 copy.6
  282.1 5.8 %cholesky.16 = f32[64,64]{1,0:T(8,128)S(1)} custom-call(f32[64,64]{1,0:T(8,128)S(1)} %fusion.13), custom_call_target="Cholesky" | custom-call | tf_op jit(solution)/shard_map/jit(cholesky)/cholesky | solution.py:10
  288.0 0.6 compare_reduce_fusion
  288.6 0.7 fusion.11
  289.3 4.9 %custom-call.6 = f32[1,64,64]{1,2,0:T(8,128)S(1)} custom-call(f32[1,64,64]{2,1,0:T(8,128)S(1)} %fusion.11), custom_call_target="InvertDiagBlocksLowerTriangular" | custom-call | tf_op jit(solution)/shard_map/triangular_solve | solution.py:11
  294.2 0.0 copy-start.1
  294.2 3.8 fusion.5
  298.0 0.0 copy-done.1
  298.0 4.9 %fusion = f32[128,64]{0,1:T(8,128)S(1)} fusion(f32[8192,64]{0,1:T(8,128)S(1)} %fusion.5, f32[1,8192,128]{2,1,0:T(8,128)S(1)} %copy-done.1, bf16[1,8192,128]{2,1,0:T(8,128)(2,1)} %param.3), kind=kOutput, calls=%fused_computation.1 | convolution fusion | flops 807403520 | bytes 8421376 | tf_op jit(solution)/shard_map/dot_general | solution.py:21
  303.0 129.3 %psum.15 = f32[128,64]{0,1:T(8,128)S(1)} all-reduce(f32[128,64]{0,1:T(8,128)S(1)} %fusion), channel_id=1, replica_groups=mesh['dp'=32,'tensor'=8] {'dp'}, use_global_device_ids=true, to_apply=%region_3.4 | all-reduce | flops 8192 | bytes 65536 | tf_op jit(solution)/shard_map/psum | solution.py:22
  432.3 0.0 copy-start.2
  432.3 10.4 %fusion.4 = (f32[1,8192,128]{2,1,0:T(8,128)}, bf16[8192,128]{1,0:T(8,128)(2,1)}) fusion(f32[1,8192,128]{2,1,0:T(8,128)} %param.4, bf16[1,8192,128]{2,1,0:T(8,128)(2,1)} %param.3, f32[8192,64]{0,1:T(8,128)S(1)} %fusion.5, f32[128,64]{0,1:T(8,128)S(1)} %broadcast_multiply_fusion), kind=kOutput, calls=%fused_computation.5 | convolution fusion | flops 809500672 | bytes 14712832 | tf_op jit(solution)/shard_map/dot_general | solution.py:23
  442.7 0.0 copy-done.2
  (3 shorter events, 0.0 us)
Async XLA Ops:
  7.2 0.8 copy-start
  7.2 270.7 %all-reduce.2.cloned.1.call-start = ((), (), s32[]{:S(2)}) async-start(), calls=%async_computation | async-start | bytes 4194304 | tf_op jit(solution)/shard_map/psum | solution.py:19
  294.2 3.8 copy-start.1
  432.3 10.4 %copy-start.2 = (f32[128,64]{0,1:T(8,128)}, f32[128,64]{0,1:T(8,128)S(1)}, u32[]{:S(2)}) copy-start(f32[128,64]{0,1:T(8,128)S(1)} %broadcast_multiply_fusion) | copy-start | bytes 98308
Sparse Core Ops, SparseCore 0:
  17.1 260.7 all-reduce.1
where the time goes:
time: 450 us
  waiting for transfers between devices  261 us (58%)
  blocking collectives  129 us (29%)
  matrix products  32.3 us (7%)
  between operations  14.1 us (3%)
  other arithmetic  12.1 us (3%)
    psum x1, waiting for transfers between devices, shards(): factor = lax.psum(local_term, ('dp', 'tensor')) * scale  261 us
    psum x1, blocking collectives, shards(): new_q = lax.psum(right_term, 'dp') * scale  129 us
    dot_general x1, matrix products, shards(): lax.dot_general(basis, new_q, (((1,), (1,)), ((), ())), precision=highest)  10.4 us
    dot_general x1, matrix products, shards(): local_term = jnp.dot(combined, warm_q, precision=highest)  9.04 us
  transfers between devices with their start and end apart: 1, of which 1 were waited for; matrix products, arithmetic and copies ran while one was open for 0% of the time, Pallas kernels for 0%

commit v1 on v0

v1 whole, which is shorter than its diff:
```python
import jax
import jax.numpy as jnp
from jax import lax
from jax.experimental import pallas as pl
from jax.experimental.pallas import tpu as pltpu
from jax.sharding import Mesh, PartitionSpec as P

ROWS = 8192
COLS = 128
RANK = 64
HALF = ROWS // 4
BLOCK = 512
STEPS = HALF // BLOCK
REPLICAS = 32
PAIR_A = [(0, 1), (1, 0), (2, 3), (3, 2)]
PAIR_B = [(1, 2), (2, 1), (3, 0), (0, 3)]
VMEM_LIMIT = 48 * 1024 * 1024


def split2(a):
    high = a.astype(jnp.bfloat16)
    low = (a - high.astype(jnp.float32)).astype(jnp.bfloat16)
    return high, low


def mm(a, b):
    return jnp.dot(a, b, preferred_element_type=jnp.float32)


def mm_t(a, b):
    return lax.dot_general(a, b, (((0,), (0,)), ((), ())), preferred_element_type=jnp.float32)


def mm_highest(a, b, dims=((1,), (0,))):
    return lax.dot_general(a, b, (dims, ((), ())), precision=lax.Precision.HIGHEST, preferred_element_type=jnp.float32)


def left_kernel(half_ref, grad_ref, error_ref, warm_ref, term_ref, top_ref, bottom_ref):
    @pl.when(pl.program_id(0) == 0)
    def _():
        high, low = split2(warm_ref[...])
        none = jnp.zeros_like(high)
        top = jnp.concatenate([high, none, low, none], axis=1)
        bottom = jnp.concatenate([none, high, none, low], axis=1)
        top_ref[...] = jnp.concatenate([top, top], axis=0)
        bottom_ref[...] = jnp.concatenate([bottom, bottom], axis=0)

    combined = grad_ref[...].astype(jnp.float32) + error_ref[...]
    top = jnp.concatenate(split2(combined[0]), axis=1)
    bottom = jnp.concatenate(split2(combined[1]), axis=1)
    wide = mm(top, top_ref[...]) + mm(bottom, bottom_ref[...])
    term_ref[...] = wide[:, :128] + wide[:, 128:]


def left_half(half, grad, error, warm_q):
    rows = pl.BlockSpec((2, BLOCK, COLS), lambda i, half: (0, half[0] * STEPS + i, 0))
    return pl.pallas_call(
        left_kernel,
        out_shape=jax.ShapeDtypeStruct((HALF, 128), jnp.float32),
        grid_spec=pltpu.PrefetchScalarGridSpec(
            num_scalar_prefetch=1,
            grid=(STEPS,),
            in_specs=[rows, rows, pl.BlockSpec((COLS, RANK), lambda i, half: (0, 0))],
            out_specs=pl.BlockSpec((BLOCK, 128), lambda i, half: (i, 0)),
            scratch_shapes=[pltpu.VMEM((256, 256), jnp.bfloat16)] * 2,
        ),
        compiler_params=pltpu.CompilerParams(vmem_limit_bytes=VMEM_LIMIT),
        cost_estimate=pl.CostEstimate(flops=2 * 2 * HALF * 256 * 256, bytes_accessed=2 * HALF * COLS * 6 + HALF * 128 * 4, transcendentals=0),
        name="left",
    )(half, grad, error, warm_q)


def both_halves(i, half):
    own = half[0] * STEPS + i
    other = (1 - half[0]) * STEPS + i - STEPS
    return (0, jnp.where(i < STEPS, own, other), 0)


def right_kernel(half_ref, grad_ref, error_ref, own_ref, other_ref, right_ref, gram_ref, acc_ref, gram_acc_ref, tail_acc_ref):
    i = pl.program_id(0)

    @pl.when(i == 0)
    def _():
        acc_ref[...] = jnp.zeros_like(acc_ref)
        gram_acc_ref[...] = jnp.zeros_like(gram_acc_ref)
        tail_acc_ref[...] = jnp.zeros_like(tail_acc_ref)

    factor = jnp.where(i < STEPS, own_ref[...], other_ref[...])
    high = factor.astype(jnp.bfloat16)
    rest = factor - high.astype(jnp.float32)
    middle, low = split2(rest)
    pair = jnp.concatenate([high, middle], axis=1)
    combined = grad_ref[...].astype(jnp.float32) + error_ref[...]
    top_high, top_low = split2(combined[0])
    bottom_high, bottom_low = split2(combined[1])
    acc_ref[...] += mm_t(pair, jnp.concatenate([top_high, bottom_high], axis=1)) + mm_t(pair, jnp.concatenate([top_low, bottom_low], axis=1))
    gram_acc_ref[...] += mm_t(pair, pair)
    tail_acc_ref[...] += mm_t(high, low)

    @pl.when(i == 2 * STEPS - 1)
    def _():
        right = acc_ref[0:128, :] + acc_ref[128:256, :]
        right_ref[...] = right[0:64, 0:128] + right[64:128, 128:256]
        cross = gram_acc_ref[0:128, 128:256] + tail_acc_ref[...]
        gram = gram_acc_ref[0:128, 0:128] + gram_acc_ref[128:256, 128:256] + (cross + cross.T)
        gram_ref[...] = gram[0:64, 0:64] + gram[64:128, 64:128]


def right_terms(half, grad, error, own, other):
    rows = pl.BlockSpec((2, BLOCK, COLS), both_halves)
    return pl.pallas_call(
        right_kernel,
        out_shape=(jax.ShapeDtypeStruct((RANK, COLS), jnp.float32), jax.ShapeDtypeStruct((RANK, RANK), jnp.float32)),
        grid_spec=pltpu.PrefetchScalarGridSpec(
            num_scalar_prefetch=1,
            grid=(2 * STEPS,),
            in_specs=[
                rows,
                rows,
                pl.BlockSpec((BLOCK, 128), lambda i, half: (jnp.minimum(i, STEPS - 1), 0)),
                pl.BlockSpec((BLOCK, 128), lambda i, half: (jnp.maximum(i - STEPS, 0), 0)),
            ],
            out_specs=(pl.BlockSpec((RANK, COLS), lambda i, half: (0, 0)), pl.BlockSpec((RANK, RANK), lambda i, half: (0, 0))),
            scratch_shapes=[pltpu.VMEM((256, 256), jnp.float32)] * 2 + [pltpu.VMEM((128, 128), jnp.float32)],
        ),
        compiler_params=pltpu.CompilerParams(vmem_limit_bytes=VMEM_LIMIT),
        cost_estimate=pl.CostEstimate(flops=7 * 2 * HALF * 256 * 256, bytes_accessed=ROWS * COLS * 8, transcendentals=0),
        name="right",
    )(half, grad, error, own, other)


def inverse_kernel(gram_ref, inverse_ref):
    a = jnp.concatenate([gram_ref[...], jnp.eye(RANK, dtype=jnp.float32)], axis=1)
    done = []
    for j in range(RANK):
        if j % 8 == 0 and j:
            a = a[8:]
        k = j % 8
        row = a[k : k + 1, :]
        pivot = a[k : k + 1, j : j + 1]
        done.append(row * lax.rsqrt(pivot))
        if j == RANK - 1:
            break
        column = a[:, j : j + 1] / pivot
        below = lax.broadcasted_iota(jnp.int32, column.shape, 0) > k
        a = a - jnp.where(below, column, 0.0) * row
    inverse_ref[...] = jnp.concatenate(done, axis=0)[:, RANK:]


def inverse_lower(gram):
    return pl.pallas_call(
        inverse_kernel,
        out_shape=jax.ShapeDtypeStruct((RANK, RANK), jnp.float32),
        compiler_params=pltpu.CompilerParams(vmem_limit_bytes=VMEM_LIMIT),
        cost_estimate=pl.CostEstimate(flops=RANK**3, bytes_accessed=RANK * RANK * 8, transcendentals=RANK),
        name="inverse",
    )(gram)


def final_kernel(half_ref, grad_ref, error_ref, own_ref, other_ref, right_ref, inverse_ref, update_ref, residual_ref, new_q_ref, high_ref, low_ref):
    i = pl.program_id(0)

    @pl.when(i == 0)
    def _():
        new_q_t = mm_highest(inverse_ref[...], right_ref[...]) * (1.0 / REPLICAS)
        new_q_ref[...] = new_q_t.T
        mixed = mm_highest(inverse_ref[...], new_q_t, ((0,), (0,)))
        for ref, part in zip((high_ref, low_ref), split2(mixed)):
            none = jnp.zeros_like(part)
            two = jnp.concatenate([jnp.concatenate([part, none], axis=1), jnp.concatenate([none, part], axis=1)], axis=0)
            ref[...] = jnp.concatenate([two, two], axis=0)

    factor = jnp.where(i < STEPS, own_ref[...], other_ref[...])
    pair = jnp.concatenate(split2(factor), axis=1)
    wide = mm(pair, high_ref[...]) + mm(pair, low_ref[...])
    for part in range(2):
        lowrank = wide[:, part * 128 : part * 128 + 128]
        update_ref[part] = lowrank.astype(jnp.bfloat16)
        residual_ref[part] = grad_ref[part].astype(jnp.float32) + error_ref[part] - lowrank


def final(half, grad, error, own, other, right, inverse):
    rows = pl.BlockSpec((2, BLOCK, COLS), both_halves)
    return pl.pallas_call(
        final_kernel,
        out_shape=(
            jax.ShapeDtypeStruct((2, ROWS // 2, COLS), jnp.bfloat16),
            jax.ShapeDtypeStruct((2, ROWS // 2, COLS), jnp.float32),
            jax.ShapeDtypeStruct((COLS, RANK), jnp.float32),
        ),
        grid_spec=pltpu.PrefetchScalarGridSpec(
            num_scalar_prefetch=1,
            grid=(2 * STEPS,),
            in_specs=[
                rows,
                rows,
                pl.BlockSpec((BLOCK, 128), lambda i, half: (jnp.minimum(i, STEPS - 1), 0)),
                pl.BlockSpec((BLOCK, 128), lambda i, half: (jnp.maximum(i - STEPS, 0), 0)),
                pl.BlockSpec((RANK, COLS), lambda i, half: (0, 0)),
                pl.BlockSpec((RANK, RANK), lambda i, half: (0, 0)),
            ],
            out_specs=(rows, rows, pl.BlockSpec((COLS, RANK), lambda i, half: (0, 0))),
            scratch_shapes=[pltpu.VMEM((256, 256), jnp.bfloat16)] * 2,
        ),
        compiler_params=pltpu.CompilerParams(vmem_limit_bytes=VMEM_LIMIT),
        cost_estimate=pl.CostEstimate(flops=2 * 2 * HALF * 256 * 256 * 2, bytes_accessed=ROWS * COLS * 14, transcendentals=0),
        name="final",
    )(half, grad, error, own, other, right, inverse)


def swap(a):
    return lax.ppermute(a, "c", [(0, 1), (1, 0)])


def scatter_sum(a, axes, count):
    return lax.all_to_all(a, axes, 0, 0, tiled=True).reshape(count, -1, 128).sum(0)


def gather(a, axes, count):
    return lax.all_to_all(jnp.tile(a, (count, 1)), axes, 0, 0, tiled=True)


def sum_over_replicas(a):
    a = a + swap(a)
    for axis in ("y", "x"):
        for pairs in (PAIR_A, PAIR_B):
            a = a + lax.ppermute(a, axis, pairs)
    return a


def shards(grad, error, warm_q):
    grad = grad.reshape(2, ROWS // 2, COLS)
    error = error.reshape(2, ROWS // 2, COLS)
    half = lax.axis_index("c").astype(jnp.int32).reshape(1)
    away = left_half(1 - half, grad, error, warm_q)
    keep = left_half(half, grad, error, warm_q)
    piece = scatter_sum(keep + swap(away), ("x", "y"), 16)
    piece = scatter_sum(piece, "z", 8)
    own = gather(gather(piece, "z", 8), ("x", "y"), 16)
    other = swap(own)
    right, gram = right_terms(half, grad, error, own, other)
    inverse = inverse_lower(gram)
    right = sum_over_replicas(right)
    update, residual, new_q = final(half, grad, error, own, other, right, inverse)
    return update.reshape(ROWS, COLS), residual.reshape(1, ROWS, COLS), new_q


def solution(mesh):
    grid = Mesh(mesh.devices.reshape(4, 4, 2, 8), ("x", "y", "c", "z"))
    replicas = ("x", "y", "c")
    return jax.shard_map(
        shards,
        mesh=grid,
        in_specs=(P(replicas, None, "z"), P(replicas, None, "z"), P("z", None)),
        out_specs=(P(None, "z"), P(replicas, None, "z"), P("z", None)),
        check_vma=False,
    )
```

time: 450 us -> 119 us (0.26)
  the two profiles are of different devices: /device:TPU:96 before, /device:TPU:6 now
where the time goes in v1:
time: 119 us
  blocking collectives  67.6 us (57%)
  Pallas kernels  27.5 us (23%)
  waiting for transfers between devices  14.9 us (13%)
  starting transfers between devices  4.22 us (4%)
  local copies, waits for them, and re-layouts  3.23 us (3%)
    all_to_all x2, blocking collectives, scatter_sum(): lax.all_to_all(a, axes, 0, 0, tiled=True).reshape(count, -1, 128).sum(0)  39.5 us
    all_to_all x2, blocking collectives, gather(): return lax.all_to_all(jnp.tile(a, (count, 1)), axes, 0, 0, tiled=True)  28.2 us
    ppermute x4, waiting for transfers between devices, sum_over_replicas(): a = a + lax.ppermute(a, axis, pairs)  11.2 us
    pallas_call x1, Pallas kernels, final(): pl.pallas_call(final_kernel, out_shape=(jax.ShapeDtypeStruct((2, ROWS //...  8.36 us
    pallas_call x1, Pallas kernels, right_terms(): pl.pallas_call(right_kernel, out_shape=(jax.ShapeDtypeStruct((RANK, COLS)...  7.04 us
    pallas_call x2, Pallas kernels, left_half(): pl.pallas_call(left_kernel, out_shape=jax.ShapeDtypeStruct((HALF, 128), j...  6.7 us
    pallas_call x1, Pallas kernels, inverse_lower(): pl.pallas_call(inverse_kernel, out_shape=jax.ShapeDtypeStruct((RANK, RANK...  5.44 us
    ppermute x4, starting transfers between devices, sum_over_replicas(): a = a + lax.ppermute(a, axis, pairs)  3.89 us
  transfers between devices with their start and end apart: 7, of which 5 were waited for; matrix products, arithmetic and copies ran while one was open for 0% of the time, Pallas kernels for 7%

profile of v1, /device:TPU:6, one launch (start us, length us, event | category | flops | bytes accessed | tf_op | source)
XLA Modules:
  0.0 118.5 jit_solution(4956248957627222486)
XLA Ops:
  0.6 0.8 copy.9.warm_ref
  1.5 0.0 copy-start
  1.5 1.6 %copy-done = bf16[1,8192,128]{2,1,0:T(8,128)(2,1)S(1)} copy-done((bf16[1,8192,128]{2,1,0:T(8,128)(2,1)S(1)}, bf16[1,8192,128]{2,1,0:T(8,128)(2,1)}, u32[]{:S(2)}) %copy-start) | copy-done | bytes 2097176
  3.1 0.0 copy-start.1
  3.1 3.4 %left.3 = f32[2048,128]{1,0:T(8,128)S(1)} custom-call(s32[1]{0:T(128)S(6)} %sub.3.half_ref, bf16[2,4096,128]{2,1,0:T(8,128)(2,1)S(1)} %bitcast.9, f32[2,4096,128]{2,1,0:T(8,128)} %bitcast.16, f32[128,64]{1,0:T(8,128)S(1)} %copy.9.warm_ref), custom_call_target="tpu_custom_call" | custom-call | flops 536870912 | bytes 4194304 | tf_op jit(solution)/shard_map/left/pallas_call | solution.py:57
  6.5 0.1 collective-permute-start
  6.6 0.0 copy-done.1
  6.6 3.3 %left.2 = f32[2048,128]{1,0:T(8,128)S(1)} custom-call(s32[1]{0:T(128)} %bitcast.half_ref, bf16[2,4096,128]{2,1,0:T(8,128)(2,1)S(1)} %bitcast.10, f32[2,4096,128]{2,1,0:T(8,128)} %bitcast.17, f32[128,64]{1,0:T(8,128)S(1)} %copy.9.warm_ref), custom_call_target="tpu_custom_call" | custom-call | flops 536870912 | bytes 4194304 | tf_op jit(solution)/shard_map/left/pallas_call | solution.py:57
  9.9 0.0 collective-permute-done
  9.9 0.1 add.18
  10.0 22.8 %all_to_all.32 = f32[16,128,128]{2,1,0:T(8,128)S(1)} all-to-all(f32[16,128,128]{2,1,0:T(8,128)S(1)} %bitcast.20), channel_id=1, replica_groups=mesh['x'=4,'y'=4,'c'=2,'z'=8] {'x','y'}, dimensions={0} | all-to-all | bytes 2097152 | tf_op jit(solution)/shard_map/all_to_all | solution.py:216
  32.9 0.1 reduce_sum.18
  32.9 16.6 %all_to_all.33 = f32[8,16,128]{2,1,0:T(8,128)S(1)} all-to-all(f32[8,16,128]{2,1,0:T(8,128)S(1)} %bitcast.21), channel_id=1, replica_groups=mesh['x'=4,'y'=4,'c'=2,'z'=8] {'z'}, dimensions={0} | all-to-all | bytes 131072 | tf_op jit(solution)/shard_map/all_to_all | solution.py:216
  49.6 10.8 %all_to_all.34 = f32[8,16,128]{2,1,0:T(8,128)S(1)} all-to-all(f32[8,16,128]{2,1,0:T(8,128)S(1)} %tile.6), channel_id=1, replica_groups=mesh['x'=4,'y'=4,'c'=2,'z'=8] {'z'}, dimensions={0} | all-to-all | bytes 131072 | tf_op jit(solution)/shard_map/all_to_all | solution.py:220
  60.3 0.1 tile.8
  60.5 17.4 %all_to_all.35 = f32[16,128,128]{2,1,0:T(8,128)S(1)} all-to-all(f32[16,128,128]{2,1,0:T(8,128)S(1)} %tile.8), channel_id=1, replica_groups=mesh['x'=4,'y'=4,'c'=2,'z'=8] {'x','y'}, dimensions={0} | all-to-all | bytes 2097152 | tf_op jit(solution)/shard_map/all_to_all | solution.py:220
  77.9 0.0 collective-permute-start.1
  77.9 2.7 %collective-permute-done.1.other_ref = f32[2048,128]{1,0:T(8,128)S(1)} collective-permute-done((f32[2048,128]{1,0:T(8,128)S(1)}, f32[2048,128]{1,0:T(8,128)S(1)}, u32[]{:S(2)}, u32[]{:S(2)}) %collective-permute-start.1) | collective-permute-done | bytes 1048608 | tf_op jit(solution)/shard_map/ppermute | solution.py:212
  80.5 7.0 %right.1 = (f32[64,128]{1,0:T(8,128)S(1)}, f32[64,64]{1,0:T(8,128)S(1)}) custom-call(s32[1]{0:T(128)} %bitcast.half_ref, bf16[2,4096,128]{2,1,0:T(8,128)(2,1)S(1)} %bitcast.11, f32[2,4096,128]{2,1,0:T(8,128)} %bitcast.18, f32[2048,128]{1,0:T(8,128)S(1)} %bitcast.14, f32[2048,128]{1,0:T(8,128)S(1)} %collective-permute-done.1.other_ref), custom_call_target="tpu_custom_call" | custom-call | flops 1879048192 | bytes 8388608 | tf_op jit(solution)/shard_map/right/pallas_call | solution.py:111
  87.6 0.2 collective-permute-start.2
  87.8 1.1 collective-permute-done.2
  88.9 0.6 collective-permute-start.3
  89.5 3.4 %collective-permute-done.3 = f32[64,128]{1,0:T(8,128)S(1)} collective-permute-done((f32[64,128]{1,0:T(8,128)S(1)}, f32[64,128]{1,0:T(8,128)S(1)}, u32[]{:S(2)}, u32[]{:S(2)}) %collective-permute-start.3) | collective-permute-done | bytes 32800 | tf_op jit(solution)/shard_map/ppermute | solution.py:227
  92.8 0.6 collective-permute-start.4
  93.4 4.5 %collective-permute-done.4 = f32[64,128]{1,0:T(8,128)S(1)} collective-permute-done((f32[64,128]{1,0:T(8,128)S(1)}, f32[64,128]{1,0:T(8,128)S(1)}, u32[]{:S(2)}, u32[]{:S(2)}) %collective-permute-start.4) | collective-permute-done | bytes 32800 | tf_op jit(solution)/shard_map/ppermute | solution.py:227
  97.9 0.6 collective-permute-start.5
  98.5 3.3 %collective-permute-done.5 = f32[64,128]{1,0:T(8,128)S(1)} collective-permute-done((f32[64,128]{1,0:T(8,128)S(1)}, f32[64,128]{1,0:T(8,128)S(1)}, u32[]{:S(2)}, u32[]{:S(2)}) %collective-permute-start.5) | collective-permute-done | bytes 32800 | tf_op jit(solution)/shard_map/ppermute | solution.py:227
  101.9 2.1 %collective-permute-start.6 = (f32[64,128]{1,0:T(8,128)S(1)}, f32[64,128]{1,0:T(8,128)S(1)}, u32[]{:S(2)}, u32[]{:S(2)}) collective-permute-start(f32[64,128]{1,0:T(8,128)S(1)} %add.22), channel_id=1, source_target_pairs={{64,128},{128,64},{192,0},{0,192},{65,129},{129,65},{193,1},{1,193... | collective-permute-start | bytes 98312 | tf_op jit(solution)/shard_map/ppermute | solution.py:227
  104.0 5.4 %inverse.1.inverse_ref = f32[64,64]{1,0:T(8,128)S(1)} custom-call(f32[64,64]{1,0:T(8,128)S(1)} %get-tuple-element.9.gram_ref), custom_call_target="tpu_custom_call" | custom-call | flops 262144 | bytes 32768 | tf_op jit(solution)/shard_map/inverse/pallas_call | solution.py:151
  109.4 0.0 collective-permute-done.6
  109.5 8.4 %final.1 = (bf16[2,4096,128]{2,1,0:T(8,128)(2,1)}, f32[2,4096,128]{2,1,0:T(8,128)}, f32[128,64]{1,0:T(8,128)S(1)}) custom-call(s32[1]{0:T(128)} %bitcast.half_ref, bf16[2,4096,128]{2,1,0:T(8,128)(2,1)S(1)} %bitcast.12, f32[2,4096,128]{2,1,0:T(8,128)} %bitcast.19, f32[2048,128]{1,0:T(8,128)S(1)} %bitcast.15, ...), custom_call_target="tpu_custom_call" | custom-call | flops 1073741824 | bytes 14680064 | tf_op jit(solution)/shard_map/final/pallas_call | solution.py:184
  117.8 0.7 copy.11
  (7 shorter events, 0.0 us)
Async XLA Ops:
  1.5 1.6 %copy-start = (bf16[1,8192,128]{2,1,0:T(8,128)(2,1)S(1)}, bf16[1,8192,128]{2,1,0:T(8,128)(2,1)}, u32[]{:S(2)}) copy-start(bf16[1,8192,128]{2,1,0:T(8,128)(2,1)} %param.3) | copy-start | bytes 6291460
  3.1 3.5 %copy-start.1 = (bf16[1,8192,128]{2,1,0:T(8,128)(2,1)S(1)}, bf16[1,8192,128]{2,1,0:T(8,128)(2,1)}, u32[]{:S(2)}) copy-start(bf16[1,8192,128]{2,1,0:T(8,128)(2,1)} %param.3) | copy-start | bytes 6291460
  6.5 3.4 %collective-permute-start = (f32[2048,128]{1,0:T(8,128)S(1)}, f32[2048,128]{1,0:T(8,128)S(1)}, u32[]{:S(2)}, u32[]{:S(2)}) collective-permute-start(f32[2048,128]{1,0:T(8,128)S(1)} %left.3), channel_id=1, source_target_pairs={{0,8},{8,0},{1,9},{9,1},{2,10},{10,2},{3,11},{11,3},{4,12},{12,4},... | collective-permute-start | bytes 3145736 | tf_op jit(solution)/shard_map/ppermute | solution.py:212
  77.9 2.7 %collective-permute-start.1 = (f32[2048,128]{1,0:T(8,128)S(1)}, f32[2048,128]{1,0:T(8,128)S(1)}, u32[]{:S(2)}, u32[]{:S(2)}) collective-permute-start(f32[2048,128]{1,0:T(8,128)S(1)} %bitcast.13), channel_id=1, source_target_pairs={{0,8},{8,0},{1,9},{9,1},{2,10},{10,2},{3,11},{11,3},{4,12},{12,4},... | collective-permute-start | bytes 3145736 | tf_op jit(solution)/shard_map/ppermute | solution.py:212
  87.6 1.3 %collective-permute-start.2 = (f32[64,128]{1,0:T(8,128)S(1)}, f32[64,128]{1,0:T(8,128)S(1)}, u32[]{:S(2)}, u32[]{:S(2)}) collective-permute-start(f32[64,128]{1,0:T(8,128)S(1)} %get-tuple-element.8), channel_id=1, source_target_pairs={{0,8},{8,0},{1,9},{9,1},{2,10},{10,2},{3,11},{11,3},{4,12},{12,4},... | collective-permute-start | bytes 98312 | tf_op jit(solution)/shard_map/ppermute | solution.py:212
  88.9 3.9 %collective-permute-start.3 = (f32[64,128]{1,0:T(8,128)S(1)}, f32[64,128]{1,0:T(8,128)S(1)}, u32[]{:S(2)}, u32[]{:S(2)}) collective-permute-start(f32[64,128]{1,0:T(8,128)S(1)} %add.19), channel_id=1, source_target_pairs={{0,16},{16,0},{32,48},{48,32},{1,17},{17,1},{33,49},{49,33},{2,18}... | collective-permute-start | bytes 98312 | tf_op jit(solution)/shard_map/ppermute | solution.py:227
  92.8 5.1 %collective-permute-start.4 = (f32[64,128]{1,0:T(8,128)S(1)}, f32[64,128]{1,0:T(8,128)S(1)}, u32[]{:S(2)}, u32[]{:S(2)}) collective-permute-start(f32[64,128]{1,0:T(8,128)S(1)} %add.20), channel_id=1, source_target_pairs={{16,32},{32,16},{48,0},{0,48},{17,33},{33,17},{49,1},{1,49},{18,34... | collective-permute-start | bytes 98312 | tf_op jit(solution)/shard_map/ppermute | solution.py:227
  97.9 3.9 %collective-permute-start.5 = (f32[64,128]{1,0:T(8,128)S(1)}, f32[64,128]{1,0:T(8,128)S(1)}, u32[]{:S(2)}, u32[]{:S(2)}) collective-permute-start(f32[64,128]{1,0:T(8,128)S(1)} %add.21), channel_id=1, source_target_pairs={{0,64},{64,0},{128,192},{192,128},{1,65},{65,1},{129,193},{193,129... | collective-permute-start | bytes 98312 | tf_op jit(solution)/shard_map/ppermute | solution.py:227
  101.9 7.6 %collective-permute-start.6 = (f32[64,128]{1,0:T(8,128)S(1)}, f32[64,128]{1,0:T(8,128)S(1)}, u32[]{:S(2)}, u32[]{:S(2)}) collective-permute-start(f32[64,128]{1,0:T(8,128)S(1)} %add.22), channel_id=1, source_target_pairs={{64,128},{128,64},{192,0},{0,192},{65,129},{129,65},{193,1},{1,193... | collective-permute-start | bytes 98312 | tf_op jit(solution)/shard_map/ppermute | solution.py:227

commit v2 on v0

v2 whole, which is shorter than its diff:
```python
import jax
import jax.numpy as jnp
from jax import lax
from jax.experimental import pallas as pl
from jax.experimental.pallas import tpu as pltpu
from jax.sharding import Mesh, PartitionSpec as P

ROWS = 8192
COLS = 128
RANK = 64
HALF = ROWS // 4
BLOCK = 512
STEPS = HALF // BLOCK
REPLICAS = 32
PAIR_A = [(0, 1), (1, 0), (2, 3), (3, 2)]
PAIR_B = [(1, 2), (2, 1), (3, 0), (0, 3)]
RIGHT_BLOCK = 512
VMEM_LIMIT = 24 * 1024 * 1024
LEFT_VMEM_LIMIT = 51 * 1024 * 1024


def split2(a):
    high = a.astype(jnp.bfloat16)
    low = (a - high.astype(jnp.float32)).astype(jnp.bfloat16)
    return high, low


def mm(a, b):
    return jnp.dot(a, b, preferred_element_type=jnp.float32)


def mm_t(a, b):
    return lax.dot_general(a, b, (((0,), (0,)), ((), ())), preferred_element_type=jnp.float32)


def mm_highest(a, b, dims=((1,), (0,))):
    return lax.dot_general(a, b, (dims, ((), ())), precision=lax.Precision.HIGHEST, preferred_element_type=jnp.float32)


def left_kernel(half_ref, grad_ref, error_ref, warm_ref, term_ref, warm_buf, grad_buf, error_buf, warm_sem, grad_sems, error_sems):
    start = pl.multiple_of(half_ref[0] * HALF, HALF)
    warm_copy = pltpu.make_async_copy(warm_ref, warm_buf, warm_sem)
    warm_copy.start()
    copies = []
    for k in range(STEPS):
        source, rows = pl.ds(start + k * BLOCK, BLOCK), pl.ds(k * BLOCK, BLOCK)
        pair = (
            pltpu.make_async_copy(grad_ref.at[:, source, :], grad_buf.at[:, rows, :], grad_sems.at[k]),
            pltpu.make_async_copy(error_ref.at[:, source, :], error_buf.at[:, rows, :], error_sems.at[k]),
        )
        for copy in pair:
            copy.start()
        copies.append(pair)
    warm_copy.wait()
    high, low = split2(warm_buf[...].T)
    none = jnp.zeros_like(high)
    top_right = jnp.concatenate([high, none, low, none], axis=1)
    bottom_right = jnp.concatenate([none, high, none, low], axis=1)
    top_right = jnp.concatenate([top_right, top_right], axis=0)
    bottom_right = jnp.concatenate([bottom_right, bottom_right], axis=0)
    for k in range(STEPS):
        for copy in copies[k]:
            copy.wait()
        rows = pl.ds(k * BLOCK, BLOCK)
        combined = grad_buf[:, rows, :].astype(jnp.float32) + error_buf[:, rows, :]
        top = jnp.concatenate(split2(combined[0]), axis=1)
        bottom = jnp.concatenate(split2(combined[1]), axis=1)
        wide = mm(top, top_right) + mm(bottom, bottom_right)
        term_ref[rows, :] = wide[:, :128] + wide[:, 128:]


SMEM = pl.BlockSpec(memory_space=pltpu.SMEM)
HBM = pl.BlockSpec(memory_space=pltpu.HBM)
VMEM = pl.BlockSpec(memory_space=pltpu.VMEM)


def left_half(half, grad, error, warm_t):
    return pl.pallas_call(
        left_kernel,
        out_shape=jax.ShapeDtypeStruct((HALF, 128), jnp.float32),
        in_specs=[SMEM, HBM, HBM, HBM],
        out_specs=VMEM,
        scratch_shapes=[
            pltpu.VMEM((RANK, COLS), jnp.float32),
            pltpu.VMEM((2, HALF, COLS), jnp.bfloat16),
            pltpu.VMEM((2, HALF, COLS), jnp.float32),
            pltpu.SemaphoreType.DMA,
            pltpu.SemaphoreType.DMA((STEPS,)),
            pltpu.SemaphoreType.DMA((STEPS,)),
        ],
        compiler_params=pltpu.CompilerParams(vmem_limit_bytes=LEFT_VMEM_LIMIT),
        cost_estimate=pl.CostEstimate(flops=2 * 2 * HALF * 256 * 256, bytes_accessed=2 * HALF * COLS * 6, transcendentals=0),
        name="left",
    )(half, grad, error, warm_t)


def rows_of(side, offset):
    return pl.ds(pl.multiple_of(side * HALF + offset, RIGHT_BLOCK), RIGHT_BLOCK)


def add_half(side, grad_ref, error_ref, factor_ref, acc_ref, gram_ref, tail_ref):
    @pl.loop(0, HALF, step=RIGHT_BLOCK)
    def _(start):
        rows = pl.ds(pl.multiple_of(start, RIGHT_BLOCK), RIGHT_BLOCK)
        factor = factor_ref[rows, :]
        high = factor.astype(jnp.bfloat16)
        middle, low = split2(factor - high.astype(jnp.float32))
        pair = jnp.concatenate([high, middle], axis=1)
        source = rows_of(side, start)
        combined = grad_ref[:, source, :].astype(jnp.float32) + error_ref[:, source, :]
        top_high, top_low = split2(combined[0])
        bottom_high, bottom_low = split2(combined[1])
        acc_ref[...] += mm_t(pair, jnp.concatenate([top_high, bottom_high], axis=1)) + mm_t(pair, jnp.concatenate([top_low, bottom_low], axis=1))
        gram_ref[...] += mm_t(pair, pair)
        tail_ref[...] += mm_t(high, low)


def right_own_kernel(half_ref, grad_ref, error_ref, factor_ref, acc_ref, gram_ref, tail_ref):
    for ref in (acc_ref, gram_ref, tail_ref):
        ref[...] = jnp.zeros_like(ref)
    add_half(half_ref[0], grad_ref, error_ref, factor_ref, acc_ref, gram_ref, tail_ref)


def right_other_kernel(half_ref, grad_ref, error_ref, factor_ref, acc_in, gram_in, tail_in, right_ref, gram_ref, acc_ref, gram_acc_ref, tail_acc_ref):
    for ref, given in ((acc_ref, acc_in), (gram_acc_ref, gram_in), (tail_acc_ref, tail_in)):
        ref[...] = given[...]
    add_half(1 - half_ref[0], grad_ref, error_ref, factor_ref, acc_ref, gram_acc_ref, tail_acc_ref)
    right = acc_ref[0:128, :] + acc_ref[128:256, :]
    right_ref[...] = right[0:64, 0:128] + right[64:128, 128:256]
    cross = gram_acc_ref[0:128, 128:256] + tail_acc_ref[...]
    gram = gram_acc_ref[0:128, 0:128] + gram_acc_ref[128:256, 128:256] + (cross + cross.T)
    gram_ref[...] = gram[0:64, 0:64] + gram[64:128, 64:128]


def right_own(half, grad, error, factor):
    square = jax.ShapeDtypeStruct((256, 256), jnp.float32)
    return pl.pallas_call(
        right_own_kernel,
        out_shape=(square, square, jax.ShapeDtypeStruct((128, 128), jnp.float32)),
        in_specs=[SMEM] + [VMEM] * 3,
        out_specs=(VMEM,) * 3,
        compiler_params=pltpu.CompilerParams(vmem_limit_bytes=VMEM_LIMIT),
        cost_estimate=pl.CostEstimate(flops=7 * HALF * 256 * 256, bytes_accessed=ROWS * COLS * 3, transcendentals=0),
        name="right_own",
    )(half, grad, error, factor)


def right_other(half, grad, error, factor, sums):
    return pl.pallas_call(
        right_other_kernel,
        out_shape=(jax.ShapeDtypeStruct((RANK, COLS), jnp.float32), jax.ShapeDtypeStruct((RANK, RANK), jnp.float32)),
        in_specs=[SMEM] + [VMEM] * 6,
        out_specs=(VMEM, VMEM),
        scratch_shapes=[pltpu.VMEM((256, 256), jnp.float32)] * 2 + [pltpu.VMEM((128, 128), jnp.float32)],
        compiler_params=pltpu.CompilerParams(vmem_limit_bytes=VMEM_LIMIT),
        cost_estimate=pl.CostEstimate(flops=7 * HALF * 256 * 256, bytes_accessed=ROWS * COLS * 3, transcendentals=0),
        name="right_other",
    )(half, grad, error, factor, *sums)


def inverse_kernel(gram_ref, inverse_ref):
    a = jnp.concatenate([gram_ref[...], jnp.eye(RANK, dtype=jnp.float32)], axis=1)
    for panel in range(0, RANK, 8):
        spread = [jnp.broadcast_to(a[:, panel + k : panel + k + 1], a.shape) for k in range(8)]
        row_at = lax.broadcasted_iota(jnp.int32, a.shape, 0)
        for k in range(8):
            pivot = spread[k][k : k + 1, :]
            row = a[k : k + 1, :]
            inverse_ref[panel + k : panel + k + 1, :] = (row * lax.rsqrt(pivot))[:, RANK:]
            ratio = jnp.where(row_at > k, spread[k] * (1.0 / pivot), 0.0)
            a = a - ratio * row
            for later in range(k + 1, 8):
                spread[later] = spread[later] - ratio * spread[later][k : k + 1, :]
        a = a[8:]


def inverse_lower(gram):
    return pl.pallas_call(
        inverse_kernel,
        out_shape=jax.ShapeDtypeStruct((RANK, RANK), jnp.float32),
        compiler_params=pltpu.CompilerParams(vmem_limit_bytes=VMEM_LIMIT),
        cost_estimate=pl.CostEstimate(flops=RANK**3, bytes_accessed=RANK * RANK * 8, transcendentals=RANK),
        name="inverse",
    )(gram)


def final_kernel(half_ref, grad_ref, error_ref, own_ref, other_ref, right_ref, inverse_ref, update_ref, residual_ref, new_q_ref, update_buf, residual_buf, update_sems, residual_sems):
    new_q_t = mm_highest(inverse_ref[...], right_ref[...]) * (1.0 / REPLICAS)
    new_q_ref[...] = new_q_t
    mixed = mm_highest(inverse_ref[...], new_q_t, ((0,), (0,)))
    spread = []
    for part in split2(mixed):
        none = jnp.zeros_like(part)
        two = jnp.concatenate([jnp.concatenate([part, none], axis=1), jnp.concatenate([none, part], axis=1)], axis=0)
        spread.append(jnp.concatenate([two, two], axis=0))
    copies = []
    for h, factor_ref in enumerate((own_ref, other_ref)):
        side = half_ref[0] if h == 0 else 1 - half_ref[0]
        start = pl.multiple_of(side * HALF, HALF)
        for k in range(STEPS):
            rows, held, n = pl.ds(k * BLOCK, BLOCK), pl.ds(h * HALF + k * BLOCK, BLOCK), h * STEPS + k
            target = pl.ds(start + k * BLOCK, BLOCK)
            pair = jnp.concatenate(split2(factor_ref[rows, :]), axis=1)
            wide = mm(pair, spread[0]) + mm(pair, spread[1])
            for part in range(2):
                lowrank = wide[:, part * 128 : part * 128 + 128]
                update_buf[part, held, :] = lowrank.astype(jnp.bfloat16)
                residual_buf[part, held, :] = grad_ref[part, target, :].astype(jnp.float32) + error_ref[part, target, :] - lowrank
            for copy in (
                pltpu.make_async_copy(update_buf.at[:, held, :], update_ref.at[:, target, :], update_sems.at[n]),
                pltpu.make_async_copy(residual_buf.at[:, held, :], residual_ref.at[:, target, :], residual_sems.at[n]),
            ):
                copy.start()
                copies.append(copy)
    for copy in copies:
        copy.wait()


def final(half, grad, error, own, other, right, inverse):
    return pl.pallas_call(
        final_kernel,
        out_shape=(
            jax.ShapeDtypeStruct((2, ROWS // 2, COLS), jnp.bfloat16),
            jax.ShapeDtypeStruct((2, ROWS // 2, COLS), jnp.float32),
            jax.ShapeDtypeStruct((RANK, COLS), jnp.float32),
        ),
        in_specs=[SMEM] + [VMEM] * 6,
        out_specs=(HBM, HBM, VMEM),
        scratch_shapes=[
            pltpu.VMEM((2, ROWS // 2, COLS), jnp.bfloat16),
            pltpu.VMEM((2, ROWS // 2, COLS), jnp.float32),
            pltpu.SemaphoreType.DMA((2 * STEPS,)),
            pltpu.SemaphoreType.DMA((2 * STEPS,)),
        ],
        compiler_params=pltpu.CompilerParams(vmem_limit_bytes=VMEM_LIMIT),
        cost_estimate=pl.CostEstimate(flops=2 * 2 * HALF * 256 * 256 * 2, bytes_accessed=ROWS * COLS * 6, transcendentals=0),
        name="final",
    )(half, grad, error, own, other, right, inverse)


def swap(a):
    return lax.ppermute(a, "c", [(0, 1), (1, 0)])


def scatter_sum(a, axes, count):
    return lax.all_to_all(a, axes, 0, 0, tiled=True).reshape(count, -1, 128).sum(0)


def gather(a, axes, count):
    return lax.all_to_all(jnp.tile(a, (count, 1)), axes, 0, 0, tiled=True)


def sum_over_replicas(a):
    a = a + swap(a)
    for axis in ("y", "x"):
        for pairs in (PAIR_A, PAIR_B):
            a = a + lax.ppermute(a, axis, pairs)
    return a


def sum_over_ring8(a):
    inner = [(i, i ^ 1) for i in range(8)]
    outer = [(i, (i + 1) % 8 if i % 2 else (i - 1) % 8) for i in range(8)]
    pair = a + lax.ppermute(a, "z", inner)
    near = lax.ppermute(pair, "z", outer)
    far = lax.ppermute(near, "z", inner)
    opposite = lax.ppermute(far, "z", outer)
    return (pair + near) + (far + opposite)


def shards(grad, error, warm_q):
    grad = grad.reshape(2, ROWS // 2, COLS)
    error = error.reshape(2, ROWS // 2, COLS)
    warm_t = warm_q.T
    half = lax.axis_index("c").astype(jnp.int32).reshape(1)
    away = left_half(1 - half, grad, error, warm_t)
    keep = left_half(half, grad, error, warm_t)
    piece = scatter_sum(keep + swap(away), ("x", "y"), 16)
    piece = sum_over_ring8(piece)
    own = gather(piece, ("x", "y"), 16)
    other = swap(own)
    sums = right_own(half, grad, error, own)
    right, gram = right_other(half, grad, error, other, sums)
    inverse = inverse_lower(gram)
    right = sum_over_replicas(right)
    update, residual, new_q_t = final(half, grad, error, own, other, right, inverse)
    return update.reshape(ROWS, COLS), residual.reshape(1, ROWS, COLS), new_q_t.T


def solution(mesh):
    grid = Mesh(mesh.devices.reshape(4, 4, 2, 8), ("x", "y", "c", "z"))
    replicas = ("x", "y", "c")
    return jax.shard_map(
        shards,
        mesh=grid,
        in_specs=(P(replicas, None, "z"), P(replicas, None, "z"), P("z", None)),
        out_specs=(P(None, "z"), P(replicas, None, "z"), P("z", None)),
        check_vma=False,
    )
```

time: 450 us -> 99.5 us (0.22)
  the two profiles are of different devices: /device:TPU:96 before, /device:TPU:6 now
where the time goes in v2:
time: 99.5 us; the launch traced here: 99.3 us
  blocking collectives  39.2 us (39%)
  waiting for transfers between devices  24.4 us (25%)
  Pallas kernels  15.8 us (16%)
  starting transfers between devices  15.7 us (16%)
  local copies, waits for them, and re-layouts  3.04 us (3%)
    all_to_all x1, blocking collectives, scatter_sum(): lax.all_to_all(a, axes, 0, 0, tiled=True).reshape(count, -1, 128).sum(0)  23 us
    all_to_all x1, blocking collectives, gather(): return lax.all_to_all(jnp.tile(a, (count, 1)), axes, 0, 0, tiled=True)  16.3 us
    ppermute x4, waiting for transfers between devices, sum_over_replicas(): a = a + lax.ppermute(a, axis, pairs)  12.4 us
    ppermute x1, starting transfers between devices, sum_over_ring8(): near = lax.ppermute(pair, 'z', outer)  5.94 us
    pallas_call x2, Pallas kernels, left_half(): pl.pallas_call(left_kernel, out_shape=jax.ShapeDtypeStruct((HALF, 128), j...  5.85 us
    ppermute x1, waiting for transfers between devices, sum_over_ring8(): far = lax.ppermute(near, 'z', inner)  4.26 us
    pallas_call x1, Pallas kernels, final(): pl.pallas_call(final_kernel, out_shape=(jax.ShapeDtypeStruct((2, ROWS //...  4.23 us
    ppermute x4, starting transfers between devices, sum_over_replicas(): a = a + lax.ppermute(a, axis, pairs)  3.85 us
  transfers between devices with their start and end apart: 11, of which 9 were waited for; matrix products, arithmetic and copies ran while one was open for 0% of the time, Pallas kernels for 7%

profile of v2, /device:TPU:6, one launch (start us, length us, event | category | flops | bytes accessed | tf_op | source)
XLA Modules:
  0.0 99.3 jit_solution(9336476968555430856)
XLA Ops:
  0.6 0.0 copy-start.2
  0.6 0.7 copy-done.2
  1.4 0.0 copy-start.3
  1.4 2.9 %left.3 = f32[2048,128]{1,0:T(8,128)S(1)} custom-call(s32[1]{0:T(128)S(6)} %sub.3.half_ref, bf16[2,4096,128]{2,1,0:T(8,128)(2,1)} %bitcast.14, f32[2,4096,128]{2,1,0:T(8,128)} %bitcast.9, f32[64,128]{1,0:T(8,128)S(1)} %bitcast.22), custom_call_target="tpu_custom_call" | custom-call | flops 536870912 | bytes 3145728 | tf_op jit(solution)/shard_map/left/pallas_call | solution.py:78
  4.3 0.1 collective-permute-start
  4.4 0.0 copy-done.3
  4.4 2.9 %left.2 = f32[2048,128]{1,0:T(8,128)S(1)} custom-call(s32[1]{0:T(128)} %bitcast.half_ref, bf16[2,4096,128]{2,1,0:T(8,128)(2,1)} %bitcast.15, f32[2,4096,128]{2,1,0:T(8,128)} %bitcast.10, f32[64,128]{1,0:T(8,128)S(1)} %bitcast.23), custom_call_target="tpu_custom_call" | custom-call | flops 536870912 | bytes 3145728 | tf_op jit(solution)/shard_map/left/pallas_call | solution.py:78
  7.4 0.0 collective-permute-done
  7.4 0.1 add.30
  7.5 0.0 copy-start.1
  7.5 23.0 %all_to_all.17 = f32[16,128,128]{2,1,0:T(8,128)S(1)} all-to-all(f32[16,128,128]{2,1,0:T(8,128)S(1)} %bitcast.24), channel_id=1, replica_groups=mesh['x'=4,'y'=4,'c'=2,'z'=8] {'x','y'}, dimensions={0} | all-to-all | bytes 2097152 | tf_op jit(solution)/shard_map/all_to_all | solution.py:246
  30.5 0.1 reduce_sum.9
  30.5 2.0 %collective-permute-start.1 = (f32[128,128]{1,0:T(8,128)S(1)}, f32[128,128]{1,0:T(8,128)S(1)}, u32[]{:S(2)}, u32[]{:S(2)}) collective-permute-start(f32[128,128]{1,0:T(8,128)S(1)} %reduce_sum.9), channel_id=1, source_target_pairs={{0,1},{1,0},{2,3},{3,2},{4,5},{5,4},{6,7},{7,6},{8,9},{9,8},{10,11... | collective-permute-start | bytes 196616 | tf_op jit(solution)/shard_map/ppermute | solution.py:264
  32.5 2.3 %collective-permute-done.1 = f32[128,128]{1,0:T(8,128)S(1)} collective-permute-done((f32[128,128]{1,0:T(8,128)S(1)}, f32[128,128]{1,0:T(8,128)S(1)}, u32[]{:S(2)}, u32[]{:S(2)}) %collective-permute-start.1) | collective-permute-done | bytes 65568 | tf_op jit(solution)/shard_map/ppermute | solution.py:264
  34.9 5.9 %collective-permute-start.2 = (f32[128,128]{1,0:T(8,128)S(1)}, f32[128,128]{1,0:T(8,128)S(1)}, u32[]{:S(2)}, u32[]{:S(2)}) collective-permute-start(f32[128,128]{1,0:T(8,128)S(1)} %add.31), channel_id=1, source_target_pairs={{0,7},{1,2},{2,1},{3,4},{4,3},{5,6},{6,5},{7,0},{8,15},{9,10},{10,... | collective-permute-start | bytes 196616 | tf_op jit(solution)/shard_map/ppermute | solution.py:265
  40.8 2.2 %collective-permute-done.2 = f32[128,128]{1,0:T(8,128)S(1)} collective-permute-done((f32[128,128]{1,0:T(8,128)S(1)}, f32[128,128]{1,0:T(8,128)S(1)}, u32[]{:S(2)}, u32[]{:S(2)}) %collective-permute-start.2) | collective-permute-done | bytes 65568 | tf_op jit(solution)/shard_map/ppermute | solution.py:265
  43.1 0.0 collective-permute-start.3
  43.1 4.3 %collective-permute-done.3 = f32[128,128]{1,0:T(8,128)S(1)} collective-permute-done((f32[128,128]{1,0:T(8,128)S(1)}, f32[128,128]{1,0:T(8,128)S(1)}, u32[]{:S(2)}, u32[]{:S(2)}) %collective-permute-start.3) | collective-permute-done | bytes 65568 | tf_op jit(solution)/shard_map/ppermute | solution.py:266
  47.3 3.2 %collective-permute-start.4 = (f32[128,128]{1,0:T(8,128)S(1)}, f32[128,128]{1,0:T(8,128)S(1)}, u32[]{:S(2)}, u32[]{:S(2)}) collective-permute-start(f32[128,128]{1,0:T(8,128)S(1)} %collective-permute-done.3), channel_id=1, source_target_pairs={{0,7},{1,2},{2,1},{3,4},{4,3},{5,6},{6,5},{7,0},{8,15},{9,10},{10,... | collective-permute-start | bytes 196616 | tf_op jit(solution)/shard_map/ppermute | solution.py:267
  50.6 2.2 %collective-permute-done.4 = f32[128,128]{1,0:T(8,128)S(1)} collective-permute-done((f32[128,128]{1,0:T(8,128)S(1)}, f32[128,128]{1,0:T(8,128)S(1)}, u32[]{:S(2)}, u32[]{:S(2)}) %collective-permute-start.4) | collective-permute-done | bytes 65568 | tf_op jit(solution)/shard_map/ppermute | solution.py:267
  52.8 0.1 tile.2
  52.9 16.3 %all_to_all.18 = f32[16,128,128]{2,1,0:T(8,128)S(1)} all-to-all(f32[16,128,128]{2,1,0:T(8,128)S(1)} %tile.2), channel_id=1, replica_groups=mesh['x'=4,'y'=4,'c'=2,'z'=8] {'x','y'}, dimensions={0} | all-to-all | bytes 2097152 | tf_op jit(solution)/shard_map/all_to_all | solution.py:250
  69.2 0.0 collective-permute-start.5
  69.2 0.0 copy-done.1
  69.2 0.0 copy-start
  69.2 2.2 %copy-done = f32[1,8192,128]{2,1,0:T(8,128)S(1)} copy-done((f32[1,8192,128]{2,1,0:T(8,128)S(1)}, f32[1,8192,128]{2,1,0:T(8,128)}, u32[]{:S(2)}) %copy-start) | copy-done | bytes 4194328
  71.4 1.9 %right_own.1 = (f32[256,256]{1,0:T(8,128)S(1)}, f32[256,256]{1,0:T(8,128)S(1)}, f32[128,128]{1,0:T(8,128)S(1)}) custom-call(s32[1]{0:T(128)} %bitcast.half_ref, bf16[2,4096,128]{2,1,0:T(8,128)(2,1)S(1)} %bitcast.16, f32[2,4096,128]{2,1,0:T(8,128)S(1)} %bitcast.11, f32[2048,128]{1,0:T(8,128)S(1)} %bitcast.20), custom_call_target="tpu_custom_call" | custom-call | flops 939524096 | bytes 3145728 | tf_op jit(solution)/shard_map/right_own/pallas_call | solution.py:137
  73.3 0.0 collective-permute-done.5.factor_ref.other_ref
  73.3 2.0 %right_other.1 = (f32[64,128]{1,0:T(8,128)S(1)}, f32[64,64]{1,0:T(8,128)S(1)}) custom-call(s32[1]{0:T(128)} %bitcast.half_ref, bf16[2,4096,128]{2,1,0:T(8,128)(2,1)S(1)} %bitcast.17, f32[2,4096,128]{2,1,0:T(8,128)S(1)} %bitcast.12, f32[2048,128]{1,0:T(8,128)S(1)} %collective-permute-done.5.factor_ref.other_ref, f32[256,256]{1,0:T(8,128)S(1)} %get-tuple-element.11.acc_in, ...), custom_call_target="tpu_custom_call" | custom-call | flops 939524096 | bytes 3145728 | tf_op jit(solution)/shard_map/right_other/pallas_call | solution.py:149
  75.3 0.6 collective-permute-start.6
  75.9 0.9 collective-permute-done.6
  76.8 0.6 collective-permute-start.7
  77.3 3.3 %collective-permute-done.7 = f32[64,128]{1,0:T(8,128)S(1)} collective-permute-done((f32[64,128]{1,0:T(8,128)S(1)}, f32[64,128]{1,0:T(8,128)S(1)}, u32[]{:S(2)}, u32[]{:S(2)}) %collective-permute-start.7) | collective-permute-done | bytes 32800 | tf_op jit(solution)/shard_map/ppermute | solution.py:257
  80.7 0.6 collective-permute-start.8
  81.3 4.5 %collective-permute-done.8 = f32[64,128]{1,0:T(8,128)S(1)} collective-permute-done((f32[64,128]{1,0:T(8,128)S(1)}, f32[64,128]{1,0:T(8,128)S(1)}, u32[]{:S(2)}, u32[]{:S(2)}) %collective-permute-start.8) | collective-permute-done | bytes 32800 | tf_op jit(solution)/shard_map/ppermute | solution.py:257
  85.8 0.5 collective-permute-start.9
  86.3 3.4 %collective-permute-done.9 = f32[64,128]{1,0:T(8,128)S(1)} collective-permute-done((f32[64,128]{1,0:T(8,128)S(1)}, f32[64,128]{1,0:T(8,128)S(1)}, u32[]{:S(2)}, u32[]{:S(2)}) %collective-permute-start.9) | collective-permute-done | bytes 32800 | tf_op jit(solution)/shard_map/ppermute | solution.py:257
  89.7 2.1 %collective-permute-start.10 = (f32[64,128]{1,0:T(8,128)S(1)}, f32[64,128]{1,0:T(8,128)S(1)}, u32[]{:S(2)}, u32[]{:S(2)}) collective-permute-start(f32[64,128]{1,0:T(8,128)S(1)} %add.38), channel_id=1, source_target_pairs={{64,128},{128,64},{192,0},{0,192},{65,129},{129,65},{193,1},{1,193... | collective-permute-start | bytes 98312 | tf_op jit(solution)/shard_map/ppermute | solution.py:257
  91.9 1.8 %inverse.1.inverse_ref = f32[64,64]{1,0:T(8,128)S(1)} custom-call(f32[64,64]{1,0:T(8,128)S(1)} %get-tuple-element.15.gram_ref), custom_call_target="tpu_custom_call" | custom-call | flops 262144 | bytes 32768 | tf_op jit(solution)/shard_map/inverse/pallas_call | solution.py:178
  93.7 1.2 %collective-permute-done.10 = f32[64,128]{1,0:T(8,128)S(1)} collective-permute-done((f32[64,128]{1,0:T(8,128)S(1)}, f32[64,128]{1,0:T(8,128)S(1)}, u32[]{:S(2)}, u32[]{:S(2)}) %collective-permute-start.10) | collective-permute-done | bytes 32800 | tf_op jit(solution)/shard_map/ppermute | solution.py:257
  94.9 4.2 %final.1 = (bf16[2,4096,128]{2,1,0:T(8,128)(2,1)}, f32[2,4096,128]{2,1,0:T(8,128)}, f32[64,128]{1,0:T(8,128)}) custom-call(s32[1]{0:T(128)} %bitcast.half_ref, bf16[2,4096,128]{2,1,0:T(8,128)(2,1)S(1)} %bitcast.18, f32[2,4096,128]{2,1,0:T(8,128)S(1)} %bitcast.13, f32[2048,128]{1,0:T(8,128)S(1)} %bitcast.21, ...), custom_call_target="tpu_custom_call" | custom-call | flops 1073741824 | bytes 6291456 | tf_op jit(solution)/shard_map/final/pallas_call | solution.py:220
  (7 shorter events, 0.1 us)
Async XLA Ops:
  0.6 0.8 copy-start.2
  1.4 3.0 %copy-start.3 = (f32[128,64]{0,1:T(8,128)S(1)}, f32[128,64]{0,1:T(8,128)}, u32[]{:S(2)}) copy-start(f32[128,64]{0,1:T(8,128)} %param.5) | copy-start | bytes 98308
  4.3 3.1 %collective-permute-start = (f32[2048,128]{1,0:T(8,128)S(1)}, f32[2048,128]{1,0:T(8,128)S(1)}, u32[]{:S(2)}, u32[]{:S(2)}) collective-permute-start(f32[2048,128]{1,0:T(8,128)S(1)} %left.3), channel_id=1, source_target_pairs={{0,8},{8,0},{1,9},{9,1},{2,10},{10,2},{3,11},{11,3},{4,12},{12,4},... | collective-permute-start | bytes 3145736 | tf_op jit(solution)/shard_map/ppermute | solution.py:242
  7.5 61.7 %copy-start.1 = (bf16[1,8192,128]{2,1,0:T(8,128)(2,1)S(1)}, bf16[1,8192,128]{2,1,0:T(8,128)(2,1)}, u32[]{:S(2)}) copy-start(bf16[1,8192,128]{2,1,0:T(8,128)(2,1)} %param.3) | copy-start | bytes 6291460
  30.5 4.4 %collective-permute-start.1 = (f32[128,128]{1,0:T(8,128)S(1)}, f32[128,128]{1,0:T(8,128)S(1)}, u32[]{:S(2)}, u32[]{:S(2)}) collective-permute-start(f32[128,128]{1,0:T(8,128)S(1)} %reduce_sum.9), channel_id=1, source_target_pairs={{0,1},{1,0},{2,3},{3,2},{4,5},{5,4},{6,7},{7,6},{8,9},{9,8},{10,11... | collective-permute-start | bytes 196616 | tf_op jit(solution)/shard_map/ppermute | solution.py:264
  34.9 8.2 %collective-permute-start.2 = (f32[128,128]{1,0:T(8,128)S(1)}, f32[128,128]{1,0:T(8,128)S(1)}, u32[]{:S(2)}, u32[]{:S(2)}) collective-permute-start(f32[128,128]{1,0:T(8,128)S(1)} %add.31), channel_id=1, source_target_pairs={{0,7},{1,2},{2,1},{3,4},{4,3},{5,6},{6,5},{7,0},{8,15},{9,10},{10,... | collective-permute-start | bytes 196616 | tf_op jit(solution)/shard_map/ppermute | solution.py:265
  43.1 4.3 %collective-permute-start.3 = (f32[128,128]{1,0:T(8,128)S(1)}, f32[128,128]{1,0:T(8,128)S(1)}, u32[]{:S(2)}, u32[]{:S(2)}) collective-permute-start(f32[128,128]{1,0:T(8,128)S(1)} %collective-permute-done.2), channel_id=1, source_target_pairs={{0,1},{1,0},{2,3},{3,2},{4,5},{5,4},{6,7},{7,6},{8,9},{9,8},{10,11... | collective-permute-start | bytes 196616 | tf_op jit(solution)/shard_map/ppermute | solution.py:266
  47.3 5.5 %collective-permute-start.4 = (f32[128,128]{1,0:T(8,128)S(1)}, f32[128,128]{1,0:T(8,128)S(1)}, u32[]{:S(2)}, u32[]{:S(2)}) collective-permute-start(f32[128,128]{1,0:T(8,128)S(1)} %collective-permute-done.3), channel_id=1, source_target_pairs={{0,7},{1,2},{2,1},{3,4},{4,3},{5,6},{6,5},{7,0},{8,15},{9,10},{10,... | collective-permute-start | bytes 196616 | tf_op jit(solution)/shard_map/ppermute | solution.py:267
  69.2 4.1 %collective-permute-start.5 = (f32[2048,128]{1,0:T(8,128)S(1)}, f32[2048,128]{1,0:T(8,128)S(1)}, u32[]{:S(2)}, u32[]{:S(2)}) collective-permute-start(f32[2048,128]{1,0:T(8,128)S(1)} %bitcast.19), channel_id=1, source_target_pairs={{0,8},{8,0},{1,9},{9,1},{2,10},{10,2},{3,11},{11,3},{4,12},{12,4},... | collective-permute-start | bytes 3145736 | tf_op jit(solution)/shard_map/ppermute | solution.py:242
  69.2 2.2 %copy-start = (f32[1,8192,128]{2,1,0:T(8,128)S(1)}, f32[1,8192,128]{2,1,0:T(8,128)}, u32[]{:S(2)}) copy-start(f32[1,8192,128]{2,1,0:T(8,128)} %param.4) | copy-start | bytes 12582916
  75.3 1.5 %collective-permute-start.6 = (f32[64,128]{1,0:T(8,128)S(1)}, f32[64,128]{1,0:T(8,128)S(1)}, u32[]{:S(2)}, u32[]{:S(2)}) collective-permute-start(f32[64,128]{1,0:T(8,128)S(1)} %get-tuple-element.14), channel_id=1, source_target_pairs={{0,8},{8,0},{1,9},{9,1},{2,10},{10,2},{3,11},{11,3},{4,12},{12,4},... | collective-permute-start | bytes 98312 | tf_op jit(solution)/shard_map/ppermute | solution.py:242
  76.8 3.9 %collective-permute-start.7 = (f32[64,128]{1,0:T(8,128)S(1)}, f32[64,128]{1,0:T(8,128)S(1)}, u32[]{:S(2)}, u32[]{:S(2)}) collective-permute-start(f32[64,128]{1,0:T(8,128)S(1)} %add.35), channel_id=1, source_target_pairs={{0,16},{16,0},{32,48},{48,32},{1,17},{17,1},{33,49},{49,33},{2,18}... | collective-permute-start | bytes 98312 | tf_op jit(solution)/shard_map/ppermute | solution.py:257
  80.7 5.1 %collective-permute-start.8 = (f32[64,128]{1,0:T(8,128)S(1)}, f32[64,128]{1,0:T(8,128)S(1)}, u32[]{:S(2)}, u32[]{:S(2)}) collective-permute-start(f32[64,128]{1,0:T(8,128)S(1)} %add.36), channel_id=1, source_target_pairs={{16,32},{32,16},{48,0},{0,48},{17,33},{33,17},{49,1},{1,49},{18,34... | collective-permute-start | bytes 98312 | tf_op jit(solution)/shard_map/ppermute | solution.py:257
  85.8 3.9 %collective-permute-start.9 = (f32[64,128]{1,0:T(8,128)S(1)}, f32[64,128]{1,0:T(8,128)S(1)}, u32[]{:S(2)}, u32[]{:S(2)}) collective-permute-start(f32[64,128]{1,0:T(8,128)S(1)} %add.37), channel_id=1, source_target_pairs={{0,64},{64,0},{128,192},{192,128},{1,65},{65,1},{129,193},{193,129... | collective-permute-start | bytes 98312 | tf_op jit(solution)/shard_map/ppermute | solution.py:257
  89.7 5.1 %collective-permute-start.10 = (f32[64,128]{1,0:T(8,128)S(1)}, f32[64,128]{1,0:T(8,128)S(1)}, u32[]{:S(2)}, u32[]{:S(2)}) collective-permute-start(f32[64,128]{1,0:T(8,128)S(1)} %add.38), channel_id=1, source_target_pairs={{64,128},{128,64},{192,0},{0,192},{65,129},{129,65},{193,1},{1,193... | collective-permute-start | bytes 98312 | tf_op jit(solution)/shard_map/ppermute | solution.py:257

commit v3 on v2

--- a/solution.py
+++ b/solution.py
@@ -94,11 +94,7 @@
     )(half, grad, error, warm_t)
 
 
-def rows_of(side, offset):
-    return pl.ds(pl.multiple_of(side * HALF + offset, RIGHT_BLOCK), RIGHT_BLOCK)
-
-
-def add_half(side, grad_ref, error_ref, factor_ref, acc_ref, gram_ref, tail_ref):
+def add_half(combined_ref, factor_ref, acc_ref, gram_ref, tail_ref):
     @pl.loop(0, HALF, step=RIGHT_BLOCK)
     def _(start):
         rows = pl.ds(pl.multiple_of(start, RIGHT_BLOCK), RIGHT_BLOCK)
@@ -106,25 +102,23 @@
         high = factor.astype(jnp.bfloat16)
         middle, low = split2(factor - high.astype(jnp.float32))
         pair = jnp.concatenate([high, middle], axis=1)
-        source = rows_of(side, start)
-        combined = grad_ref[:, source, :].astype(jnp.float32) + error_ref[:, source, :]
-        top_high, top_low = split2(combined[0])
-        bottom_high, bottom_low = split2(combined[1])
+        top_high, top_low = split2(combined_ref[0, rows, :])
+        bottom_high, bottom_low = split2(combined_ref[1, rows, :])
         acc_ref[...] += mm_t(pair, jnp.concatenate([top_high, bottom_high], axis=1)) + mm_t(pair, jnp.concatenate([top_low, bottom_low], axis=1))
         gram_ref[...] += mm_t(pair, pair)
         tail_ref[...] += mm_t(high, low)
 
 
-def right_own_kernel(half_ref, grad_ref, error_ref, factor_ref, acc_ref, gram_ref, tail_ref):
+def right_own_kernel(combined_ref, factor_ref, acc_ref, gram_ref, tail_ref):
     for ref in (acc_ref, gram_ref, tail_ref):
         ref[...] = jnp.zeros_like(ref)
-    add_half(half_ref[0], grad_ref, error_ref, factor_ref, acc_ref, gram_ref, tail_ref)
-
-
-def right_other_kernel(half_ref, grad_ref, error_ref, factor_ref, acc_in, gram_in, tail_in, right_ref, gram_ref, acc_ref, gram_acc_ref, tail_acc_ref):
+    add_half(combined_ref, factor_ref, acc_ref, gram_ref, tail_ref)
+
+
+def right_other_kernel(combined_ref, factor_ref, acc_in, gram_in, tail_in, right_ref, gram_ref, acc_ref, gram_acc_ref, tail_acc_ref):
     for ref, given in ((acc_ref, acc_in), (gram_acc_ref, gram_in), (tail_acc_ref, tail_in)):
         ref[...] = given[...]
-    add_half(1 - half_ref[0], grad_ref, error_ref, factor_ref, acc_ref, gram_acc_ref, tail_acc_ref)
+    add_half(combined_ref, factor_ref, acc_ref, gram_acc_ref, tail_acc_ref)
     right = acc_ref[0:128, :] + acc_ref[128:256, :]
     right_ref[...] = right[0:64, 0:128] + right[64:128, 128:256]
     cross = gram_acc_ref[0:128, 128:256] + tail_acc_ref[...]
@@ -132,30 +126,30 @@
     gram_ref[...] = gram[0:64, 0:64] + gram[64:128, 64:128]
 
 
-def right_own(half, grad, error, factor):
+def right_own(combined, factor):
     square = jax.ShapeDtypeStruct((256, 256), jnp.float32)
     return pl.pallas_call(
         right_own_kernel,
         out_shape=(square, square, jax.ShapeDtypeStruct((128, 128), jnp.float32)),
-        in_specs=[SMEM] + [VMEM] * 3,
+        in_specs=[VMEM] * 2,
         out_specs=(VMEM,) * 3,
         compiler_params=pltpu.CompilerParams(vmem_limit_bytes=VMEM_LIMIT),
         cost_estimate=pl.CostEstimate(flops=7 * HALF * 256 * 256, bytes_accessed=ROWS * COLS * 3, transcendentals=0),
         name="right_own",
-    )(half, grad, error, factor)
-
-
-def right_other(half, grad, error, factor, sums):
+    )(combined, factor)
+
+
+def right_other(combined, factor, sums):
     return pl.pallas_call(
         right_other_kernel,
         out_shape=(jax.ShapeDtypeStruct((RANK, COLS), jnp.float32), jax.ShapeDtypeStruct((RANK, RANK), jnp.float32)),
-        in_specs=[SMEM] + [VMEM] * 6,
+        in_specs=[VMEM] * 5,
         out_specs=(VMEM, VMEM),
         scratch_shapes=[pltpu.VMEM((256, 256), jnp.float32)] * 2 + [pltpu.VMEM((128, 128), jnp.float32)],
         compiler_params=pltpu.CompilerParams(vmem_limit_bytes=VMEM_LIMIT),
         cost_estimate=pl.CostEstimate(flops=7 * HALF * 256 * 256, bytes_accessed=ROWS * COLS * 3, transcendentals=0),
         name="right_other",
-    )(half, grad, error, factor, *sums)
+    )(combined, factor, *sums)
 
 
 def inverse_kernel(gram_ref, inverse_ref):
@@ -184,7 +178,7 @@
     )(gram)
 
 
-def final_kernel(half_ref, grad_ref, error_ref, own_ref, other_ref, right_ref, inverse_ref, update_ref, residual_ref, new_q_ref, update_buf, residual_buf, update_sems, residual_sems):
+def final_kernel(half_ref, own_combined_ref, other_combined_ref, own_ref, other_ref, right_ref, inverse_ref, update_ref, residual_ref, new_q_ref, update_buf, residual_buf, update_sems, residual_sems):
     new_q_t = mm_highest(inverse_ref[...], right_ref[...]) * (1.0 / REPLICAS)
     new_q_ref[...] = new_q_t
     mixed = mm_highest(inverse_ref[...], new_q_t, ((0,), (0,)))
@@ -194,7 +188,7 @@
         two = jnp.concatenate([jnp.concatenate([part, none], axis=1), jnp.concatenate([none, part], axis=1)], axis=0)
         spread.append(jnp.concatenate([two, two], axis=0))
     copies = []
-    for h, factor_ref in enumerate((own_ref, other_ref)):
+    for h, (combined_ref, factor_ref) in enumerate(((own_combined_ref, own_ref), (other_combined_ref, other_ref))):
         side = half_ref[0] if h == 0 else 1 - half_ref[0]
         start = pl.multiple_of(side * HALF, HALF)
         for k in range(STEPS):
@@ -205,7 +199,7 @@
             for part in range(2):
                 lowrank = wide[:, part * 128 : part * 128 + 128]
                 update_buf[part, held, :] = lowrank.astype(jnp.bfloat16)
-                residual_buf[part, held, :] = grad_ref[part, target, :].astype(jnp.float32) + error_ref[part, target, :] - lowrank
+                residual_buf[part, held, :] = combined_ref[part, rows, :] - lowrank
             for copy in (
                 pltpu.make_async_copy(update_buf.at[:, held, :], update_ref.at[:, target, :], update_sems.at[n]),
                 pltpu.make_async_copy(residual_buf.at[:, held, :], residual_ref.at[:, target, :], residual_sems.at[n]),
@@ -216,7 +210,7 @@
         copy.wait()
 
 
-def final(half, grad, error, own, other, right, inverse):
+def final(half, own_combined, other_combined, own, other, right, inverse):
     return pl.pallas_call(
         final_kernel,
         out_shape=(
@@ -235,7 +229,7 @@
         compiler_params=pltpu.CompilerParams(vmem_limit_bytes=VMEM_LIMIT),
         cost_estimate=pl.CostEstimate(flops=2 * 2 * HALF * 256 * 256 * 2, bytes_accessed=ROWS * COLS * 6, transcendentals=0),
         name="final",
-    )(half, grad, error, own, other, right, inverse)
+    )(half, own_combined, other_combined, own, other, right, inverse)
 
 
 def swap(a):
@@ -250,22 +244,24 @@
     return lax.all_to_all(jnp.tile(a, (count, 1)), axes, 0, 0, tiled=True)
 
 
-def sum_over_replicas(a):
+def sum_over_replicas(a, gram):
     a = a + swap(a)
     for axis in ("y", "x"):
         for pairs in (PAIR_A, PAIR_B):
             a = a + lax.ppermute(a, axis, pairs)
-    return a
-
-
-def sum_over_ring8(a):
-    inner = [(i, i ^ 1) for i in range(8)]
-    outer = [(i, (i + 1) % 8 if i % 2 else (i - 1) % 8) for i in range(8)]
-    pair = a + lax.ppermute(a, "z", inner)
-    near = lax.ppermute(pair, "z", outer)
-    far = lax.ppermute(near, "z", inner)
-    opposite = lax.ppermute(far, "z", outer)
-    return (pair + near) + (far + opposite)
+        if axis == "y":
+            a, inverse = lax.optimization_barrier((a, inverse_lower(gram)))
+    return a, inverse
+
+
+def combined_half(grad, error, half):
+    start = half[0] * HALF
+    part = (2, HALF, COLS)
+    return lax.dynamic_slice(grad, (0, start, 0), part).astype(jnp.float32) + lax.dynamic_slice(error, (0, start, 0), part)
+
+
+RING_A = [(i, i ^ 1) for i in range(8)]
+RING_B = [(i, (i + 1) % 8 if i % 2 else (i - 1) % 8) for i in range(8)]
 
 
 def shards(grad, error, warm_q):
@@ -276,14 +272,20 @@
     away = left_half(1 - half, grad, error, warm_t)
     keep = left_half(half, grad, error, warm_t)
     piece = scatter_sum(keep + swap(away), ("x", "y"), 16)
-    piece = sum_over_ring8(piece)
+    pair = piece + lax.ppermute(piece, "z", RING_A)
+    pair, grad, error = lax.optimization_barrier((pair, grad, error))
+    near = lax.ppermute(pair, "z", RING_B)
+    near, own_combined, grad, error = lax.optimization_barrier((near, combined_half(grad, error, half), grad, error))
+    far = lax.ppermute(near, "z", RING_A)
+    far, other_combined = lax.optimization_barrier((far, combined_half(grad, error, 1 - half)))
+    opposite = lax.ppermute(far, "z", RING_B)
+    piece = (pair + near) + (far + opposite)
     own = gather(piece, ("x", "y"), 16)
     other = swap(own)
-    sums = right_own(half, grad, error, own)
-    right, gram = right_other(half, grad, error, other, sums)
-    inverse = inverse_lower(gram)
-    right = sum_over_replicas(right)
-    update, residual, new_q_t = final(half, grad, error, own, other, right, inverse)
+    sums = right_own(own_combined, own)
+    right, gram = right_other(other_combined, other, sums)
+    right, inverse = sum_over_replicas(right, gram)
+    update, residual, new_q_t = final(half, own_combined, other_combined, own, other, right, inverse)
     return update.reshape(ROWS, COLS), residual.reshape(1, ROWS, COLS), new_q_t.T
 
 

time: 99.5 us -> 97.7 us (0.982)
  other arithmetic: 0.22 us -> 3.78 us
  waiting for transfers between devices: 24.4 us -> 21.9 us
  local copies, waits for them, and re-layouts: 3.04 us -> 0.86 us
    ppermute x4, waiting for transfers between devices: 11.1 us -> 7.57 us  [the longest x1 2.77 us: shards(): far = lax.ppermute(near, 'z', RING_A)]
    add x2 -> x4, other arithmetic: 0.03 us -> 3.55 us  [the longest x2 3.52 us: combined_half(): lax.dynamic_slice(grad, (0, start, 0), part).astype(jnp.float32)]
    unnamed x8 -> x6, local copies, waits for them, and re-layouts: 2.95 us -> 0.76 us
    ppermute x3, waiting for transfers between devices: 0.87 us -> 1.9 us  [swap(): return lax.ppermute(a, 'c', [(0, 1), (1, 0)])]
  transfers between devices with their start and end apart: 11 -> 11, of which waited for: 9 -> 10; matrix products, arithmetic and copies ran while one was open for 0% -> 4% of each run, Pallas kernels for 7% -> 7%
where the time goes in v3:
time: 97.7 us; the launch traced here: 97.4 us
  blocking collectives  39.1 us (40%)
  waiting for transfers between devices  21.9 us (22%)
  Pallas kernels  15.7 us (16%)
  starting transfers between devices  15.3 us (16%)
  other arithmetic  3.78 us (4%)
    all_to_all x1, blocking collectives, scatter_sum(): lax.all_to_all(a, axes, 0, 0, tiled=True).reshape(count, -1, 128).sum(0)  22.8 us
    all_to_all x1, blocking collectives, gather(): return lax.all_to_all(jnp.tile(a, (count, 1)), axes, 0, 0, tiled=True)  16.3 us
    ppermute x4, waiting for transfers between devices, sum_over_replicas(): a = a + lax.ppermute(a, axis, pairs)  12.4 us
    ppermute x1, starting transfers between devices, shards(): near = lax.ppermute(pair, 'z', RING_B)  5.94 us
    pallas_call x2, Pallas kernels, left_half(): pl.pallas_call(left_kernel, out_shape=jax.ShapeDtypeStruct((HALF, 128), j...  5.85 us
    pallas_call x1, Pallas kernels, final(): pl.pallas_call(final_kernel, out_shape=(jax.ShapeDtypeStruct((2, ROWS //...  4.21 us
    ppermute x4, starting transfers between devices, sum_over_replicas(): a = a + lax.ppermute(a, axis, pairs)  3.84 us
    add x2, other arithmetic, combined_half(): lax.dynamic_slice(grad, (0, start, 0), part).astype(jnp.float32)  3.52 us
  transfers between devices with their start and end apart: 11, of which 10 were waited for; matrix products, arithmetic and copies ran while one was open for 4% of the time, Pallas kernels for 7%

profile of v3, /device:TPU:6, one launch (start us, length us, event | category | flops | bytes accessed | tf_op | source)
XLA Modules:
  0.0 97.4 jit_solution(9593402165374738904)
XLA Ops:
  0.6 0.0 copy-start
  0.6 0.7 copy-done
  1.4 0.0 copy-start.1
  1.4 2.9 %left.3 = f32[2048,128]{1,0:T(8,128)S(1)} custom-call(s32[1]{0:T(128)S(6)} %sub.4.half_ref, bf16[2,4096,128]{2,1,0:T(8,128)(2,1)} %bitcast.19, f32[2,4096,128]{2,1,0:T(8,128)} %bitcast.15, f32[64,128]{1,0:T(8,128)S(1)} %bitcast.13), custom_call_target="tpu_custom_call" | custom-call | flops 536870912 | bytes 3145728 | tf_op jit(solution)/shard_map/left/pallas_call | solution.py:78
  4.3 0.1 collective-permute-start
  4.4 0.0 copy-done.1
  4.4 2.9 %left.2 = f32[2048,128]{1,0:T(8,128)S(1)} custom-call(s32[1]{0:T(128)} %bitcast.half_ref, bf16[2,4096,128]{2,1,0:T(8,128)(2,1)} %bitcast.20, f32[2,4096,128]{2,1,0:T(8,128)} %bitcast.16, f32[64,128]{1,0:T(8,128)S(1)} %bitcast.14), custom_call_target="tpu_custom_call" | custom-call | flops 536870912 | bytes 3145728 | tf_op jit(solution)/shard_map/left/pallas_call | solution.py:78
  7.4 0.0 collective-permute-done
  7.4 0.2 add.44
  7.5 22.8 %all_to_all.17 = f32[16,128,128]{2,1,0:T(8,128)S(1)} all-to-all(f32[16,128,128]{2,1,0:T(8,128)S(1)} %bitcast.23), channel_id=1, replica_groups=mesh['x'=4,'y'=4,'c'=2,'z'=8] {'x','y'}, dimensions={0} | all-to-all | bytes 2097152 | tf_op jit(solution)/shard_map/all_to_all | solution.py:240
  30.4 0.1 reduce_sum.9
  30.4 2.0 %collective-permute-start.1 = (f32[128,128]{1,0:T(8,128)S(1)}, f32[128,128]{1,0:T(8,128)S(1)}, u32[]{:S(2)}, u32[]{:S(2)}) collective-permute-start(f32[128,128]{1,0:T(8,128)S(1)} %reduce_sum.9), channel_id=1, source_target_pairs={{0,1},{1,0},{2,3},{3,2},{4,5},{5,4},{6,7},{7,6},{8,9},{9,8},{10,11... | collective-permute-start | bytes 196616 | tf_op jit(solution)/shard_map/ppermute | solution.py:275
  32.4 2.3 %collective-permute-done.1 = f32[128,128]{1,0:T(8,128)S(1)} collective-permute-done((f32[128,128]{1,0:T(8,128)S(1)}, f32[128,128]{1,0:T(8,128)S(1)}, u32[]{:S(2)}, u32[]{:S(2)}) %collective-permute-start.1) | collective-permute-done | bytes 65568 | tf_op jit(solution)/shard_map/ppermute | solution.py:275
  34.8 0.0 copy-start.2
  34.8 5.9 %collective-permute-start.2 = (f32[128,128]{1,0:T(8,128)S(1)}, f32[128,128]{1,0:T(8,128)S(1)}, u32[]{:S(2)}, u32[]{:S(2)}) collective-permute-start(f32[128,128]{1,0:T(8,128)S(1)} %add.45), channel_id=1, source_target_pairs={{0,7},{1,2},{2,1},{3,4},{4,3},{5,6},{6,5},{7,0},{8,15},{9,10},{10,... | collective-permute-start | bytes 196616 | tf_op jit(solution)/shard_map/ppermute | solution.py:277
  40.7 2.0 %dynamic-slice_add_fusion.1.combined_ref.own_combined_ref = f32[2,2048,128]{2,1,0:T(8,128)S(1)} fusion(f32[2,4096,128]{2,1,0:T(8,128)} %bitcast.17, s32[]{:T(128)S(6)} %select_n.8, bf16[2,4096,128]{2,1,0:T(8,128)(2,1)} %bitcast.21), kind=kLoop, calls=%fused_computation.1 | loop fusion | flops 1048576 | bytes 5242884 | tf_op jit(solution)/shard_map/add | solution.py:260
  42.8 0.2 collective-permute-done.2
  43.0 0.0 collective-permute-start.3
  43.0 0.0 copy-done.2
  43.0 1.5 %dynamic-slice_add_fusion.combined_ref.other_combined_ref = f32[2,2048,128]{2,1,0:T(8,128)S(1)} fusion(f32[2,4096,128]{2,1,0:T(8,128)S(1)} %bitcast.18, s32[]{:T(128)S(6)} %select_n.9, bf16[2,4096,128]{2,1,0:T(8,128)(2,1)} %bitcast.22), kind=kLoop, calls=%fused_computation | loop fusion | flops 1048576 | bytes 5242884 | tf_op jit(solution)/shard_map/add | solution.py:260
  44.5 2.8 %collective-permute-done.3 = f32[128,128]{1,0:T(8,128)S(1)} collective-permute-done((f32[128,128]{1,0:T(8,128)S(1)}, f32[128,128]{1,0:T(8,128)S(1)}, u32[]{:S(2)}, u32[]{:S(2)}) %collective-permute-start.3) | collective-permute-done | bytes 65568 | tf_op jit(solution)/shard_map/ppermute | solution.py:279
  47.2 3.2 %collective-permute-start.4 = (f32[128,128]{1,0:T(8,128)S(1)}, f32[128,128]{1,0:T(8,128)S(1)}, u32[]{:S(2)}, u32[]{:S(2)}) collective-permute-start(f32[128,128]{1,0:T(8,128)S(1)} %collective-permute-done.3), channel_id=1, source_target_pairs={{0,7},{1,2},{2,1},{3,4},{4,3},{5,6},{6,5},{7,0},{8,15},{9,10},{10,... | collective-permute-start | bytes 196616 | tf_op jit(solution)/shard_map/ppermute | solution.py:281
  50.5 2.2 %collective-permute-done.4 = f32[128,128]{1,0:T(8,128)S(1)} collective-permute-done((f32[128,128]{1,0:T(8,128)S(1)}, f32[128,128]{1,0:T(8,128)S(1)}, u32[]{:S(2)}, u32[]{:S(2)}) %collective-permute-start.4) | collective-permute-done | bytes 65568 | tf_op jit(solution)/shard_map/ppermute | solution.py:281
  52.7 0.1 tile.2
  52.8 16.3 %all_to_all.18 = f32[16,128,128]{2,1,0:T(8,128)S(1)} all-to-all(f32[16,128,128]{2,1,0:T(8,128)S(1)} %tile.2), channel_id=1, replica_groups=mesh['x'=4,'y'=4,'c'=2,'z'=8] {'x','y'}, dimensions={0} | all-to-all | bytes 2097152 | tf_op jit(solution)/shard_map/all_to_all | solution.py:244
  69.1 0.0 collective-permute-start.5
  69.1 1.8 %right_own.1 = (f32[256,256]{1,0:T(8,128)S(1)}, f32[256,256]{1,0:T(8,128)S(1)}, f32[128,128]{1,0:T(8,128)S(1)}) custom-call(f32[2,2048,128]{2,1,0:T(8,128)S(1)} %dynamic-slice_add_fusion.1.combined_ref.own_combined_ref, f32[2048,128]{1,0:T(8,128)S(1)} %bitcast.11), custom_call_target="tpu_custom_call" | custom-call | flops 939524096 | bytes 3145728 | tf_op jit(solution)/shard_map/right_own/pallas_call | solution.py:131
  71.0 0.8 collective-permute-done.5.factor_ref.other_ref
  71.8 2.0 %right_other.1 = (f32[64,128]{1,0:T(8,128)S(1)}, f32[64,64]{1,0:T(8,128)S(1)}) custom-call(f32[2,2048,128]{2,1,0:T(8,128)S(1)} %dynamic-slice_add_fusion.combined_ref.other_combined_ref, f32[2048,128]{1,0:T(8,128)S(1)} %collective-permute-done.5.factor_ref.other_ref, f32[256,256]{1,0:T(8,128)S(1)} %get-tuple-element.31.acc_in, ...), custom_call_target="tpu_custom_call" | custom-call | flops 939524096 | bytes 3145728 | tf_op jit(solution)/shard_map/right_other/pallas_call | solution.py:143
  73.8 0.2 collective-permute-start.6
  74.0 1.1 %collective-permute-done.6 = f32[64,128]{1,0:T(8,128)S(1)} collective-permute-done((f32[64,128]{1,0:T(8,128)S(1)}, f32[64,128]{1,0:T(8,128)S(1)}, u32[]{:S(2)}, u32[]{:S(2)}) %collective-permute-start.6) | collective-permute-done | bytes 32800 | tf_op jit(solution)/shard_map/ppermute | solution.py:236
  75.1 0.6 collective-permute-start.7
  75.6 3.4 %collective-permute-done.7 = f32[64,128]{1,0:T(8,128)S(1)} collective-permute-done((f32[64,128]{1,0:T(8,128)S(1)}, f32[64,128]{1,0:T(8,128)S(1)}, u32[]{:S(2)}, u32[]{:S(2)}) %collective-permute-start.7) | collective-permute-done | bytes 32800 | tf_op jit(solution)/shard_map/ppermute | solution.py:251
  79.0 0.6 collective-permute-start.8
  79.6 1.8 %inverse.1.inverse_ref = f32[64,64]{1,0:T(8,128)S(1)} custom-call(f32[64,64]{1,0:T(8,128)S(1)} %get-tuple-element.35.gram_ref), custom_call_target="tpu_custom_call" | custom-call | flops 262144 | bytes 32768 | tf_op jit(solution)/shard_map/inverse/pallas_call | solution.py:172
  81.4 2.7 %collective-permute-done.8 = f32[64,128]{1,0:T(8,128)S(1)} collective-permute-done((f32[64,128]{1,0:T(8,128)S(1)}, f32[64,128]{1,0:T(8,128)S(1)}, u32[]{:S(2)}, u32[]{:S(2)}) %collective-permute-start.8) | collective-permute-done | bytes 32800 | tf_op jit(solution)/shard_map/ppermute | solution.py:251
  84.1 0.5 collective-permute-start.9
  84.6 3.4 %collective-permute-done.9 = f32[64,128]{1,0:T(8,128)S(1)} collective-permute-done((f32[64,128]{1,0:T(8,128)S(1)}, f32[64,128]{1,0:T(8,128)S(1)}, u32[]{:S(2)}, u32[]{:S(2)}) %collective-permute-start.9) | collective-permute-done | bytes 32800 | tf_op jit(solution)/shard_map/ppermute | solution.py:251
  88.0 2.1 %collective-permute-start.10 = (f32[64,128]{1,0:T(8,128)S(1)}, f32[64,128]{1,0:T(8,128)S(1)}, u32[]{:S(2)}, u32[]{:S(2)}) collective-permute-start(f32[64,128]{1,0:T(8,128)S(1)} %add.56), channel_id=1, source_target_pairs={{64,128},{128,64},{192,0},{0,192},{65,129},{129,65},{193,1},{1,193... | collective-permute-start | bytes 98312 | tf_op jit(solution)/shard_map/ppermute | solution.py:251
  90.2 3.0 %collective-permute-done.10 = f32[64,128]{1,0:T(8,128)S(1)} collective-permute-done((f32[64,128]{1,0:T(8,128)S(1)}, f32[64,128]{1,0:T(8,128)S(1)}, u32[]{:S(2)}, u32[]{:S(2)}) %collective-permute-start.10) | collective-permute-done | bytes 32800 | tf_op jit(solution)/shard_map/ppermute | solution.py:251
  93.2 4.2 %final.1 = (bf16[2,4096,128]{2,1,0:T(8,128)(2,1)}, f32[2,4096,128]{2,1,0:T(8,128)}, f32[64,128]{1,0:T(8,128)}) custom-call(s32[1]{0:T(128)} %bitcast.half_ref, f32[2,2048,128]{2,1,0:T(8,128)S(1)} %dynamic-slice_add_fusion.1.combined_ref.own_combined_ref, f32[2,2048,128]{2,1,0:T(8,128)S(1)} %dynamic-slice_add_fusion.combined_ref.other_combined_ref, ...), custom_call_target="tpu_custom_call" | custom-call | flops 1073741824 | bytes 6291456 | tf_op jit(solution)/shard_map/final/pallas_call | solution.py:214
  (7 shorter events, 0.1 us)
Async XLA Ops:
  0.6 0.8 copy-start
  1.4 3.0 %copy-start.1 = (f32[128,64]{0,1:T(8,128)S(1)}, f32[128,64]{0,1:T(8,128)}, u32[]{:S(2)}) copy-start(f32[128,64]{0,1:T(8,128)} %param.5) | copy-start | bytes 98308
  4.3 3.1 %collective-permute-start = (f32[2048,128]{1,0:T(8,128)S(1)}, f32[2048,128]{1,0:T(8,128)S(1)}, u32[]{:S(2)}, u32[]{:S(2)}) collective-permute-start(f32[2048,128]{1,0:T(8,128)S(1)} %left.3), channel_id=1, source_target_pairs={{0,8},{8,0},{1,9},{9,1},{2,10},{10,2},{3,11},{11,3},{4,12},{12,4},... | collective-permute-start | bytes 3145736 | tf_op jit(solution)/shard_map/ppermute | solution.py:236
  30.4 4.4 %collective-permute-start.1 = (f32[128,128]{1,0:T(8,128)S(1)}, f32[128,128]{1,0:T(8,128)S(1)}, u32[]{:S(2)}, u32[]{:S(2)}) collective-permute-start(f32[128,128]{1,0:T(8,128)S(1)} %reduce_sum.9), channel_id=1, source_target_pairs={{0,1},{1,0},{2,3},{3,2},{4,5},{5,4},{6,7},{7,6},{8,9},{9,8},{10,11... | collective-permute-start | bytes 196616 | tf_op jit(solution)/shard_map/ppermute | solution.py:275
  34.8 8.2 %copy-start.2 = (f32[1,8192,128]{2,1,0:T(8,128)S(1)}, f32[1,8192,128]{2,1,0:T(8,128)}, u32[]{:S(2)}) copy-start(f32[1,8192,128]{2,1,0:T(8,128)} %param.4) | copy-start | bytes 12582916
  34.8 8.2 %collective-permute-start.2 = (f32[128,128]{1,0:T(8,128)S(1)}, f32[128,128]{1,0:T(8,128)S(1)}, u32[]{:S(2)}, u32[]{:S(2)}) collective-permute-start(f32[128,128]{1,0:T(8,128)S(1)} %add.45), channel_id=1, source_target_pairs={{0,7},{1,2},{2,1},{3,4},{4,3},{5,6},{6,5},{7,0},{8,15},{9,10},{10,... | collective-permute-start | bytes 196616 | tf_op jit(solution)/shard_map/ppermute | solution.py:277
  43.0 4.3 %collective-permute-start.3 = (f32[128,128]{1,0:T(8,128)S(1)}, f32[128,128]{1,0:T(8,128)S(1)}, u32[]{:S(2)}, u32[]{:S(2)}) collective-permute-start(f32[128,128]{1,0:T(8,128)S(1)} %collective-permute-done.2), channel_id=1, source_target_pairs={{0,1},{1,0},{2,3},{3,2},{4,5},{5,4},{6,7},{7,6},{8,9},{9,8},{10,11... | collective-permute-start | bytes 196616 | tf_op jit(solution)/shard_map/ppermute | solution.py:279
  47.2 5.5 %collective-permute-start.4 = (f32[128,128]{1,0:T(8,128)S(1)}, f32[128,128]{1,0:T(8,128)S(1)}, u32[]{:S(2)}, u32[]{:S(2)}) collective-permute-start(f32[128,128]{1,0:T(8,128)S(1)} %collective-permute-done.3), channel_id=1, source_target_pairs={{0,7},{1,2},{2,1},{3,4},{4,3},{5,6},{6,5},{7,0},{8,15},{9,10},{10,... | collective-permute-start | bytes 196616 | tf_op jit(solution)/shard_map/ppermute | solution.py:281
  69.1 2.7 %collective-permute-start.5 = (f32[2048,128]{1,0:T(8,128)S(1)}, f32[2048,128]{1,0:T(8,128)S(1)}, u32[]{:S(2)}, u32[]{:S(2)}) collective-permute-start(f32[2048,128]{1,0:T(8,128)S(1)} %bitcast.10), channel_id=1, source_target_pairs={{0,8},{8,0},{1,9},{9,1},{2,10},{10,2},{3,11},{11,3},{4,12},{12,4},... | collective-permute-start | bytes 3145736 | tf_op jit(solution)/shard_map/ppermute | solution.py:236
  73.8 1.3 %collective-permute-start.6 = (f32[64,128]{1,0:T(8,128)S(1)}, f32[64,128]{1,0:T(8,128)S(1)}, u32[]{:S(2)}, u32[]{:S(2)}) collective-permute-start(f32[64,128]{1,0:T(8,128)S(1)} %get-tuple-element.34), channel_id=1, source_target_pairs={{0,8},{8,0},{1,9},{9,1},{2,10},{10,2},{3,11},{11,3},{4,12},{12,4},... | collective-permute-start | bytes 98312 | tf_op jit(solution)/shard_map/ppermute | solution.py:236
  75.1 3.9 %collective-permute-start.7 = (f32[64,128]{1,0:T(8,128)S(1)}, f32[64,128]{1,0:T(8,128)S(1)}, u32[]{:S(2)}, u32[]{:S(2)}) collective-permute-start(f32[64,128]{1,0:T(8,128)S(1)} %add.53), channel_id=1, source_target_pairs={{0,16},{16,0},{32,48},{48,32},{1,17},{17,1},{33,49},{49,33},{2,18}... | collective-permute-start | bytes 98312 | tf_op jit(solution)/shard_map/ppermute | solution.py:251
  79.0 5.1 %collective-permute-start.8 = (f32[64,128]{1,0:T(8,128)S(1)}, f32[64,128]{1,0:T(8,128)S(1)}, u32[]{:S(2)}, u32[]{:S(2)}) collective-permute-start(f32[64,128]{1,0:T(8,128)S(1)} %add.54), channel_id=1, source_target_pairs={{16,32},{32,16},{48,0},{0,48},{17,33},{33,17},{49,1},{1,49},{18,34... | collective-permute-start | bytes 98312 | tf_op jit(solution)/shard_map/ppermute | solution.py:251
  84.1 3.9 %collective-permute-start.9 = (f32[64,128]{1,0:T(8,128)S(1)}, f32[64,128]{1,0:T(8,128)S(1)}, u32[]{:S(2)}, u32[]{:S(2)}) collective-permute-start(f32[64,128]{1,0:T(8,128)S(1)} %add.55), channel_id=1, source_target_pairs={{0,64},{64,0},{128,192},{192,128},{1,65},{65,1},{129,193},{193,129... | collective-permute-start | bytes 98312 | tf_op jit(solution)/shard_map/ppermute | solution.py:251
  88.0 5.1 %collective-permute-start.10 = (f32[64,128]{1,0:T(8,128)S(1)}, f32[64,128]{1,0:T(8,128)S(1)}, u32[]{:S(2)}, u32[]{:S(2)}) collective-permute-start(f32[64,128]{1,0:T(8,128)S(1)} %add.56), channel_id=1, source_target_pairs={{64,128},{128,64},{192,0},{0,192},{65,129},{129,65},{193,1},{1,193... | collective-permute-start | bytes 98312 | tf_op jit(solution)/shard_map/ppermute | solution.py:251

commit v4 on v3

--- a/solution.py
+++ b/solution.py
@@ -14,6 +14,8 @@
 REPLICAS = 32
 PAIR_A = [(0, 1), (1, 0), (2, 3), (3, 2)]
 PAIR_B = [(1, 2), (2, 1), (3, 0), (0, 3)]
+LEFT_BLOCK = 1024
+LEFT_STEPS = HALF // LEFT_BLOCK
 RIGHT_BLOCK = 512
 VMEM_LIMIT = 24 * 1024 * 1024
 LEFT_VMEM_LIMIT = 51 * 1024 * 1024
@@ -42,8 +44,8 @@
     warm_copy = pltpu.make_async_copy(warm_ref, warm_buf, warm_sem)
     warm_copy.start()
     copies = []
-    for k in range(STEPS):
-        source, rows = pl.ds(start + k * BLOCK, BLOCK), pl.ds(k * BLOCK, BLOCK)
+    for k in range(LEFT_STEPS):
+        source, rows = pl.ds(start + k * LEFT_BLOCK, LEFT_BLOCK), pl.ds(k * LEFT_BLOCK, LEFT_BLOCK)
         pair = (
             pltpu.make_async_copy(grad_ref.at[:, source, :], grad_buf.at[:, rows, :], grad_sems.at[k]),
             pltpu.make_async_copy(error_ref.at[:, source, :], error_buf.at[:, rows, :], error_sems.at[k]),
@@ -58,10 +60,10 @@
     bottom_right = jnp.concatenate([none, high, none, low], axis=1)
     top_right = jnp.concatenate([top_right, top_right], axis=0)
     bottom_right = jnp.concatenate([bottom_right, bottom_right], axis=0)
-    for k in range(STEPS):
+    for k in range(LEFT_STEPS):
         for copy in copies[k]:
             copy.wait()
-        rows = pl.ds(k * BLOCK, BLOCK)
+        rows = pl.ds(k * LEFT_BLOCK, LEFT_BLOCK)
         combined = grad_buf[:, rows, :].astype(jnp.float32) + error_buf[:, rows, :]
         top = jnp.concatenate(split2(combined[0]), axis=1)
         bottom = jnp.concatenate(split2(combined[1]), axis=1)
@@ -85,8 +87,8 @@
             pltpu.VMEM((2, HALF, COLS), jnp.bfloat16),
             pltpu.VMEM((2, HALF, COLS), jnp.float32),
             pltpu.SemaphoreType.DMA,
-            pltpu.SemaphoreType.DMA((STEPS,)),
-            pltpu.SemaphoreType.DMA((STEPS,)),
+            pltpu.SemaphoreType.DMA((LEFT_STEPS,)),
+            pltpu.SemaphoreType.DMA((LEFT_STEPS,)),
         ],
         compiler_params=pltpu.CompilerParams(vmem_limit_bytes=LEFT_VMEM_LIMIT),
         cost_estimate=pl.CostEstimate(flops=2 * 2 * HALF * 256 * 256, bytes_accessed=2 * HALF * COLS * 6, transcendentals=0),
@@ -248,7 +250,7 @@
     a = a + swap(a)
     for axis in ("y", "x"):
         for pairs in (PAIR_A, PAIR_B):
-            a = a + lax.ppermute(a, axis, pairs)
+            a = a + lax.ppermute(a, (axis, "c"), [(2 * i + c, 2 * j + 1 - c) for i, j in pairs for c in range(2)])
         if axis == "y":
             a, inverse = lax.optimization_barrier((a, inverse_lower(gram)))
     return a, inverse

time: 97.7 us -> 98 us (level)
  the two profiles are of different devices: /device:TPU:6 before, /device:TPU:1 now
where the time goes in v4:
time: 98 us; the launch traced here: 97.8 us
  blocking collectives  36.5 us (37%)
  starting transfers between devices  21.2 us (22%)
  waiting for transfers between devices  19.2 us (20%)
  Pallas kernels  15.5 us (16%)
  other arithmetic  3.79 us (4%)
    all_to_all x1, blocking collectives, scatter_sum(): lax.all_to_all(a, axes, 0, 0, tiled=True).reshape(count, -1, 128).sum(0)  20.6 us
    all_to_all x1, blocking collectives, gather(): return lax.all_to_all(jnp.tile(a, (count, 1)), axes, 0, 0, tiled=True)  16 us
    ppermute x4, waiting for transfers between devices, sum_over_replicas(): lax.ppermute(a, (axis, 'c'), [(2 * i + c, 2 * j + 1 - c) for i, j in pair...  11.9 us
    ppermute x3, starting transfers between devices, swap(): return lax.ppermute(a, 'c', [(0, 1), (1, 0)])  9.87 us
    pallas_call x2, Pallas kernels, left_half(): pl.pallas_call(left_kernel, out_shape=jax.ShapeDtypeStruct((HALF, 128), j...  5.67 us
    ppermute x1, starting transfers between devices, shards(): near = lax.ppermute(pair, 'z', RING_B)  5.48 us
    pallas_call x1, Pallas kernels, final(): pl.pallas_call(final_kernel, out_shape=(jax.ShapeDtypeStruct((2, ROWS //...  4.21 us
    add x2, other arithmetic, combined_half(): lax.dynamic_slice(grad, (0, start, 0), part).astype(jnp.float32)  3.53 us
  transfers between devices with their start and end apart: 11, of which 9 were waited for; matrix products, arithmetic and copies ran while one was open for 4% of the time, Pallas kernels for 7%

profile of v4, /device:TPU:1, one launch (start us, length us, event | category | flops | bytes accessed | tf_op | source)
XLA Modules:
  0.0 97.8 jit_solution(389690874761612857)
XLA Ops:
  0.6 0.0 copy-start
  0.6 0.7 copy-done
  1.4 0.0 copy-start.1
  1.4 2.8 %left.3 = f32[2048,128]{1,0:T(8,128)S(1)} custom-call(s32[1]{0:T(128)S(6)} %sub.4.half_ref, bf16[2,4096,128]{2,1,0:T(8,128)(2,1)} %bitcast.19, f32[2,4096,128]{2,1,0:T(8,128)} %bitcast.15, f32[64,128]{1,0:T(8,128)S(1)} %bitcast.13), custom_call_target="tpu_custom_call" | custom-call | flops 536870912 | bytes 3145728 | tf_op jit(solution)/shard_map/left/pallas_call | solution.py:80
  4.2 3.3 %collective-permute-start = (f32[2048,128]{1,0:T(8,128)S(1)}, f32[2048,128]{1,0:T(8,128)S(1)}, u32[]{:S(2)}, u32[]{:S(2)}) collective-permute-start(f32[2048,128]{1,0:T(8,128)S(1)} %left.3), channel_id=1, source_target_pairs={{0,8},{8,0},{1,9},{9,1},{2,10},{10,2},{3,11},{11,3},{4,12},{12,4},... | collective-permute-start | bytes 3145736 | tf_op jit(solution)/shard_map/ppermute | solution.py:238
  7.6 0.0 copy-done.1
  7.6 2.8 %left.2 = f32[2048,128]{1,0:T(8,128)S(1)} custom-call(s32[1]{0:T(128)} %bitcast.half_ref, bf16[2,4096,128]{2,1,0:T(8,128)(2,1)} %bitcast.20, f32[2,4096,128]{2,1,0:T(8,128)} %bitcast.16, f32[64,128]{1,0:T(8,128)S(1)} %bitcast.14), custom_call_target="tpu_custom_call" | custom-call | flops 536870912 | bytes 3145728 | tf_op jit(solution)/shard_map/left/pallas_call | solution.py:80
  10.4 0.0 collective-permute-done
  10.4 0.2 add.44
  10.6 20.6 %all_to_all.17 = f32[16,128,128]{2,1,0:T(8,128)S(1)} all-to-all(f32[16,128,128]{2,1,0:T(8,128)S(1)} %bitcast.23), channel_id=1, replica_groups=mesh['x'=4,'y'=4,'c'=2,'z'=8] {'x','y'}, dimensions={0} | all-to-all | bytes 2097152 | tf_op jit(solution)/shard_map/all_to_all | solution.py:242
  31.2 0.1 reduce_sum.9
  31.2 1.7 %collective-permute-start.1 = (f32[128,128]{1,0:T(8,128)S(1)}, f32[128,128]{1,0:T(8,128)S(1)}, u32[]{:S(2)}, u32[]{:S(2)}) collective-permute-start(f32[128,128]{1,0:T(8,128)S(1)} %reduce_sum.9), channel_id=1, source_target_pairs={{0,1},{1,0},{2,3},{3,2},{4,5},{5,4},{6,7},{7,6},{8,9},{9,8},{10,11... | collective-permute-start | bytes 196616 | tf_op jit(solution)/shard_map/ppermute | solution.py:277
  32.9 1.7 %collective-permute-done.1 = f32[128,128]{1,0:T(8,128)S(1)} collective-permute-done((f32[128,128]{1,0:T(8,128)S(1)}, f32[128,128]{1,0:T(8,128)S(1)}, u32[]{:S(2)}, u32[]{:S(2)}) %collective-permute-start.1) | collective-permute-done | bytes 65568 | tf_op jit(solution)/shard_map/ppermute | solution.py:277
  34.6 0.0 copy-start.2
  34.6 5.5 %collective-permute-start.2 = (f32[128,128]{1,0:T(8,128)S(1)}, f32[128,128]{1,0:T(8,128)S(1)}, u32[]{:S(2)}, u32[]{:S(2)}) collective-permute-start(f32[128,128]{1,0:T(8,128)S(1)} %add.45), channel_id=1, source_target_pairs={{0,7},{1,2},{2,1},{3,4},{4,3},{5,6},{6,5},{7,0},{8,15},{9,10},{10,... | collective-permute-start | bytes 196616 | tf_op jit(solution)/shard_map/ppermute | solution.py:279
  40.1 2.0 %dynamic-slice_add_fusion.1.combined_ref.own_combined_ref = f32[2,2048,128]{2,1,0:T(8,128)S(1)} fusion(f32[2,4096,128]{2,1,0:T(8,128)} %bitcast.17, s32[]{:T(128)S(6)} %select_n.8, bf16[2,4096,128]{2,1,0:T(8,128)(2,1)} %bitcast.21), kind=kLoop, calls=%fused_computation.1 | loop fusion | flops 1048576 | bytes 5242884 | tf_op jit(solution)/shard_map/add | solution.py:262
  42.1 0.0 collective-permute-done.2
  42.1 0.1 collective-permute-start.3
  42.2 0.0 copy-done.2
  42.3 1.5 %dynamic-slice_add_fusion.combined_ref.other_combined_ref = f32[2,2048,128]{2,1,0:T(8,128)S(1)} fusion(f32[2,4096,128]{2,1,0:T(8,128)S(1)} %bitcast.18, s32[]{:T(128)S(6)} %select_n.9, bf16[2,4096,128]{2,1,0:T(8,128)(2,1)} %bitcast.22), kind=kLoop, calls=%fused_computation | loop fusion | flops 1048576 | bytes 5242884 | tf_op jit(solution)/shard_map/add | solution.py:262
  43.8 1.9 %collective-permute-done.3 = f32[128,128]{1,0:T(8,128)S(1)} collective-permute-done((f32[128,128]{1,0:T(8,128)S(1)}, f32[128,128]{1,0:T(8,128)S(1)}, u32[]{:S(2)}, u32[]{:S(2)}) %collective-permute-start.3) | collective-permute-done | bytes 65568 | tf_op jit(solution)/shard_map/ppermute | solution.py:281
  45.6 1.9 %collective-permute-start.4 = (f32[128,128]{1,0:T(8,128)S(1)}, f32[128,128]{1,0:T(8,128)S(1)}, u32[]{:S(2)}, u32[]{:S(2)}) collective-permute-start(f32[128,128]{1,0:T(8,128)S(1)} %collective-permute-done.3), channel_id=1, source_target_pairs={{0,7},{1,2},{2,1},{3,4},{4,3},{5,6},{6,5},{7,0},{8,15},{9,10},{10,... | collective-permute-start | bytes 196616 | tf_op jit(solution)/shard_map/ppermute | solution.py:283
  47.5 2.4 %collective-permute-done.4 = f32[128,128]{1,0:T(8,128)S(1)} collective-permute-done((f32[128,128]{1,0:T(8,128)S(1)}, f32[128,128]{1,0:T(8,128)S(1)}, u32[]{:S(2)}, u32[]{:S(2)}) %collective-permute-start.4) | collective-permute-done | bytes 65568 | tf_op jit(solution)/shard_map/ppermute | solution.py:283
  50.0 0.1 tile.2
  50.1 16.0 %all_to_all.18 = f32[16,128,128]{2,1,0:T(8,128)S(1)} all-to-all(f32[16,128,128]{2,1,0:T(8,128)S(1)} %tile.2), channel_id=1, replica_groups=mesh['x'=4,'y'=4,'c'=2,'z'=8] {'x','y'}, dimensions={0} | all-to-all | bytes 2097152 | tf_op jit(solution)/shard_map/all_to_all | solution.py:246
  66.0 6.1 %collective-permute-start.5 = (f32[2048,128]{1,0:T(8,128)S(1)}, f32[2048,128]{1,0:T(8,128)S(1)}, u32[]{:S(2)}, u32[]{:S(2)}) collective-permute-start(f32[2048,128]{1,0:T(8,128)S(1)} %bitcast.10), channel_id=1, source_target_pairs={{0,8},{8,0},{1,9},{9,1},{2,10},{10,2},{3,11},{11,3},{4,12},{12,4},... | collective-permute-start | bytes 3145736 | tf_op jit(solution)/shard_map/ppermute | solution.py:238
  72.1 1.8 %right_own.1 = (f32[256,256]{1,0:T(8,128)S(1)}, f32[256,256]{1,0:T(8,128)S(1)}, f32[128,128]{1,0:T(8,128)S(1)}) custom-call(f32[2,2048,128]{2,1,0:T(8,128)S(1)} %dynamic-slice_add_fusion.1.combined_ref.own_combined_ref, f32[2048,128]{1,0:T(8,128)S(1)} %bitcast.11), custom_call_target="tpu_custom_call" | custom-call | flops 939524096 | bytes 3145728 | tf_op jit(solution)/shard_map/right_own/pallas_call | solution.py:133
  74.0 0.5 collective-permute-done.5.factor_ref.other_ref
  74.4 2.0 %right_other.1 = (f32[64,128]{1,0:T(8,128)S(1)}, f32[64,64]{1,0:T(8,128)S(1)}) custom-call(f32[2,2048,128]{2,1,0:T(8,128)S(1)} %dynamic-slice_add_fusion.combined_ref.other_combined_ref, f32[2048,128]{1,0:T(8,128)S(1)} %collective-permute-done.5.factor_ref.other_ref, f32[256,256]{1,0:T(8,128)S(1)} %get-tuple-element.31.acc_in, ...), custom_call_target="tpu_custom_call" | custom-call | flops 939524096 | bytes 3145728 | tf_op jit(solution)/shard_map/right_other/pallas_call | solution.py:145
  76.4 0.5 collective-permute-start.6
  76.9 0.9 collective-permute-done.6
  77.7 0.5 collective-permute-start.7
  78.2 2.8 %collective-permute-done.7 = f32[64,128]{1,0:T(8,128)S(1)} collective-permute-done((f32[64,128]{1,0:T(8,128)S(1)}, f32[64,128]{1,0:T(8,128)S(1)}, u32[]{:S(2)}, u32[]{:S(2)}) %collective-permute-start.7) | collective-permute-done | bytes 32800 | tf_op jit(solution)/shard_map/ppermute | solution.py:253
  81.1 0.5 collective-permute-start.8
  81.6 1.8 %inverse.1.inverse_ref = f32[64,64]{1,0:T(8,128)S(1)} custom-call(f32[64,64]{1,0:T(8,128)S(1)} %get-tuple-element.35.gram_ref), custom_call_target="tpu_custom_call" | custom-call | flops 262144 | bytes 32768 | tf_op jit(solution)/shard_map/inverse/pallas_call | solution.py:174
  83.4 2.2 %collective-permute-done.8 = f32[64,128]{1,0:T(8,128)S(1)} collective-permute-done((f32[64,128]{1,0:T(8,128)S(1)}, f32[64,128]{1,0:T(8,128)S(1)}, u32[]{:S(2)}, u32[]{:S(2)}) %collective-permute-start.8) | collective-permute-done | bytes 32800 | tf_op jit(solution)/shard_map/ppermute | solution.py:253
  85.6 0.0 collective-permute-start.9
  85.7 3.3 %collective-permute-done.9 = f32[64,128]{1,0:T(8,128)S(1)} collective-permute-done((f32[64,128]{1,0:T(8,128)S(1)}, f32[64,128]{1,0:T(8,128)S(1)}, u32[]{:S(2)}, u32[]{:S(2)}) %collective-permute-start.9) | collective-permute-done | bytes 32800 | tf_op jit(solution)/shard_map/ppermute | solution.py:253
  89.0 1.1 %collective-permute-start.10 = (f32[64,128]{1,0:T(8,128)S(1)}, f32[64,128]{1,0:T(8,128)S(1)}, u32[]{:S(2)}, u32[]{:S(2)}) collective-permute-start(f32[64,128]{1,0:T(8,128)S(1)} %add.56), channel_id=1, source_target_pairs={{64,136},{72,128},{128,72},{136,64},{192,8},{200,0},{0,200},{8,192... | collective-permute-start | bytes 98312 | tf_op jit(solution)/shard_map/ppermute | solution.py:253
  90.0 3.5 %collective-permute-done.10 = f32[64,128]{1,0:T(8,128)S(1)} collective-permute-done((f32[64,128]{1,0:T(8,128)S(1)}, f32[64,128]{1,0:T(8,128)S(1)}, u32[]{:S(2)}, u32[]{:S(2)}) %collective-permute-start.10) | collective-permute-done | bytes 32800 | tf_op jit(solution)/shard_map/ppermute | solution.py:253
  93.5 4.2 %final.1 = (bf16[2,4096,128]{2,1,0:T(8,128)(2,1)}, f32[2,4096,128]{2,1,0:T(8,128)}, f32[64,128]{1,0:T(8,128)}) custom-call(s32[1]{0:T(128)} %bitcast.half_ref, f32[2,2048,128]{2,1,0:T(8,128)S(1)} %dynamic-slice_add_fusion.1.combined_ref.own_combined_ref, f32[2,2048,128]{2,1,0:T(8,128)S(1)} %dynamic-slice_add_fusion.combined_ref.other_combined_ref, ...), custom_call_target="tpu_custom_call" | custom-call | flops 1073741824 | bytes 6291456 | tf_op jit(solution)/shard_map/final/pallas_call | solution.py:216
  (7 shorter events, 0.1 us)
Async XLA Ops:
  0.6 0.8 copy-start
  1.4 6.2 %copy-start.1 = (f32[128,64]{0,1:T(8,128)S(1)}, f32[128,64]{0,1:T(8,128)}, u32[]{:S(2)}) copy-start(f32[128,64]{0,1:T(8,128)} %param.5) | copy-start | bytes 98308
  4.2 6.2 %collective-permute-start = (f32[2048,128]{1,0:T(8,128)S(1)}, f32[2048,128]{1,0:T(8,128)S(1)}, u32[]{:S(2)}, u32[]{:S(2)}) collective-permute-start(f32[2048,128]{1,0:T(8,128)S(1)} %left.3), channel_id=1, source_target_pairs={{0,8},{8,0},{1,9},{9,1},{2,10},{10,2},{3,11},{11,3},{4,12},{12,4},... | collective-permute-start | bytes 3145736 | tf_op jit(solution)/shard_map/ppermute | solution.py:238
  31.2 3.4 %collective-permute-start.1 = (f32[128,128]{1,0:T(8,128)S(1)}, f32[128,128]{1,0:T(8,128)S(1)}, u32[]{:S(2)}, u32[]{:S(2)}) collective-permute-start(f32[128,128]{1,0:T(8,128)S(1)} %reduce_sum.9), channel_id=1, source_target_pairs={{0,1},{1,0},{2,3},{3,2},{4,5},{5,4},{6,7},{7,6},{8,9},{9,8},{10,11... | collective-permute-start | bytes 196616 | tf_op jit(solution)/shard_map/ppermute | solution.py:277
  34.6 7.6 %copy-start.2 = (f32[1,8192,128]{2,1,0:T(8,128)S(1)}, f32[1,8192,128]{2,1,0:T(8,128)}, u32[]{:S(2)}) copy-start(f32[1,8192,128]{2,1,0:T(8,128)} %param.4) | copy-start | bytes 12582916
  34.6 7.5 %collective-permute-start.2 = (f32[128,128]{1,0:T(8,128)S(1)}, f32[128,128]{1,0:T(8,128)S(1)}, u32[]{:S(2)}, u32[]{:S(2)}) collective-permute-start(f32[128,128]{1,0:T(8,128)S(1)} %add.45), channel_id=1, source_target_pairs={{0,7},{1,2},{2,1},{3,4},{4,3},{5,6},{6,5},{7,0},{8,15},{9,10},{10,... | collective-permute-start | bytes 196616 | tf_op jit(solution)/shard_map/ppermute | solution.py:279
  42.1 3.5 %collective-permute-start.3 = (f32[128,128]{1,0:T(8,128)S(1)}, f32[128,128]{1,0:T(8,128)S(1)}, u32[]{:S(2)}, u32[]{:S(2)}) collective-permute-start(f32[128,128]{1,0:T(8,128)S(1)} %collective-permute-done.2), channel_id=1, source_target_pairs={{0,1},{1,0},{2,3},{3,2},{4,5},{5,4},{6,7},{7,6},{8,9},{9,8},{10,11... | collective-permute-start | bytes 196616 | tf_op jit(solution)/shard_map/ppermute | solution.py:281
  45.6 4.3 %collective-permute-start.4 = (f32[128,128]{1,0:T(8,128)S(1)}, f32[128,128]{1,0:T(8,128)S(1)}, u32[]{:S(2)}, u32[]{:S(2)}) collective-permute-start(f32[128,128]{1,0:T(8,128)S(1)} %collective-permute-done.3), channel_id=1, source_target_pairs={{0,7},{1,2},{2,1},{3,4},{4,3},{5,6},{6,5},{7,0},{8,15},{9,10},{10,... | collective-permute-start | bytes 196616 | tf_op jit(solution)/shard_map/ppermute | solution.py:283
  66.0 8.4 %collective-permute-start.5 = (f32[2048,128]{1,0:T(8,128)S(1)}, f32[2048,128]{1,0:T(8,128)S(1)}, u32[]{:S(2)}, u32[]{:S(2)}) collective-permute-start(f32[2048,128]{1,0:T(8,128)S(1)} %bitcast.10), channel_id=1, source_target_pairs={{0,8},{8,0},{1,9},{9,1},{2,10},{10,2},{3,11},{11,3},{4,12},{12,4},... | collective-permute-start | bytes 3145736 | tf_op jit(solution)/shard_map/ppermute | solution.py:238
  76.4 1.3 %collective-permute-start.6 = (f32[64,128]{1,0:T(8,128)S(1)}, f32[64,128]{1,0:T(8,128)S(1)}, u32[]{:S(2)}, u32[]{:S(2)}) collective-permute-start(f32[64,128]{1,0:T(8,128)S(1)} %get-tuple-element.34), channel_id=1, source_target_pairs={{0,8},{8,0},{1,9},{9,1},{2,10},{10,2},{3,11},{11,3},{4,12},{12,4},... | collective-permute-start | bytes 98312 | tf_op jit(solution)/shard_map/ppermute | solution.py:238
  77.7 3.3 %collective-permute-start.7 = (f32[64,128]{1,0:T(8,128)S(1)}, f32[64,128]{1,0:T(8,128)S(1)}, u32[]{:S(2)}, u32[]{:S(2)}) collective-permute-start(f32[64,128]{1,0:T(8,128)S(1)} %add.53), channel_id=1, source_target_pairs={{0,24},{8,16},{16,8},{24,0},{32,56},{40,48},{48,40},{56,32},{1,25}... | collective-permute-start | bytes 98312 | tf_op jit(solution)/shard_map/ppermute | solution.py:253
  81.1 4.6 %collective-permute-start.8 = (f32[64,128]{1,0:T(8,128)S(1)}, f32[64,128]{1,0:T(8,128)S(1)}, u32[]{:S(2)}, u32[]{:S(2)}) collective-permute-start(f32[64,128]{1,0:T(8,128)S(1)} %add.54), channel_id=1, source_target_pairs={{16,40},{24,32},{32,24},{40,16},{48,8},{56,0},{0,56},{8,48},{17,41... | collective-permute-start | bytes 98312 | tf_op jit(solution)/shard_map/ppermute | solution.py:253
  85.6 3.3 %collective-permute-start.9 = (f32[64,128]{1,0:T(8,128)S(1)}, f32[64,128]{1,0:T(8,128)S(1)}, u32[]{:S(2)}, u32[]{:S(2)}) collective-permute-start(f32[64,128]{1,0:T(8,128)S(1)} %add.55), channel_id=1, source_target_pairs={{0,72},{8,64},{64,8},{72,0},{128,200},{136,192},{192,136},{200,128... | collective-permute-start | bytes 98312 | tf_op jit(solution)/shard_map/ppermute | solution.py:253
  89.0 4.6 %collective-permute-start.10 = (f32[64,128]{1,0:T(8,128)S(1)}, f32[64,128]{1,0:T(8,128)S(1)}, u32[]{:S(2)}, u32[]{:S(2)}) collective-permute-start(f32[64,128]{1,0:T(8,128)S(1)} %add.56), channel_id=1, source_target_pairs={{64,136},{72,128},{128,72},{136,64},{192,8},{200,0},{0,200},{8,192... | collective-permute-start | bytes 98312 | tf_op jit(solution)/shard_map/ppermute | solution.py:253

commit v5 on v4

--- a/solution.py
+++ b/solution.py
@@ -12,8 +12,6 @@
 BLOCK = 512
 STEPS = HALF // BLOCK
 REPLICAS = 32
-PAIR_A = [(0, 1), (1, 0), (2, 3), (3, 2)]
-PAIR_B = [(1, 2), (2, 1), (3, 0), (0, 3)]
 LEFT_BLOCK = 1024
 LEFT_STEPS = HALF // LEFT_BLOCK
 RIGHT_BLOCK = 512
@@ -249,8 +247,8 @@
 def sum_over_replicas(a, gram):
     a = a + swap(a)
     for axis in ("y", "x"):
-        for pairs in (PAIR_A, PAIR_B):
-            a = a + lax.ppermute(a, (axis, "c"), [(2 * i + c, 2 * j + 1 - c) for i, j in pairs for c in range(2)])
+        near, far, back = [lax.ppermute(a, axis, [(i, (i + k) % 4) for i in range(4)]) for k in (1, 2, 3)]
+        a = (a + near) + (far + back)
         if axis == "y":
             a, inverse = lax.optimization_barrier((a, inverse_lower(gram)))
     return a, inverse

time: 98 us -> 95.2 us (0.971)
  the two profiles are of different devices: /device:TPU:1 before, /device:TPU:6 now
where the time goes in v5:
time: 95.2 us; the launch traced here: 94.8 us
  blocking collectives  39.1 us (41%)
  starting transfers between devices  18.2 us (19%)
  waiting for transfers between devices  16.4 us (17%)
  Pallas kernels  15.5 us (16%)
  other arithmetic  3.78 us (4%)
    all_to_all x1, blocking collectives, scatter_sum(): lax.all_to_all(a, axes, 0, 0, tiled=True).reshape(count, -1, 128).sum(0)  22.8 us
    all_to_all x1, blocking collectives, gather(): return lax.all_to_all(jnp.tile(a, (count, 1)), axes, 0, 0, tiled=True)  16.3 us
    ppermute x6, waiting for transfers between devices, sum_over_replicas(): lax.ppermute(a, axis, [(i, (i + k) % 4) for i in range(4)])  6.95 us
    ppermute x6, starting transfers between devices, sum_over_replicas(): lax.ppermute(a, axis, [(i, (i + k) % 4) for i in range(4)])  6.73 us
    ppermute x1, starting transfers between devices, shards(): near = lax.ppermute(pair, 'z', RING_B)  5.94 us
    pallas_call x2, Pallas kernels, left_half(): pl.pallas_call(left_kernel, out_shape=jax.ShapeDtypeStruct((HALF, 128), j...  5.7 us
    pallas_call x1, Pallas kernels, final(): pl.pallas_call(final_kernel, out_shape=(jax.ShapeDtypeStruct((2, ROWS //...  4.21 us
    add x2, other arithmetic, combined_half(): lax.dynamic_slice(grad, (0, start, 0), part).astype(jnp.float32)  3.52 us
  transfers between devices with their start and end apart: 13, of which 11 were waited for; matrix products, arithmetic and copies ran while one was open for 4% of the time, Pallas kernels for 7%

profile of v5, /device:TPU:6, one launch (start us, length us, event | category | flops | bytes accessed | tf_op | source)
XLA Modules:
  0.0 94.8 jit_solution(18317993952543381704)
XLA Ops:
  0.6 0.0 copy-start
  0.6 0.7 copy-done
  1.4 0.0 copy-start.1
  1.4 2.8 %left.3 = f32[2048,128]{1,0:T(8,128)S(1)} custom-call(s32[1]{0:T(128)S(6)} %sub.4.half_ref, bf16[2,4096,128]{2,1,0:T(8,128)(2,1)} %bitcast.19, f32[2,4096,128]{2,1,0:T(8,128)} %bitcast.15, f32[64,128]{1,0:T(8,128)S(1)} %bitcast.13), custom_call_target="tpu_custom_call" | custom-call | flops 536870912 | bytes 3145728 | tf_op jit(solution)/shard_map/left/pallas_call | solution.py:78
  4.2 0.1 collective-permute-start
  4.3 0.0 copy-done.1
  4.3 2.9 %left.2 = f32[2048,128]{1,0:T(8,128)S(1)} custom-call(s32[1]{0:T(128)} %bitcast.half_ref, bf16[2,4096,128]{2,1,0:T(8,128)(2,1)} %bitcast.20, f32[2,4096,128]{2,1,0:T(8,128)} %bitcast.16, f32[64,128]{1,0:T(8,128)S(1)} %bitcast.14), custom_call_target="tpu_custom_call" | custom-call | flops 536870912 | bytes 3145728 | tf_op jit(solution)/shard_map/left/pallas_call | solution.py:78
  7.2 0.0 collective-permute-done
  7.2 0.2 add.50
  7.4 22.8 %all_to_all.17 = f32[16,128,128]{2,1,0:T(8,128)S(1)} all-to-all(f32[16,128,128]{2,1,0:T(8,128)S(1)} %bitcast.23), channel_id=1, replica_groups=mesh['x'=4,'y'=4,'c'=2,'z'=8] {'x','y'}, dimensions={0} | all-to-all | bytes 2097152 | tf_op jit(solution)/shard_map/all_to_all | solution.py:240
  30.2 0.1 reduce_sum.9
  30.3 2.0 %collective-permute-start.1 = (f32[128,128]{1,0:T(8,128)S(1)}, f32[128,128]{1,0:T(8,128)S(1)}, u32[]{:S(2)}, u32[]{:S(2)}) collective-permute-start(f32[128,128]{1,0:T(8,128)S(1)} %reduce_sum.9), channel_id=1, source_target_pairs={{0,1},{1,0},{2,3},{3,2},{4,5},{5,4},{6,7},{7,6},{8,9},{9,8},{10,11... | collective-permute-start | bytes 196616 | tf_op jit(solution)/shard_map/ppermute | solution.py:275
  32.3 2.3 %collective-permute-done.1 = f32[128,128]{1,0:T(8,128)S(1)} collective-permute-done((f32[128,128]{1,0:T(8,128)S(1)}, f32[128,128]{1,0:T(8,128)S(1)}, u32[]{:S(2)}, u32[]{:S(2)}) %collective-permute-start.1) | collective-permute-done | bytes 65568 | tf_op jit(solution)/shard_map/ppermute | solution.py:275
  34.6 0.0 copy-start.2
  34.6 5.9 %collective-permute-start.2 = (f32[128,128]{1,0:T(8,128)S(1)}, f32[128,128]{1,0:T(8,128)S(1)}, u32[]{:S(2)}, u32[]{:S(2)}) collective-permute-start(f32[128,128]{1,0:T(8,128)S(1)} %add.51), channel_id=1, source_target_pairs={{0,7},{1,2},{2,1},{3,4},{4,3},{5,6},{6,5},{7,0},{8,15},{9,10},{10,... | collective-permute-start | bytes 196616 | tf_op jit(solution)/shard_map/ppermute | solution.py:277
  40.6 2.0 %dynamic-slice_add_fusion.1.combined_ref.own_combined_ref = f32[2,2048,128]{2,1,0:T(8,128)S(1)} fusion(f32[2,4096,128]{2,1,0:T(8,128)} %bitcast.17, s32[]{:T(128)S(6)} %select_n.8, bf16[2,4096,128]{2,1,0:T(8,128)(2,1)} %bitcast.21), kind=kLoop, calls=%fused_computation.1 | loop fusion | flops 1048576 | bytes 5242884 | tf_op jit(solution)/shard_map/add | solution.py:260
  42.6 0.2 collective-permute-done.2
  42.8 0.0 collective-permute-start.3
  42.8 0.0 copy-done.2
  42.8 1.5 %dynamic-slice_add_fusion.combined_ref.other_combined_ref = f32[2,2048,128]{2,1,0:T(8,128)S(1)} fusion(f32[2,4096,128]{2,1,0:T(8,128)S(1)} %bitcast.18, s32[]{:T(128)S(6)} %select_n.9, bf16[2,4096,128]{2,1,0:T(8,128)(2,1)} %bitcast.22), kind=kLoop, calls=%fused_computation | loop fusion | flops 1048576 | bytes 5242884 | tf_op jit(solution)/shard_map/add | solution.py:260
  44.3 2.8 %collective-permute-done.3 = f32[128,128]{1,0:T(8,128)S(1)} collective-permute-done((f32[128,128]{1,0:T(8,128)S(1)}, f32[128,128]{1,0:T(8,128)S(1)}, u32[]{:S(2)}, u32[]{:S(2)}) %collective-permute-start.3) | collective-permute-done | bytes 65568 | tf_op jit(solution)/shard_map/ppermute | solution.py:279
  47.1 3.2 %collective-permute-start.4 = (f32[128,128]{1,0:T(8,128)S(1)}, f32[128,128]{1,0:T(8,128)S(1)}, u32[]{:S(2)}, u32[]{:S(2)}) collective-permute-start(f32[128,128]{1,0:T(8,128)S(1)} %collective-permute-done.3), channel_id=1, source_target_pairs={{0,7},{1,2},{2,1},{3,4},{4,3},{5,6},{6,5},{7,0},{8,15},{9,10},{10,... | collective-permute-start | bytes 196616 | tf_op jit(solution)/shard_map/ppermute | solution.py:281
  50.3 2.2 %collective-permute-done.4 = f32[128,128]{1,0:T(8,128)S(1)} collective-permute-done((f32[128,128]{1,0:T(8,128)S(1)}, f32[128,128]{1,0:T(8,128)S(1)}, u32[]{:S(2)}, u32[]{:S(2)}) %collective-permute-start.4) | collective-permute-done | bytes 65568 | tf_op jit(solution)/shard_map/ppermute | solution.py:281
  52.6 0.1 tile.2
  52.7 16.3 %all_to_all.18 = f32[16,128,128]{2,1,0:T(8,128)S(1)} all-to-all(f32[16,128,128]{2,1,0:T(8,128)S(1)} %tile.2), channel_id=1, replica_groups=mesh['x'=4,'y'=4,'c'=2,'z'=8] {'x','y'}, dimensions={0} | all-to-all | bytes 2097152 | tf_op jit(solution)/shard_map/all_to_all | solution.py:244
  69.0 0.0 collective-permute-start.5
  69.0 1.8 %right_own.1 = (f32[256,256]{1,0:T(8,128)S(1)}, f32[256,256]{1,0:T(8,128)S(1)}, f32[128,128]{1,0:T(8,128)S(1)}) custom-call(f32[2,2048,128]{2,1,0:T(8,128)S(1)} %dynamic-slice_add_fusion.1.combined_ref.own_combined_ref, f32[2048,128]{1,0:T(8,128)S(1)} %bitcast.11), custom_call_target="tpu_custom_call" | custom-call | flops 939524096 | bytes 3145728 | tf_op jit(solution)/shard_map/right_own/pallas_call | solution.py:131
  70.8 0.8 collective-permute-done.5.factor_ref.other_ref
  71.6 2.0 %right_other.1 = (f32[64,128]{1,0:T(8,128)S(1)}, f32[64,64]{1,0:T(8,128)S(1)}) custom-call(f32[2,2048,128]{2,1,0:T(8,128)S(1)} %dynamic-slice_add_fusion.combined_ref.other_combined_ref, f32[2048,128]{1,0:T(8,128)S(1)} %collective-permute-done.5.factor_ref.other_ref, f32[256,256]{1,0:T(8,128)S(1)} %get-tuple-element.31.acc_in, ...), custom_call_target="tpu_custom_call" | custom-call | flops 939524096 | bytes 3145728 | tf_op jit(solution)/shard_map/right_other/pallas_call | solution.py:143
  73.6 0.2 collective-permute-start.6
  73.8 1.1 %collective-permute-done.6 = f32[64,128]{1,0:T(8,128)S(1)} collective-permute-done((f32[64,128]{1,0:T(8,128)S(1)}, f32[64,128]{1,0:T(8,128)S(1)}, u32[]{:S(2)}, u32[]{:S(2)}) %collective-permute-start.6) | collective-permute-done | bytes 32800 | tf_op jit(solution)/shard_map/ppermute | solution.py:236
  74.9 0.6 collective-permute-start.9
  75.5 2.0 %collective-permute-start.8 = (f32[64,128]{1,0:T(8,128)S(1)}, f32[64,128]{1,0:T(8,128)S(1)}, u32[]{:S(2)}, u32[]{:S(2)}) collective-permute-start(f32[64,128]{1,0:T(8,128)S(1)} %add.59), channel_id=1, source_target_pairs={{0,32},{16,48},{32,0},{48,16},{1,33},{17,49},{33,1},{49,17},{2,34}... | collective-permute-start | bytes 98312 | tf_op jit(solution)/shard_map/ppermute | solution.py:250
  77.6 0.0 collective-permute-start.7
  77.6 1.8 %inverse.1.inverse_ref = f32[64,64]{1,0:T(8,128)S(1)} custom-call(f32[64,64]{1,0:T(8,128)S(1)} %get-tuple-element.35.gram_ref), custom_call_target="tpu_custom_call" | custom-call | flops 262144 | bytes 32768 | tf_op jit(solution)/shard_map/inverse/pallas_call | solution.py:172
  79.4 0.0 collective-permute-done.9
  79.4 1.6 %collective-permute-done.8 = f32[64,128]{1,0:T(8,128)S(1)} collective-permute-done((f32[64,128]{1,0:T(8,128)S(1)}, f32[64,128]{1,0:T(8,128)S(1)}, u32[]{:S(2)}, u32[]{:S(2)}) %collective-permute-start.8) | collective-permute-done | bytes 32800 | tf_op jit(solution)/shard_map/ppermute | solution.py:250
  81.0 1.7 %collective-permute-done.7 = f32[64,128]{1,0:T(8,128)S(1)} collective-permute-done((f32[64,128]{1,0:T(8,128)S(1)}, f32[64,128]{1,0:T(8,128)S(1)}, u32[]{:S(2)}, u32[]{:S(2)}) %collective-permute-start.7) | collective-permute-done | bytes 32800 | tf_op jit(solution)/shard_map/ppermute | solution.py:250
  82.7 0.6 collective-permute-start.12
  83.3 3.3 %collective-permute-start.11 = (f32[64,128]{1,0:T(8,128)S(1)}, f32[64,128]{1,0:T(8,128)S(1)}, u32[]{:S(2)}, u32[]{:S(2)}) collective-permute-start(f32[64,128]{1,0:T(8,128)S(1)} %add_add_fusion.2), channel_id=1, source_target_pairs={{0,128},{64,192},{128,0},{192,64},{1,129},{65,193},{129,1},{193,65... | collective-permute-start | bytes 98312 | tf_op jit(solution)/shard_map/ppermute | solution.py:250
  86.5 0.2 collective-permute-start.10
  86.8 1.3 %collective-permute-done.12 = f32[64,128]{1,0:T(8,128)S(1)} collective-permute-done((f32[64,128]{1,0:T(8,128)S(1)}, f32[64,128]{1,0:T(8,128)S(1)}, u32[]{:S(2)}, u32[]{:S(2)}) %collective-permute-start.12) | collective-permute-done | bytes 32800 | tf_op jit(solution)/shard_map/ppermute | solution.py:250
  88.1 0.7 collective-permute-done.11
  88.8 1.7 %collective-permute-done.10 = f32[64,128]{1,0:T(8,128)S(1)} collective-permute-done((f32[64,128]{1,0:T(8,128)S(1)}, f32[64,128]{1,0:T(8,128)S(1)}, u32[]{:S(2)}, u32[]{:S(2)}) %collective-permute-start.10) | collective-permute-done | bytes 32800 | tf_op jit(solution)/shard_map/ppermute | solution.py:250
  90.5 4.2 %final.1 = (bf16[2,4096,128]{2,1,0:T(8,128)(2,1)}, f32[2,4096,128]{2,1,0:T(8,128)}, f32[64,128]{1,0:T(8,128)}) custom-call(s32[1]{0:T(128)} %bitcast.half_ref, f32[2,2048,128]{2,1,0:T(8,128)S(1)} %dynamic-slice_add_fusion.1.combined_ref.own_combined_ref, f32[2,2048,128]{2,1,0:T(8,128)S(1)} %dynamic-slice_add_fusion.combined_ref.other_combined_ref, ...), custom_call_target="tpu_custom_call" | custom-call | flops 1073741824 | bytes 6291456 | tf_op jit(solution)/shard_map/final/pallas_call | solution.py:214
  (5 shorter events, 0.0 us)
Async XLA Ops:
  0.6 0.8 copy-start
  1.4 2.9 %copy-start.1 = (f32[128,64]{0,1:T(8,128)S(1)}, f32[128,64]{0,1:T(8,128)}, u32[]{:S(2)}) copy-start(f32[128,64]{0,1:T(8,128)} %param.5) | copy-start | bytes 98308
  4.2 3.0 %collective-permute-start = (f32[2048,128]{1,0:T(8,128)S(1)}, f32[2048,128]{1,0:T(8,128)S(1)}, u32[]{:S(2)}, u32[]{:S(2)}) collective-permute-start(f32[2048,128]{1,0:T(8,128)S(1)} %left.3), channel_id=1, source_target_pairs={{0,8},{8,0},{1,9},{9,1},{2,10},{10,2},{3,11},{11,3},{4,12},{12,4},... | collective-permute-start | bytes 3145736 | tf_op jit(solution)/shard_map/ppermute | solution.py:236
  30.3 4.4 %collective-permute-start.1 = (f32[128,128]{1,0:T(8,128)S(1)}, f32[128,128]{1,0:T(8,128)S(1)}, u32[]{:S(2)}, u32[]{:S(2)}) collective-permute-start(f32[128,128]{1,0:T(8,128)S(1)} %reduce_sum.9), channel_id=1, source_target_pairs={{0,1},{1,0},{2,3},{3,2},{4,5},{5,4},{6,7},{7,6},{8,9},{9,8},{10,11... | collective-permute-start | bytes 196616 | tf_op jit(solution)/shard_map/ppermute | solution.py:275
  34.6 8.2 %copy-start.2 = (f32[1,8192,128]{2,1,0:T(8,128)S(1)}, f32[1,8192,128]{2,1,0:T(8,128)}, u32[]{:S(2)}) copy-start(f32[1,8192,128]{2,1,0:T(8,128)} %param.4) | copy-start | bytes 12582916
  34.6 8.2 %collective-permute-start.2 = (f32[128,128]{1,0:T(8,128)S(1)}, f32[128,128]{1,0:T(8,128)S(1)}, u32[]{:S(2)}, u32[]{:S(2)}) collective-permute-start(f32[128,128]{1,0:T(8,128)S(1)} %add.51), channel_id=1, source_target_pairs={{0,7},{1,2},{2,1},{3,4},{4,3},{5,6},{6,5},{7,0},{8,15},{9,10},{10,... | collective-permute-start | bytes 196616 | tf_op jit(solution)/shard_map/ppermute | solution.py:277
  42.8 4.3 %collective-permute-start.3 = (f32[128,128]{1,0:T(8,128)S(1)}, f32[128,128]{1,0:T(8,128)S(1)}, u32[]{:S(2)}, u32[]{:S(2)}) collective-permute-start(f32[128,128]{1,0:T(8,128)S(1)} %collective-permute-done.2), channel_id=1, source_target_pairs={{0,1},{1,0},{2,3},{3,2},{4,5},{5,4},{6,7},{7,6},{8,9},{9,8},{10,11... | collective-permute-start | bytes 196616 | tf_op jit(solution)/shard_map/ppermute | solution.py:279
  47.1 5.5 %collective-permute-start.4 = (f32[128,128]{1,0:T(8,128)S(1)}, f32[128,128]{1,0:T(8,128)S(1)}, u32[]{:S(2)}, u32[]{:S(2)}) collective-permute-start(f32[128,128]{1,0:T(8,128)S(1)} %collective-permute-done.3), channel_id=1, source_target_pairs={{0,7},{1,2},{2,1},{3,4},{4,3},{5,6},{6,5},{7,0},{8,15},{9,10},{10,... | collective-permute-start | bytes 196616 | tf_op jit(solution)/shard_map/ppermute | solution.py:281
  69.0 2.7 %collective-permute-start.5 = (f32[2048,128]{1,0:T(8,128)S(1)}, f32[2048,128]{1,0:T(8,128)S(1)}, u32[]{:S(2)}, u32[]{:S(2)}) collective-permute-start(f32[2048,128]{1,0:T(8,128)S(1)} %bitcast.10), channel_id=1, source_target_pairs={{0,8},{8,0},{1,9},{9,1},{2,10},{10,2},{3,11},{11,3},{4,12},{12,4},... | collective-permute-start | bytes 3145736 | tf_op jit(solution)/shard_map/ppermute | solution.py:236
  73.6 1.3 %collective-permute-start.6 = (f32[64,128]{1,0:T(8,128)S(1)}, f32[64,128]{1,0:T(8,128)S(1)}, u32[]{:S(2)}, u32[]{:S(2)}) collective-permute-start(f32[64,128]{1,0:T(8,128)S(1)} %get-tuple-element.34), channel_id=1, source_target_pairs={{0,8},{8,0},{1,9},{9,1},{2,10},{10,2},{3,11},{11,3},{4,12},{12,4},... | collective-permute-start | bytes 98312 | tf_op jit(solution)/shard_map/ppermute | solution.py:236
  74.9 4.5 %collective-permute-start.9 = (f32[64,128]{1,0:T(8,128)S(1)}, f32[64,128]{1,0:T(8,128)S(1)}, u32[]{:S(2)}, u32[]{:S(2)}) collective-permute-start(f32[64,128]{1,0:T(8,128)S(1)} %add.59), channel_id=1, source_target_pairs={{0,48},{16,0},{32,16},{48,32},{1,49},{17,1},{33,17},{49,33},{2,50}... | collective-permute-start | bytes 98312 | tf_op jit(solution)/shard_map/ppermute | solution.py:250
  75.5 5.4 %collective-permute-start.8 = (f32[64,128]{1,0:T(8,128)S(1)}, f32[64,128]{1,0:T(8,128)S(1)}, u32[]{:S(2)}, u32[]{:S(2)}) collective-permute-start(f32[64,128]{1,0:T(8,128)S(1)} %add.59), channel_id=1, source_target_pairs={{0,32},{16,48},{32,0},{48,16},{1,33},{17,49},{33,1},{49,17},{2,34}... | collective-permute-start | bytes 98312 | tf_op jit(solution)/shard_map/ppermute | solution.py:250
  77.6 5.1 %collective-permute-start.7 = (f32[64,128]{1,0:T(8,128)S(1)}, f32[64,128]{1,0:T(8,128)S(1)}, u32[]{:S(2)}, u32[]{:S(2)}) collective-permute-start(f32[64,128]{1,0:T(8,128)S(1)} %add.59), channel_id=1, source_target_pairs={{0,16},{16,32},{32,48},{48,0},{1,17},{17,33},{33,49},{49,1},{2,18}... | collective-permute-start | bytes 98312 | tf_op jit(solution)/shard_map/ppermute | solution.py:250
  82.7 5.4 %collective-permute-start.12 = (f32[64,128]{1,0:T(8,128)S(1)}, f32[64,128]{1,0:T(8,128)S(1)}, u32[]{:S(2)}, u32[]{:S(2)}) collective-permute-start(f32[64,128]{1,0:T(8,128)S(1)} %add_add_fusion.2), channel_id=1, source_target_pairs={{0,192},{64,0},{128,64},{192,128},{1,193},{65,1},{129,65},{193,129... | collective-permute-start | bytes 98312 | tf_op jit(solution)/shard_map/ppermute | solution.py:250
  83.3 5.5 %collective-permute-start.11 = (f32[64,128]{1,0:T(8,128)S(1)}, f32[64,128]{1,0:T(8,128)S(1)}, u32[]{:S(2)}, u32[]{:S(2)}) collective-permute-start(f32[64,128]{1,0:T(8,128)S(1)} %add_add_fusion.2), channel_id=1, source_target_pairs={{0,128},{64,192},{128,0},{192,64},{1,129},{65,193},{129,1},{193,65... | collective-permute-start | bytes 98312 | tf_op jit(solution)/shard_map/ppermute | solution.py:250
  86.5 3.9 %collective-permute-start.10 = (f32[64,128]{1,0:T(8,128)S(1)}, f32[64,128]{1,0:T(8,128)S(1)}, u32[]{:S(2)}, u32[]{:S(2)}) collective-permute-start(f32[64,128]{1,0:T(8,128)S(1)} %add_add_fusion.2), channel_id=1, source_target_pairs={{0,64},{64,128},{128,192},{192,0},{1,65},{65,129},{129,193},{193,1... | collective-permute-start | bytes 98312 | tf_op jit(solution)/shard_map/ppermute | solution.py:250

commit v6 on v5

--- a/solution.py
+++ b/solution.py
@@ -244,24 +244,22 @@
     return lax.all_to_all(jnp.tile(a, (count, 1)), axes, 0, 0, tiled=True)
 
 
+def sum_of_four(a, axis):
+    places = range(0, lax.axis_size(axis), 4)
+    others = [lax.ppermute(a, axis, [(p + i, p + (i ^ k)) for p in places for i in range(4)]) for k in (1, 2, 3)]
+    return (a + others[0]) + (others[1] + others[2])
+
+
 def sum_over_replicas(a, gram):
-    a = a + swap(a)
-    for axis in ("y", "x"):
-        near, far, back = [lax.ppermute(a, axis, [(i, (i + k) % 4) for i in range(4)]) for k in (1, 2, 3)]
-        a = (a + near) + (far + back)
-        if axis == "y":
-            a, inverse = lax.optimization_barrier((a, inverse_lower(gram)))
-    return a, inverse
+    a = sum_of_four(a + swap(a), "y")
+    a, inverse = lax.optimization_barrier((a, inverse_lower(gram)))
+    return sum_of_four(a, "x"), inverse
 
 
 def combined_half(grad, error, half):
     start = half[0] * HALF
     part = (2, HALF, COLS)
     return lax.dynamic_slice(grad, (0, start, 0), part).astype(jnp.float32) + lax.dynamic_slice(error, (0, start, 0), part)
-
-
-RING_A = [(i, i ^ 1) for i in range(8)]
-RING_B = [(i, (i + 1) % 8 if i % 2 else (i - 1) % 8) for i in range(8)]
 
 
 def shards(grad, error, warm_q):
@@ -272,14 +270,12 @@
     away = left_half(1 - half, grad, error, warm_t)
     keep = left_half(half, grad, error, warm_t)
     piece = scatter_sum(keep + swap(away), ("x", "y"), 16)
-    pair = piece + lax.ppermute(piece, "z", RING_A)
-    pair, grad, error = lax.optimization_barrier((pair, grad, error))
-    near = lax.ppermute(pair, "z", RING_B)
-    near, own_combined, grad, error = lax.optimization_barrier((near, combined_half(grad, error, half), grad, error))
-    far = lax.ppermute(near, "z", RING_A)
-    far, other_combined = lax.optimization_barrier((far, combined_half(grad, error, 1 - half)))
-    opposite = lax.ppermute(far, "z", RING_B)
-    piece = (pair + near) + (far + opposite)
+    piece, grad, error = lax.optimization_barrier((sum_of_four(piece, "z"), grad, error))
+    piece = piece + lax.ppermute(piece, "z", [(i, 7 - i) for i in range(8)])
+    own_combined = combined_half(grad, error, half)
+    own_combined, grad, error = lax.optimization_barrier((own_combined, grad, error))
+    other_combined = combined_half(grad, error, 1 - half)
+    piece, own_combined, other_combined = lax.optimization_barrier((piece, own_combined, other_combined))
     own = gather(piece, ("x", "y"), 16)
     other = swap(own)
     sums = right_own(own_combined, own)

time: 95.2 us -> 92.4 us (0.971)
  waiting for transfers between devices: 16.4 us -> 11.2 us
  blocking collectives: 39.1 us -> 42.4 us
  other arithmetic: 3.78 us -> 2.26 us
    ppermute x10, waiting for transfers between devices: 14.5 us -> 9.28 us  [the longest x9 8.53 us: sum_of_four(): lax.ppermute(a, axis, [(p + i, p + (i ^ k)) for p in places for i in rang...]
    all_to_all x1, blocking collectives: 16.3 us -> 19.5 us  [gather(): return lax.all_to_all(jnp.tile(a, (count, 1)), axes, 0, 0, tiled=True)]
    add x2, other arithmetic: 3.52 us -> 2.04 us  [combined_half(): lax.dynamic_slice(grad, (0, start, 0), part).astype(jnp.float32)]
  transfers between devices with their start and end apart: 13 -> 13, of which waited for: 11 -> 9; matrix products, arithmetic and copies ran while one was open for 4% -> 2% of each run, Pallas kernels for 7% -> 7%
where the time goes in v6:
time: 92.4 us; the launch traced here: 91.5 us
  blocking collectives  42.4 us (46%)
  starting transfers between devices  18.4 us (20%)
  Pallas kernels  15.5 us (17%)
  waiting for transfers between devices  11.2 us (12%)
  other arithmetic  2.26 us (2%)
    all_to_all x1, blocking collectives, scatter_sum(): lax.all_to_all(a, axes, 0, 0, tiled=True).reshape(count, -1, 128).sum(0)  23 us
    all_to_all x1, blocking collectives, gather(): return lax.all_to_all(jnp.tile(a, (count, 1)), axes, 0, 0, tiled=True)  19.5 us
    ppermute x9, starting transfers between devices, sum_of_four(): lax.ppermute(a, axis, [(p + i, p + (i ^ k)) for p in places for i in rang...  13.6 us
    ppermute x9, waiting for transfers between devices, sum_of_four(): lax.ppermute(a, axis, [(p + i, p + (i ^ k)) for p in places for i in rang...  8.53 us
    pallas_call x2, Pallas kernels, left_half(): pl.pallas_call(left_kernel, out_shape=jax.ShapeDtypeStruct((HALF, 128), j...  5.7 us
    ppermute x1, starting transfers between devices, shards(): piece = piece + lax.ppermute(piece, 'z', [(i, 7 - i) for i in range(8)])  4.43 us
    pallas_call x1, Pallas kernels, final(): pl.pallas_call(final_kernel, out_shape=(jax.ShapeDtypeStruct((2, ROWS //...  4.21 us
    add x2, other arithmetic, combined_half(): lax.dynamic_slice(grad, (0, start, 0), part).astype(jnp.float32)  2.04 us
  transfers between devices with their start and end apart: 13, of which 9 were waited for; matrix products, arithmetic and copies ran while one was open for 2% of the time, Pallas kernels for 7%

profile of v6, /device:TPU:6, one launch (start us, length us, event | category | flops | bytes accessed | tf_op | source)
XLA Modules:
  0.0 91.5 jit_solution(7939039559614472121)
XLA Ops:
  0.6 0.0 copy-start
  0.6 0.7 copy-done
  1.4 0.0 copy-start.1
  1.4 2.8 %left.3 = f32[2048,128]{1,0:T(8,128)S(1)} custom-call(s32[1]{0:T(128)S(6)} %sub.4.half_ref, bf16[2,4096,128]{2,1,0:T(8,128)(2,1)} %bitcast.19, f32[2,4096,128]{2,1,0:T(8,128)} %bitcast.15, f32[64,128]{1,0:T(8,128)S(1)} %bitcast.13), custom_call_target="tpu_custom_call" | custom-call | flops 536870912 | bytes 3145728 | tf_op jit(solution)/shard_map/left/pallas_call | solution.py:78
  4.2 0.1 collective-permute-start
  4.3 0.0 copy-done.1
  4.3 2.9 %left.2 = f32[2048,128]{1,0:T(8,128)S(1)} custom-call(s32[1]{0:T(128)} %bitcast.half_ref, bf16[2,4096,128]{2,1,0:T(8,128)(2,1)} %bitcast.20, f32[2,4096,128]{2,1,0:T(8,128)} %bitcast.16, f32[64,128]{1,0:T(8,128)S(1)} %bitcast.14), custom_call_target="tpu_custom_call" | custom-call | flops 536870912 | bytes 3145728 | tf_op jit(solution)/shard_map/left/pallas_call | solution.py:78
  7.2 0.0 collective-permute-done
  7.2 0.1 add.50
  7.3 0.0 copy-start.3
  7.4 23.0 %all_to_all.17 = f32[16,128,128]{2,1,0:T(8,128)S(1)} all-to-all(f32[16,128,128]{2,1,0:T(8,128)S(1)} %bitcast.23), channel_id=1, replica_groups=mesh['x'=4,'y'=4,'c'=2,'z'=8] {'x','y'}, dimensions={0} | all-to-all | bytes 2097152 | tf_op jit(solution)/shard_map/all_to_all | solution.py:240
  30.3 0.1 reduce_sum.9
  30.4 4.7 %collective-permute-start.3 = (f32[128,128]{1,0:T(8,128)S(1)}, f32[128,128]{1,0:T(8,128)S(1)}, u32[]{:S(2)}, u32[]{:S(2)}) collective-permute-start(f32[128,128]{1,0:T(8,128)S(1)} %reduce_sum.9), channel_id=1, source_target_pairs={{0,3},{1,2},{2,1},{3,0},{4,7},{5,6},{6,5},{7,4},{8,11},{9,10},{10,... | collective-permute-start | bytes 196616 | tf_op jit(solution)/shard_map/ppermute | solution.py:249
  35.1 0.0 collective-permute-start.2
  35.1 0.7 collective-permute-start.1
  35.7 1.7 %collective-permute-done.3 = f32[128,128]{1,0:T(8,128)S(1)} collective-permute-done((f32[128,128]{1,0:T(8,128)S(1)}, f32[128,128]{1,0:T(8,128)S(1)}, u32[]{:S(2)}, u32[]{:S(2)}) %collective-permute-start.3) | collective-permute-done | bytes 65568 | tf_op jit(solution)/shard_map/ppermute | solution.py:249
  37.4 2.8 %collective-permute-done.2 = f32[128,128]{1,0:T(8,128)S(1)} collective-permute-done((f32[128,128]{1,0:T(8,128)S(1)}, f32[128,128]{1,0:T(8,128)S(1)}, u32[]{:S(2)}, u32[]{:S(2)}) %collective-permute-start.2) | collective-permute-done | bytes 65568 | tf_op jit(solution)/shard_map/ppermute | solution.py:249
  40.2 0.0 collective-permute-done.1
  40.3 0.0 copy-start.2
  40.3 4.4 %collective-permute-start.4 = (f32[128,128]{1,0:T(8,128)S(1)}, f32[128,128]{1,0:T(8,128)S(1)}, u32[]{:S(2)}, u32[]{:S(2)}) collective-permute-start(f32[128,128]{1,0:T(8,128)S(1)} %add_add_fusion), channel_id=1, source_target_pairs={{0,7},{1,6},{2,5},{3,4},{4,3},{5,2},{6,1},{7,0},{8,15},{9,14},{10,... | collective-permute-start | bytes 196616 | tf_op jit(solution)/shard_map/ppermute | solution.py:274
  44.7 0.0 copy-done.3
  44.7 1.8 %dynamic-slice_add_fusion.1.combined_ref.own_combined_ref = f32[2,2048,128]{2,1,0:T(8,128)S(1)} fusion(f32[2,4096,128]{2,1,0:T(8,128)} %bitcast.17, s32[]{:T(128)S(6)} %select_n.8, bf16[2,4096,128]{2,1,0:T(8,128)(2,1)S(1)} %bitcast.21), kind=kLoop, calls=%fused_computation.1 | loop fusion | flops 1048576 | bytes 5242884 | tf_op jit(solution)/shard_map/add | solution.py:262
  46.5 0.0 copy-done.2
  46.5 0.3 dynamic-slice_add_fusion.combined_ref.other_combined_ref
  46.8 0.8 collective-permute-done.4
  47.5 0.1 tile.2
  47.6 19.5 %all_to_all.18 = f32[16,128,128]{2,1,0:T(8,128)S(1)} all-to-all(f32[16,128,128]{2,1,0:T(8,128)S(1)} %tile.2), channel_id=1, replica_groups=mesh['x'=4,'y'=4,'c'=2,'z'=8] {'x','y'}, dimensions={0} | all-to-all | bytes 2097152 | tf_op jit(solution)/shard_map/all_to_all | solution.py:244
  67.1 0.0 collective-permute-start.5
  67.1 1.8 %right_own.1 = (f32[256,256]{1,0:T(8,128)S(1)}, f32[256,256]{1,0:T(8,128)S(1)}, f32[128,128]{1,0:T(8,128)S(1)}) custom-call(f32[2,2048,128]{2,1,0:T(8,128)S(1)} %dynamic-slice_add_fusion.1.combined_ref.own_combined_ref, f32[2048,128]{1,0:T(8,128)S(1)} %bitcast.11), custom_call_target="tpu_custom_call" | custom-call | flops 939524096 | bytes 3145728 | tf_op jit(solution)/shard_map/right_own/pallas_call | solution.py:131
  69.0 0.8 collective-permute-done.5.factor_ref.other_ref
  69.8 2.0 %right_other.1 = (f32[64,128]{1,0:T(8,128)S(1)}, f32[64,64]{1,0:T(8,128)S(1)}) custom-call(f32[2,2048,128]{2,1,0:T(8,128)S(1)} %dynamic-slice_add_fusion.combined_ref.other_combined_ref, f32[2048,128]{1,0:T(8,128)S(1)} %collective-permute-done.5.factor_ref.other_ref, f32[256,256]{1,0:T(8,128)S(1)} %get-tuple-element.31.acc_in, ...), custom_call_target="tpu_custom_call" | custom-call | flops 939524096 | bytes 3145728 | tf_op jit(solution)/shard_map/right_other/pallas_call | solution.py:143
  71.8 0.2 collective-permute-start.6
  72.0 1.1 %collective-permute-done.6 = f32[64,128]{1,0:T(8,128)S(1)} collective-permute-done((f32[64,128]{1,0:T(8,128)S(1)}, f32[64,128]{1,0:T(8,128)S(1)}, u32[]{:S(2)}, u32[]{:S(2)}) %collective-permute-start.6) | collective-permute-done | bytes 32800 | tf_op jit(solution)/shard_map/ppermute | solution.py:236
  73.1 0.6 collective-permute-start.9
  73.7 2.0 %collective-permute-start.8 = (f32[64,128]{1,0:T(8,128)S(1)}, f32[64,128]{1,0:T(8,128)S(1)}, u32[]{:S(2)}, u32[]{:S(2)}) collective-permute-start(f32[64,128]{1,0:T(8,128)S(1)} %add.59), channel_id=1, source_target_pairs={{0,32},{16,48},{32,0},{48,16},{1,33},{17,49},{33,1},{49,17},{2,34}... | collective-permute-start | bytes 98312 | tf_op jit(solution)/shard_map/ppermute | solution.py:249
  75.7 1.5 %collective-permute-start.7 = (f32[64,128]{1,0:T(8,128)S(1)}, f32[64,128]{1,0:T(8,128)S(1)}, u32[]{:S(2)}, u32[]{:S(2)}) collective-permute-start(f32[64,128]{1,0:T(8,128)S(1)} %add.59), channel_id=1, source_target_pairs={{0,16},{16,0},{32,48},{48,32},{1,17},{17,1},{33,49},{49,33},{2,18}... | collective-permute-start | bytes 98312 | tf_op jit(solution)/shard_map/ppermute | solution.py:249
  77.2 1.8 %inverse.1.inverse_ref = f32[64,64]{1,0:T(8,128)S(1)} custom-call(f32[64,64]{1,0:T(8,128)S(1)} %get-tuple-element.35.gram_ref), custom_call_target="tpu_custom_call" | custom-call | flops 262144 | bytes 32768 | tf_op jit(solution)/shard_map/inverse/pallas_call | solution.py:172
  79.0 0.0 collective-permute-done.9
  79.0 0.1 collective-permute-done.8
  79.1 0.5 collective-permute-done.7
  79.6 2.2 %collective-permute-start.12 = (f32[64,128]{1,0:T(8,128)S(1)}, f32[64,128]{1,0:T(8,128)S(1)}, u32[]{:S(2)}, u32[]{:S(2)}) collective-permute-start(f32[64,128]{1,0:T(8,128)S(1)} %add_add_fusion.2), channel_id=1, source_target_pairs={{0,192},{64,128},{128,64},{192,0},{1,193},{65,129},{129,65},{193,1... | collective-permute-start | bytes 98312 | tf_op jit(solution)/shard_map/ppermute | solution.py:249
  81.8 0.5 collective-permute-start.11
  82.4 1.5 %collective-permute-start.10 = (f32[64,128]{1,0:T(8,128)S(1)}, f32[64,128]{1,0:T(8,128)S(1)}, u32[]{:S(2)}, u32[]{:S(2)}) collective-permute-start(f32[64,128]{1,0:T(8,128)S(1)} %add_add_fusion.2), channel_id=1, source_target_pairs={{0,64},{64,0},{128,192},{192,128},{1,65},{65,1},{129,193},{193,129... | collective-permute-start | bytes 98312 | tf_op jit(solution)/shard_map/ppermute | solution.py:249
  83.8 1.3 %collective-permute-done.12 = f32[64,128]{1,0:T(8,128)S(1)} collective-permute-done((f32[64,128]{1,0:T(8,128)S(1)}, f32[64,128]{1,0:T(8,128)S(1)}, u32[]{:S(2)}, u32[]{:S(2)}) %collective-permute-start.12) | collective-permute-done | bytes 32800 | tf_op jit(solution)/shard_map/ppermute | solution.py:249
  85.1 2.1 %collective-permute-done.11 = f32[64,128]{1,0:T(8,128)S(1)} collective-permute-done((f32[64,128]{1,0:T(8,128)S(1)}, f32[64,128]{1,0:T(8,128)S(1)}, u32[]{:S(2)}, u32[]{:S(2)}) %collective-permute-start.11) | collective-permute-done | bytes 32800 | tf_op jit(solution)/shard_map/ppermute | solution.py:249
  87.2 0.0 collective-permute-done.10
  87.2 4.2 %final.1 = (bf16[2,4096,128]{2,1,0:T(8,128)(2,1)}, f32[2,4096,128]{2,1,0:T(8,128)}, f32[64,128]{1,0:T(8,128)}) custom-call(s32[1]{0:T(128)} %bitcast.half_ref, f32[2,2048,128]{2,1,0:T(8,128)S(1)} %dynamic-slice_add_fusion.1.combined_ref.own_combined_ref, f32[2,2048,128]{2,1,0:T(8,128)S(1)} %dynamic-slice_add_fusion.combined_ref.other_combined_ref, ...), custom_call_target="tpu_custom_call" | custom-call | flops 1073741824 | bytes 6291456 | tf_op jit(solution)/shard_map/final/pallas_call | solution.py:214
  (5 shorter events, 0.0 us)
Async XLA Ops:
  0.6 0.8 copy-start
  1.4 2.9 %copy-start.1 = (f32[128,64]{0,1:T(8,128)S(1)}, f32[128,64]{0,1:T(8,128)}, u32[]{:S(2)}) copy-start(f32[128,64]{0,1:T(8,128)} %param.5) | copy-start | bytes 98308
  4.2 3.0 %collective-permute-start = (f32[2048,128]{1,0:T(8,128)S(1)}, f32[2048,128]{1,0:T(8,128)S(1)}, u32[]{:S(2)}, u32[]{:S(2)}) collective-permute-start(f32[2048,128]{1,0:T(8,128)S(1)} %left.3), channel_id=1, source_target_pairs={{0,8},{8,0},{1,9},{9,1},{2,10},{10,2},{3,11},{11,3},{4,12},{12,4},... | collective-permute-start | bytes 3145736 | tf_op jit(solution)/shard_map/ppermute | solution.py:236
  7.3 37.4 %copy-start.3 = (bf16[1,8192,128]{2,1,0:T(8,128)(2,1)S(1)}, bf16[1,8192,128]{2,1,0:T(8,128)(2,1)}, u32[]{:S(2)}) copy-start(bf16[1,8192,128]{2,1,0:T(8,128)(2,1)} %param.3) | copy-start | bytes 6291460
  30.4 7.1 %collective-permute-start.3 = (f32[128,128]{1,0:T(8,128)S(1)}, f32[128,128]{1,0:T(8,128)S(1)}, u32[]{:S(2)}, u32[]{:S(2)}) collective-permute-start(f32[128,128]{1,0:T(8,128)S(1)} %reduce_sum.9), channel_id=1, source_target_pairs={{0,3},{1,2},{2,1},{3,0},{4,7},{5,6},{6,5},{7,4},{8,11},{9,10},{10,... | collective-permute-start | bytes 196616 | tf_op jit(solution)/shard_map/ppermute | solution.py:249
  35.1 5.2 %collective-permute-start.2 = (f32[128,128]{1,0:T(8,128)S(1)}, f32[128,128]{1,0:T(8,128)S(1)}, u32[]{:S(2)}, u32[]{:S(2)}) collective-permute-start(f32[128,128]{1,0:T(8,128)S(1)} %reduce_sum.9), channel_id=1, source_target_pairs={{0,2},{1,3},{2,0},{3,1},{4,6},{5,7},{6,4},{7,5},{8,10},{9,11},{10,... | collective-permute-start | bytes 196616 | tf_op jit(solution)/shard_map/ppermute | solution.py:249
  35.1 5.2 %collective-permute-start.1 = (f32[128,128]{1,0:T(8,128)S(1)}, f32[128,128]{1,0:T(8,128)S(1)}, u32[]{:S(2)}, u32[]{:S(2)}) collective-permute-start(f32[128,128]{1,0:T(8,128)S(1)} %reduce_sum.9), channel_id=1, source_target_pairs={{0,1},{1,0},{2,3},{3,2},{4,5},{5,4},{6,7},{7,6},{8,9},{9,8},{10,11... | collective-permute-start | bytes 196616 | tf_op jit(solution)/shard_map/ppermute | solution.py:249
  40.3 6.2 %copy-start.2 = (f32[1,8192,128]{2,1,0:T(8,128)S(1)}, f32[1,8192,128]{2,1,0:T(8,128)}, u32[]{:S(2)}) copy-start(f32[1,8192,128]{2,1,0:T(8,128)} %param.4) | copy-start | bytes 12582916
  40.3 7.2 %collective-permute-start.4 = (f32[128,128]{1,0:T(8,128)S(1)}, f32[128,128]{1,0:T(8,128)S(1)}, u32[]{:S(2)}, u32[]{:S(2)}) collective-permute-start(f32[128,128]{1,0:T(8,128)S(1)} %add_add_fusion), channel_id=1, source_target_pairs={{0,7},{1,6},{2,5},{3,4},{4,3},{5,2},{6,1},{7,0},{8,15},{9,14},{10,... | collective-permute-start | bytes 196616 | tf_op jit(solution)/shard_map/ppermute | solution.py:274
  67.1 2.7 %collective-permute-start.5 = (f32[2048,128]{1,0:T(8,128)S(1)}, f32[2048,128]{1,0:T(8,128)S(1)}, u32[]{:S(2)}, u32[]{:S(2)}) collective-permute-start(f32[2048,128]{1,0:T(8,128)S(1)} %bitcast.10), channel_id=1, source_target_pairs={{0,8},{8,0},{1,9},{9,1},{2,10},{10,2},{3,11},{11,3},{4,12},{12,4},... | collective-permute-start | bytes 3145736 | tf_op jit(solution)/shard_map/ppermute | solution.py:236
  71.8 1.3 %collective-permute-start.6 = (f32[64,128]{1,0:T(8,128)S(1)}, f32[64,128]{1,0:T(8,128)S(1)}, u32[]{:S(2)}, u32[]{:S(2)}) collective-permute-start(f32[64,128]{1,0:T(8,128)S(1)} %get-tuple-element.34), channel_id=1, source_target_pairs={{0,8},{8,0},{1,9},{9,1},{2,10},{10,2},{3,11},{11,3},{4,12},{12,4},... | collective-permute-start | bytes 98312 | tf_op jit(solution)/shard_map/ppermute | solution.py:236
  73.1 5.9 %collective-permute-start.9 = (f32[64,128]{1,0:T(8,128)S(1)}, f32[64,128]{1,0:T(8,128)S(1)}, u32[]{:S(2)}, u32[]{:S(2)}) collective-permute-start(f32[64,128]{1,0:T(8,128)S(1)} %add.59), channel_id=1, source_target_pairs={{0,48},{16,32},{32,16},{48,0},{1,49},{17,33},{33,17},{49,1},{2,50}... | collective-permute-start | bytes 98312 | tf_op jit(solution)/shard_map/ppermute | solution.py:249
  73.7 5.5 %collective-permute-start.8 = (f32[64,128]{1,0:T(8,128)S(1)}, f32[64,128]{1,0:T(8,128)S(1)}, u32[]{:S(2)}, u32[]{:S(2)}) collective-permute-start(f32[64,128]{1,0:T(8,128)S(1)} %add.59), channel_id=1, source_target_pairs={{0,32},{16,48},{32,0},{48,16},{1,33},{17,49},{33,1},{49,17},{2,34}... | collective-permute-start | bytes 98312 | tf_op jit(solution)/shard_map/ppermute | solution.py:249
  75.7 3.9 %collective-permute-start.7 = (f32[64,128]{1,0:T(8,128)S(1)}, f32[64,128]{1,0:T(8,128)S(1)}, u32[]{:S(2)}, u32[]{:S(2)}) collective-permute-start(f32[64,128]{1,0:T(8,128)S(1)} %add.59), channel_id=1, source_target_pairs={{0,16},{16,0},{32,48},{48,32},{1,17},{17,1},{33,49},{49,33},{2,18}... | collective-permute-start | bytes 98312 | tf_op jit(solution)/shard_map/ppermute | solution.py:249
  79.6 5.5 %collective-permute-start.12 = (f32[64,128]{1,0:T(8,128)S(1)}, f32[64,128]{1,0:T(8,128)S(1)}, u32[]{:S(2)}, u32[]{:S(2)}) collective-permute-start(f32[64,128]{1,0:T(8,128)S(1)} %add_add_fusion.2), channel_id=1, source_target_pairs={{0,192},{64,128},{128,64},{192,0},{1,193},{65,129},{129,65},{193,1... | collective-permute-start | bytes 98312 | tf_op jit(solution)/shard_map/ppermute | solution.py:249
  81.8 5.4 %collective-permute-start.11 = (f32[64,128]{1,0:T(8,128)S(1)}, f32[64,128]{1,0:T(8,128)S(1)}, u32[]{:S(2)}, u32[]{:S(2)}) collective-permute-start(f32[64,128]{1,0:T(8,128)S(1)} %add_add_fusion.2), channel_id=1, source_target_pairs={{0,128},{64,192},{128,0},{192,64},{1,129},{65,193},{129,1},{193,65... | collective-permute-start | bytes 98312 | tf_op jit(solution)/shard_map/ppermute | solution.py:249
  82.4 4.9 %collective-permute-start.10 = (f32[64,128]{1,0:T(8,128)S(1)}, f32[64,128]{1,0:T(8,128)S(1)}, u32[]{:S(2)}, u32[]{:S(2)}) collective-permute-start(f32[64,128]{1,0:T(8,128)S(1)} %add_add_fusion.2), channel_id=1, source_target_pairs={{0,64},{64,0},{128,192},{192,128},{1,65},{65,1},{129,193},{193,129... | collective-permute-start | bytes 98312 | tf_op jit(solution)/shard_map/ppermute | solution.py:249

commit v7 on v6

--- a/solution.py
+++ b/solution.py
@@ -14,7 +14,7 @@
 REPLICAS = 32
 LEFT_BLOCK = 1024
 LEFT_STEPS = HALF // LEFT_BLOCK
-RIGHT_BLOCK = 512
+RIGHT_BLOCK = 1024
 VMEM_LIMIT = 24 * 1024 * 1024
 LEFT_VMEM_LIMIT = 51 * 1024 * 1024
 

time: 92.4 us -> 92.3 us (level)
  no operation moved by 1% of the time
where the time goes in v7:
time: 92.3 us; the launch traced here: 91.4 us
  blocking collectives  42.4 us (46%)
  starting transfers between devices  18.6 us (20%)
  Pallas kernels  14.7 us (16%)
  waiting for transfers between devices  11.6 us (13%)
  other arithmetic  2.26 us (2%)
  between operations  0.93 us (1%)
    all_to_all x1, blocking collectives, scatter_sum(): lax.all_to_all(a, axes, 0, 0, tiled=True).reshape(count, -1, 128).sum(0)  23 us
    all_to_all x1, blocking collectives, gather(): return lax.all_to_all(jnp.tile(a, (count, 1)), axes, 0, 0, tiled=True)  19.5 us
    ppermute x9, starting transfers between devices, sum_of_four(): lax.ppermute(a, axis, [(p + i, p + (i ^ k)) for p in places for i in rang...  13.8 us
    ppermute x9, waiting for transfers between devices, sum_of_four(): lax.ppermute(a, axis, [(p + i, p + (i ^ k)) for p in places for i in rang...  8.53 us
    pallas_call x2, Pallas kernels, left_half(): pl.pallas_call(left_kernel, out_shape=jax.ShapeDtypeStruct((HALF, 128), j...  5.7 us
    ppermute x1, starting transfers between devices, shards(): piece = piece + lax.ppermute(piece, 'z', [(i, 7 - i) for i in range(8)])  4.43 us
    pallas_call x1, Pallas kernels, final(): pl.pallas_call(final_kernel, out_shape=(jax.ShapeDtypeStruct((2, ROWS //...  4.21 us
    ppermute x3, waiting for transfers between devices, swap(): return lax.ppermute(a, 'c', [(0, 1), (1, 0)])  2.31 us
  transfers between devices with their start and end apart: 13, of which 9 were waited for; matrix products, arithmetic and copies ran while one was open for 2% of the time, Pallas kernels for 7%

profile of v7, /device:TPU:6, one launch (start us, length us, event | category | flops | bytes accessed | tf_op | source)
XLA Modules:
  0.0 91.4 jit_solution(10518136640368724463)
XLA Ops:
  0.6 0.0 copy-start
  0.6 0.7 copy-done
  1.4 0.0 copy-start.1
  1.4 2.8 %left.3 = f32[2048,128]{1,0:T(8,128)S(1)} custom-call(s32[1]{0:T(128)S(6)} %sub.4.half_ref, bf16[2,4096,128]{2,1,0:T(8,128)(2,1)} %bitcast.19, f32[2,4096,128]{2,1,0:T(8,128)} %bitcast.15, f32[64,128]{1,0:T(8,128)S(1)} %bitcast.13), custom_call_target="tpu_custom_call" | custom-call | flops 536870912 | bytes 3145728 | tf_op jit(solution)/shard_map/left/pallas_call | solution.py:78
  4.2 0.1 collective-permute-start
  4.3 0.0 copy-done.1
  4.3 2.9 %left.2 = f32[2048,128]{1,0:T(8,128)S(1)} custom-call(s32[1]{0:T(128)} %bitcast.half_ref, bf16[2,4096,128]{2,1,0:T(8,128)(2,1)} %bitcast.20, f32[2,4096,128]{2,1,0:T(8,128)} %bitcast.16, f32[64,128]{1,0:T(8,128)S(1)} %bitcast.14), custom_call_target="tpu_custom_call" | custom-call | flops 536870912 | bytes 3145728 | tf_op jit(solution)/shard_map/left/pallas_call | solution.py:78
  7.2 0.0 collective-permute-done
  7.2 0.1 add.50
  7.3 0.0 copy-start.3
  7.4 23.0 %all_to_all.17 = f32[16,128,128]{2,1,0:T(8,128)S(1)} all-to-all(f32[16,128,128]{2,1,0:T(8,128)S(1)} %bitcast.23), channel_id=1, replica_groups=mesh['x'=4,'y'=4,'c'=2,'z'=8] {'x','y'}, dimensions={0} | all-to-all | bytes 2097152 | tf_op jit(solution)/shard_map/all_to_all | solution.py:240
  30.3 0.1 reduce_sum.9
  30.4 4.7 %collective-permute-start.3 = (f32[128,128]{1,0:T(8,128)S(1)}, f32[128,128]{1,0:T(8,128)S(1)}, u32[]{:S(2)}, u32[]{:S(2)}) collective-permute-start(f32[128,128]{1,0:T(8,128)S(1)} %reduce_sum.9), channel_id=1, source_target_pairs={{0,3},{1,2},{2,1},{3,0},{4,7},{5,6},{6,5},{7,4},{8,11},{9,10},{10,... | collective-permute-start | bytes 196616 | tf_op jit(solution)/shard_map/ppermute | solution.py:249
  35.1 0.0 collective-permute-start.2
  35.1 0.7 collective-permute-start.1
  35.7 1.7 %collective-permute-done.3 = f32[128,128]{1,0:T(8,128)S(1)} collective-permute-done((f32[128,128]{1,0:T(8,128)S(1)}, f32[128,128]{1,0:T(8,128)S(1)}, u32[]{:S(2)}, u32[]{:S(2)}) %collective-permute-start.3) | collective-permute-done | bytes 65568 | tf_op jit(solution)/shard_map/ppermute | solution.py:249
  37.4 2.8 %collective-permute-done.2 = f32[128,128]{1,0:T(8,128)S(1)} collective-permute-done((f32[128,128]{1,0:T(8,128)S(1)}, f32[128,128]{1,0:T(8,128)S(1)}, u32[]{:S(2)}, u32[]{:S(2)}) %collective-permute-start.2) | collective-permute-done | bytes 65568 | tf_op jit(solution)/shard_map/ppermute | solution.py:249
  40.2 0.0 collective-permute-done.1
  40.3 0.0 copy-start.2
  40.3 4.4 %collective-permute-start.4 = (f32[128,128]{1,0:T(8,128)S(1)}, f32[128,128]{1,0:T(8,128)S(1)}, u32[]{:S(2)}, u32[]{:S(2)}) collective-permute-start(f32[128,128]{1,0:T(8,128)S(1)} %add_add_fusion), channel_id=1, source_target_pairs={{0,7},{1,6},{2,5},{3,4},{4,3},{5,2},{6,1},{7,0},{8,15},{9,14},{10,... | collective-permute-start | bytes 196616 | tf_op jit(solution)/shard_map/ppermute | solution.py:274
  44.7 0.0 copy-done.3
  44.7 1.8 %dynamic-slice_add_fusion.1.combined_ref.own_combined_ref = f32[2,2048,128]{2,1,0:T(8,128)S(1)} fusion(f32[2,4096,128]{2,1,0:T(8,128)} %bitcast.17, s32[]{:T(128)S(6)} %select_n.8, bf16[2,4096,128]{2,1,0:T(8,128)(2,1)S(1)} %bitcast.21), kind=kLoop, calls=%fused_computation.1 | loop fusion | flops 1048576 | bytes 5242884 | tf_op jit(solution)/shard_map/add | solution.py:262
  46.5 0.0 copy-done.2
  46.5 0.3 dynamic-slice_add_fusion.combined_ref.other_combined_ref
  46.8 0.8 collective-permute-done.4
  47.5 0.1 tile.2
  47.6 19.5 %all_to_all.18 = f32[16,128,128]{2,1,0:T(8,128)S(1)} all-to-all(f32[16,128,128]{2,1,0:T(8,128)S(1)} %tile.2), channel_id=1, replica_groups=mesh['x'=4,'y'=4,'c'=2,'z'=8] {'x','y'}, dimensions={0} | all-to-all | bytes 2097152 | tf_op jit(solution)/shard_map/all_to_all | solution.py:244
  67.1 0.0 collective-permute-start.5
  67.1 1.4 %right_own.1 = (f32[256,256]{1,0:T(8,128)S(1)}, f32[256,256]{1,0:T(8,128)S(1)}, f32[128,128]{1,0:T(8,128)S(1)}) custom-call(f32[2,2048,128]{2,1,0:T(8,128)S(1)} %dynamic-slice_add_fusion.1.combined_ref.own_combined_ref, f32[2048,128]{1,0:T(8,128)S(1)} %bitcast.11), custom_call_target="tpu_custom_call" | custom-call | flops 939524096 | bytes 3145728 | tf_op jit(solution)/shard_map/right_own/pallas_call | solution.py:131
  68.6 1.2 %collective-permute-done.5.factor_ref.other_ref = f32[2048,128]{1,0:T(8,128)S(1)} collective-permute-done((f32[2048,128]{1,0:T(8,128)S(1)}, f32[2048,128]{1,0:T(8,128)S(1)}, u32[]{:S(2)}, u32[]{:S(2)}) %collective-permute-start.5) | collective-permute-done | bytes 1048608 | tf_op jit(solution)/shard_map/ppermute | solution.py:236
  69.8 1.6 %right_other.1 = (f32[64,128]{1,0:T(8,128)S(1)}, f32[64,64]{1,0:T(8,128)S(1)}) custom-call(f32[2,2048,128]{2,1,0:T(8,128)S(1)} %dynamic-slice_add_fusion.combined_ref.other_combined_ref, f32[2048,128]{1,0:T(8,128)S(1)} %collective-permute-done.5.factor_ref.other_ref, f32[256,256]{1,0:T(8,128)S(1)} %get-tuple-element.31.acc_in, ...), custom_call_target="tpu_custom_call" | custom-call | flops 939524096 | bytes 3145728 | tf_op jit(solution)/shard_map/right_other/pallas_call | solution.py:143
  71.4 0.2 collective-permute-start.6
  71.6 1.1 %collective-permute-done.6 = f32[64,128]{1,0:T(8,128)S(1)} collective-permute-done((f32[64,128]{1,0:T(8,128)S(1)}, f32[64,128]{1,0:T(8,128)S(1)}, u32[]{:S(2)}, u32[]{:S(2)}) %collective-permute-start.6) | collective-permute-done | bytes 32800 | tf_op jit(solution)/shard_map/ppermute | solution.py:236
  72.7 0.6 collective-permute-start.9
  73.2 2.1 %collective-permute-start.8 = (f32[64,128]{1,0:T(8,128)S(1)}, f32[64,128]{1,0:T(8,128)S(1)}, u32[]{:S(2)}, u32[]{:S(2)}) collective-permute-start(f32[64,128]{1,0:T(8,128)S(1)} %add.59), channel_id=1, source_target_pairs={{0,32},{16,48},{32,0},{48,16},{1,33},{17,49},{33,1},{49,17},{2,34}... | collective-permute-start | bytes 98312 | tf_op jit(solution)/shard_map/ppermute | solution.py:249
  75.3 1.5 %collective-permute-start.7 = (f32[64,128]{1,0:T(8,128)S(1)}, f32[64,128]{1,0:T(8,128)S(1)}, u32[]{:S(2)}, u32[]{:S(2)}) collective-permute-start(f32[64,128]{1,0:T(8,128)S(1)} %add.59), channel_id=1, source_target_pairs={{0,16},{16,0},{32,48},{48,32},{1,17},{17,1},{33,49},{49,33},{2,18}... | collective-permute-start | bytes 98312 | tf_op jit(solution)/shard_map/ppermute | solution.py:249
  76.8 1.8 %inverse.1.inverse_ref = f32[64,64]{1,0:T(8,128)S(1)} custom-call(f32[64,64]{1,0:T(8,128)S(1)} %get-tuple-element.35.gram_ref), custom_call_target="tpu_custom_call" | custom-call | flops 262144 | bytes 32768 | tf_op jit(solution)/shard_map/inverse/pallas_call | solution.py:172
  78.6 0.0 collective-permute-done.9
  78.6 0.1 collective-permute-done.8
  78.7 0.5 collective-permute-done.7
  79.2 2.3 %collective-permute-start.12 = (f32[64,128]{1,0:T(8,128)S(1)}, f32[64,128]{1,0:T(8,128)S(1)}, u32[]{:S(2)}, u32[]{:S(2)}) collective-permute-start(f32[64,128]{1,0:T(8,128)S(1)} %add_add_fusion.2), channel_id=1, source_target_pairs={{0,192},{64,128},{128,64},{192,0},{1,193},{65,129},{129,65},{193,1... | collective-permute-start | bytes 98312 | tf_op jit(solution)/shard_map/ppermute | solution.py:249
  81.6 0.5 collective-permute-start.11
  82.1 1.5 %collective-permute-start.10 = (f32[64,128]{1,0:T(8,128)S(1)}, f32[64,128]{1,0:T(8,128)S(1)}, u32[]{:S(2)}, u32[]{:S(2)}) collective-permute-start(f32[64,128]{1,0:T(8,128)S(1)} %add_add_fusion.2), channel_id=1, source_target_pairs={{0,64},{64,0},{128,192},{192,128},{1,65},{65,1},{129,193},{193,129... | collective-permute-start | bytes 98312 | tf_op jit(solution)/shard_map/ppermute | solution.py:249
  83.6 1.3 %collective-permute-done.12 = f32[64,128]{1,0:T(8,128)S(1)} collective-permute-done((f32[64,128]{1,0:T(8,128)S(1)}, f32[64,128]{1,0:T(8,128)S(1)}, u32[]{:S(2)}, u32[]{:S(2)}) %collective-permute-start.12) | collective-permute-done | bytes 32800 | tf_op jit(solution)/shard_map/ppermute | solution.py:249
  84.9 2.1 %collective-permute-done.11 = f32[64,128]{1,0:T(8,128)S(1)} collective-permute-done((f32[64,128]{1,0:T(8,128)S(1)}, f32[64,128]{1,0:T(8,128)S(1)}, u32[]{:S(2)}, u32[]{:S(2)}) %collective-permute-start.11) | collective-permute-done | bytes 32800 | tf_op jit(solution)/shard_map/ppermute | solution.py:249
  87.0 0.0 collective-permute-done.10
  87.0 4.2 %final.1 = (bf16[2,4096,128]{2,1,0:T(8,128)(2,1)}, f32[2,4096,128]{2,1,0:T(8,128)}, f32[64,128]{1,0:T(8,128)}) custom-call(s32[1]{0:T(128)} %bitcast.half_ref, f32[2,2048,128]{2,1,0:T(8,128)S(1)} %dynamic-slice_add_fusion.1.combined_ref.own_combined_ref, f32[2,2048,128]{2,1,0:T(8,128)S(1)} %dynamic-slice_add_fusion.combined_ref.other_combined_ref, ...), custom_call_target="tpu_custom_call" | custom-call | flops 1073741824 | bytes 6291456 | tf_op jit(solution)/shard_map/final/pallas_call | solution.py:214
  (5 shorter events, 0.0 us)
Async XLA Ops:
  0.6 0.8 copy-start
  1.4 2.9 %copy-start.1 = (f32[128,64]{0,1:T(8,128)S(1)}, f32[128,64]{0,1:T(8,128)}, u32[]{:S(2)}) copy-start(f32[128,64]{0,1:T(8,128)} %param.5) | copy-start | bytes 98308
  4.2 3.0 %collective-permute-start = (f32[2048,128]{1,0:T(8,128)S(1)}, f32[2048,128]{1,0:T(8,128)S(1)}, u32[]{:S(2)}, u32[]{:S(2)}) collective-permute-start(f32[2048,128]{1,0:T(8,128)S(1)} %left.3), channel_id=1, source_target_pairs={{0,8},{8,0},{1,9},{9,1},{2,10},{10,2},{3,11},{11,3},{4,12},{12,4},... | collective-permute-start | bytes 3145736 | tf_op jit(solution)/shard_map/ppermute | solution.py:236
  7.3 37.4 %copy-start.3 = (bf16[1,8192,128]{2,1,0:T(8,128)(2,1)S(1)}, bf16[1,8192,128]{2,1,0:T(8,128)(2,1)}, u32[]{:S(2)}) copy-start(bf16[1,8192,128]{2,1,0:T(8,128)(2,1)} %param.3) | copy-start | bytes 6291460
  30.4 7.1 %collective-permute-start.3 = (f32[128,128]{1,0:T(8,128)S(1)}, f32[128,128]{1,0:T(8,128)S(1)}, u32[]{:S(2)}, u32[]{:S(2)}) collective-permute-start(f32[128,128]{1,0:T(8,128)S(1)} %reduce_sum.9), channel_id=1, source_target_pairs={{0,3},{1,2},{2,1},{3,0},{4,7},{5,6},{6,5},{7,4},{8,11},{9,10},{10,... | collective-permute-start | bytes 196616 | tf_op jit(solution)/shard_map/ppermute | solution.py:249
  35.1 5.2 %collective-permute-start.2 = (f32[128,128]{1,0:T(8,128)S(1)}, f32[128,128]{1,0:T(8,128)S(1)}, u32[]{:S(2)}, u32[]{:S(2)}) collective-permute-start(f32[128,128]{1,0:T(8,128)S(1)} %reduce_sum.9), channel_id=1, source_target_pairs={{0,2},{1,3},{2,0},{3,1},{4,6},{5,7},{6,4},{7,5},{8,10},{9,11},{10,... | collective-permute-start | bytes 196616 | tf_op jit(solution)/shard_map/ppermute | solution.py:249
  35.1 5.2 %collective-permute-start.1 = (f32[128,128]{1,0:T(8,128)S(1)}, f32[128,128]{1,0:T(8,128)S(1)}, u32[]{:S(2)}, u32[]{:S(2)}) collective-permute-start(f32[128,128]{1,0:T(8,128)S(1)} %reduce_sum.9), channel_id=1, source_target_pairs={{0,1},{1,0},{2,3},{3,2},{4,5},{5,4},{6,7},{7,6},{8,9},{9,8},{10,11... | collective-permute-start | bytes 196616 | tf_op jit(solution)/shard_map/ppermute | solution.py:249
  40.3 6.2 %copy-start.2 = (f32[1,8192,128]{2,1,0:T(8,128)S(1)}, f32[1,8192,128]{2,1,0:T(8,128)}, u32[]{:S(2)}) copy-start(f32[1,8192,128]{2,1,0:T(8,128)} %param.4) | copy-start | bytes 12582916
  40.3 7.2 %collective-permute-start.4 = (f32[128,128]{1,0:T(8,128)S(1)}, f32[128,128]{1,0:T(8,128)S(1)}, u32[]{:S(2)}, u32[]{:S(2)}) collective-permute-start(f32[128,128]{1,0:T(8,128)S(1)} %add_add_fusion), channel_id=1, source_target_pairs={{0,7},{1,6},{2,5},{3,4},{4,3},{5,2},{6,1},{7,0},{8,15},{9,14},{10,... | collective-permute-start | bytes 196616 | tf_op jit(solution)/shard_map/ppermute | solution.py:274
  67.1 2.7 %collective-permute-start.5 = (f32[2048,128]{1,0:T(8,128)S(1)}, f32[2048,128]{1,0:T(8,128)S(1)}, u32[]{:S(2)}, u32[]{:S(2)}) collective-permute-start(f32[2048,128]{1,0:T(8,128)S(1)} %bitcast.10), channel_id=1, source_target_pairs={{0,8},{8,0},{1,9},{9,1},{2,10},{10,2},{3,11},{11,3},{4,12},{12,4},... | collective-permute-start | bytes 3145736 | tf_op jit(solution)/shard_map/ppermute | solution.py:236
  71.4 1.3 %collective-permute-start.6 = (f32[64,128]{1,0:T(8,128)S(1)}, f32[64,128]{1,0:T(8,128)S(1)}, u32[]{:S(2)}, u32[]{:S(2)}) collective-permute-start(f32[64,128]{1,0:T(8,128)S(1)} %get-tuple-element.34), channel_id=1, source_target_pairs={{0,8},{8,0},{1,9},{9,1},{2,10},{10,2},{3,11},{11,3},{4,12},{12,4},... | collective-permute-start | bytes 98312 | tf_op jit(solution)/shard_map/ppermute | solution.py:236
  72.7 5.9 %collective-permute-start.9 = (f32[64,128]{1,0:T(8,128)S(1)}, f32[64,128]{1,0:T(8,128)S(1)}, u32[]{:S(2)}, u32[]{:S(2)}) collective-permute-start(f32[64,128]{1,0:T(8,128)S(1)} %add.59), channel_id=1, source_target_pairs={{0,48},{16,32},{32,16},{48,0},{1,49},{17,33},{33,17},{49,1},{2,50}... | collective-permute-start | bytes 98312 | tf_op jit(solution)/shard_map/ppermute | solution.py:249
  73.2 5.5 %collective-permute-start.8 = (f32[64,128]{1,0:T(8,128)S(1)}, f32[64,128]{1,0:T(8,128)S(1)}, u32[]{:S(2)}, u32[]{:S(2)}) collective-permute-start(f32[64,128]{1,0:T(8,128)S(1)} %add.59), channel_id=1, source_target_pairs={{0,32},{16,48},{32,0},{48,16},{1,33},{17,49},{33,1},{49,17},{2,34}... | collective-permute-start | bytes 98312 | tf_op jit(solution)/shard_map/ppermute | solution.py:249
  75.3 3.9 %collective-permute-start.7 = (f32[64,128]{1,0:T(8,128)S(1)}, f32[64,128]{1,0:T(8,128)S(1)}, u32[]{:S(2)}, u32[]{:S(2)}) collective-permute-start(f32[64,128]{1,0:T(8,128)S(1)} %add.59), channel_id=1, source_target_pairs={{0,16},{16,0},{32,48},{48,32},{1,17},{17,1},{33,49},{49,33},{2,18}... | collective-permute-start | bytes 98312 | tf_op jit(solution)/shard_map/ppermute | solution.py:249
  79.2 5.7 %collective-permute-start.12 = (f32[64,128]{1,0:T(8,128)S(1)}, f32[64,128]{1,0:T(8,128)S(1)}, u32[]{:S(2)}, u32[]{:S(2)}) collective-permute-start(f32[64,128]{1,0:T(8,128)S(1)} %add_add_fusion.2), channel_id=1, source_target_pairs={{0,192},{64,128},{128,64},{192,0},{1,193},{65,129},{129,65},{193,1... | collective-permute-start | bytes 98312 | tf_op jit(solution)/shard_map/ppermute | solution.py:249
  81.6 5.4 %collective-permute-start.11 = (f32[64,128]{1,0:T(8,128)S(1)}, f32[64,128]{1,0:T(8,128)S(1)}, u32[]{:S(2)}, u32[]{:S(2)}) collective-permute-start(f32[64,128]{1,0:T(8,128)S(1)} %add_add_fusion.2), channel_id=1, source_target_pairs={{0,128},{64,192},{128,0},{192,64},{1,129},{65,193},{129,1},{193,65... | collective-permute-start | bytes 98312 | tf_op jit(solution)/shard_map/ppermute | solution.py:249
  82.1 4.9 %collective-permute-start.10 = (f32[64,128]{1,0:T(8,128)S(1)}, f32[64,128]{1,0:T(8,128)S(1)}, u32[]{:S(2)}, u32[]{:S(2)}) collective-permute-start(f32[64,128]{1,0:T(8,128)S(1)} %add_add_fusion.2), channel_id=1, source_target_pairs={{0,64},{64,0},{128,192},{192,128},{1,65},{65,1},{129,193},{193,129... | collective-permute-start | bytes 98312 | tf_op jit(solution)/shard_map/ppermute | solution.py:249
